TPU v7x, 128 devices: a whole 4x4x4 slice. The times are simulated.
128 devices in a mesh: dp: 64 (over z_lo, x, y, core), tensor: 2 (over z_hi).
Axes of the slice: x: 4, y: 4, z: 4 (z_hi: 2, z_lo: 2; z = z_hi * 2 + z_lo), core: 2. Of those that a mesh axis runs over, the one named last changes fastest.
Arguments:
- tokens: bfloat16 [16384, 384], P('dp'), may hold values from -6 to 6
- cotangent: bfloat16 [16384, 384], P('dp'), may hold values from -6 to 6
- pos_table: float32 [50, 384], replicated, may hold values from -3 to 3
- norm_params: float32 [4, 384], replicated
- qkv_weight: float32 [384, 1152], P(None, ('tensor', 'dp'))
- out_weight: float32 [384, 384], P(('tensor', 'dp'))
- up_weight: float32 [384, 1536], P(None, ('tensor', 'dp'))
- down_weight: float32 [1536, 384], P(('tensor', 'dp'))
- qkv_moment: float32 [384, 1152], P(None, ('tensor', 'dp')), may hold values from -0.0030070327 to 0.0030070327
- out_moment: float32 [384, 384], P(('tensor', 'dp')), may hold values from -0.0030070327 to 0.0030070327
- up_moment: float32 [384, 1536], P(None, ('tensor', 'dp')), may hold values from -0.0030070327 to 0.0030070327
- down_moment: float32 [1536, 384], P(('tensor', 'dp')), may hold values from -0.0030070327 to 0.0030070327
- norm_moment: float32 [4, 384], replicated, may hold values from -0.030070327 to 0.030070327
- pos_moment: float32 [50, 384], replicated, may hold values from -0.030070327 to 0.030070327
- res_ids: int32 [320], P('dp'), may hold values from 0 to 2, as said below
- offsets: int32 [320], P('dp'), may hold values from 0 to 256, as said below
- pos_index: int32 [16384], P('dp'), may hold values from 0 to 49, as said below
Outputs:
- result: bfloat16 [16384, 384], P('dp')
- in_grad: float32 [16384, 384], P('dp')
- grad_norm: float32 [], replicated
- qkv_moment_next: float32 [384, 1152], P(None, ('tensor', 'dp'))
- qkv_weight_next: float32 [384, 1152], P(None, ('tensor', 'dp'))
- out_moment_next: float32 [384, 384], P(('tensor', 'dp'))
- out_weight_next: float32 [384, 384], P(('tensor', 'dp'))
- up_moment_next: float32 [384, 1536], P(None, ('tensor', 'dp'))
- up_weight_next: float32 [384, 1536], P(None, ('tensor', 'dp'))
- down_moment_next: float32 [1536, 384], P(('tensor', 'dp'))
- down_weight_next: float32 [1536, 384], P(('tensor', 'dp'))
- norm_moment_next: float32 [4, 384], replicated
- norm_params_next: float32 [4, 384], replicated
- pos_moment_next: float32 [50, 384], replicated
- pos_table_next: float32 [50, 384], replicated
Inputs may be any that keep to these rules, and one draw needn't show every extreme that they name: `res_ids`: 0 marks a 224-pixel image of 50 tokens, 1 a 384-pixel image of 145 tokens, 2 an empty slot; the 5 slots of a dp index hold its images first and empty slots last, and at most one 384-pixel image. `offsets`: images of a dp index lie end to end from its slot 0 in slot order; an empty slot holds 256; token slots after the last image are padding. `pos_index`: 0 for an image's first token and for padding; for patch (r, c) of a g x g grid (g = 7 or 12), in row order after the first token, 1 + 7 (r * 7 // g) + (c * 7 // g).
All inputs are finite; a program needn't handle non-finite values.
Results may differ from a plain program's by a relative error of at most 0.015.
The roundings to bfloat16 on the way count: a program that leaves them out, or rounds other values in their place, can miss the bound.
Values may be sent and summed in bfloat16 or wider, within the bound.
No kernel may reach another device: no remote copies, remote signals or barrier semaphores. Data moves between devices by JAX's collectives and lax.ppermute only.
A program may use at most 128 MiB of HBM per device.

v0:
```python
import math

import jax
import jax.numpy as jnp
import numpy as np
from jax import lax
from jax.experimental import pallas as pl
from jax.experimental.pallas import tpu as pltpu
from jax.sharding import Mesh
from jax.sharding import PartitionSpec as P

D = 384
HEADS = 6
HD = 64
FF = 1536
SMALL_LEN = 50
BIG_LEN = 145
NS_STEPS = 5
COEF_A = 3.4445
COEF_B = -4.775
COEF_C = 2.0315
NORM_EPS = 1e-06
CLIP_LIMIT = 1.0
MOMENTUM = 0.5
SMALL_RATE = 10.0
NORM_RATE = 40.0

DP = ("zl", "x", "y", "c")
ROWS = ("zh",) + DP
COLUMN = ("zh", "zl")
PLANE = ("x", "y")
HALF = ("zl", "x", "y")
CHIPS = ("zh", "zl", "x", "y")

BF = jnp.bfloat16
F32 = jnp.float32
BLOCK = 12
GROUP = 48
SENT = 40
VMEM = 60 << 20


def unit_places():
    places = np.zeros((2, 768, 1536), np.float32)
    for core in range(2):
        for xy in range(16):
            for z in range(4):
                block = (z * 16 + xy) * 2 + core
                for r in range(BLOCK):
                    row = xy * GROUP + z * BLOCK + r
                    if r < 9:
                        head, rest = divmod(block * 9 + r, 192)
                        part, e = divmod(rest, 64)
                        places[core, row, part * 384 + head * 64 + e] = 1
                    else:
                        places[core, row, 1152 + block * 3 + r - 9] = 1
    return places


def small_places():
    places = np.zeros((768, 64), np.float32)
    for n in range(64):
        places[(n // 4) * GROUP + (n % 4) * BLOCK, n] = 1
    return places


def dot(a, b):
    return lax.dot_general(a, b, (((1,), (0,)), ((), ())), preferred_element_type=F32)


def dot_nt(a, b):
    return lax.dot_general(a, b, (((1,), (1,)), ((), ())), preferred_element_type=F32)


def dot_tn(a, b):
    return lax.dot_general(a, b, (((0,), (0,)), ((), ())), preferred_element_type=F32)


def halves(a):
    high = a.astype(BF)
    return high, (a - high.astype(F32)).astype(BF)


def norm_parts(v):
    cen = v - jnp.mean(v, axis=-1, keepdims=True)
    var = jnp.mean(cen * cen, axis=-1, keepdims=True)
    r = lax.rsqrt(var + NORM_EPS)
    return cen * r, r


def norm_back(dy, n, r, gain):
    e = dy * gain
    return r * (
        e - jnp.mean(e, axis=-1, keepdims=True) - n * jnp.mean(e * n, axis=-1, keepdims=True)
    )


def group_rows(source, first, xy):
    return jnp.concatenate(
        [source[z * 16 + xy].astype(F32)[first : first + BLOCK] for z in range(4)], axis=0
    )


def layer_kernel(
    where_ref,
    res_ref,
    off_ref,
    tok_ref,
    cot_ref,
    table_ref,
    norms_ref,
    pos_ref,
    own_ref,
    oth_ref,
    places_ref,
    small_ref,
    result_ref,
    in_grad_ref,
    keep_ref,
    send_ref,
    wup,
    wdn,
    wat,
    probs_ref,
    qkv_ref,
    ctx_ref,
    dqkv_ref,
):
    core = where_ref[0]
    half = where_ref[1]
    count = tok_ref.shape[0]

    for s, src in enumerate((own_ref, oth_ref)):

        def regroup(xy, _, s=s, src=src):
            at = pl.multiple_of(s * 768 + xy * GROUP, 16)
            for first, dst in ((0, wup), (12, wdn), (24, wat)):
                dst[pl.ds(at, GROUP), :] = group_rows(src, first, xy).astype(BF)
            return 0

        lax.fori_loop(0, 16, regroup, 0)

    def place(s):
        return core if s == 0 else 1 - core

    hits = (
        lax.broadcasted_iota(jnp.int32, (64, count), 0) == jnp.broadcast_to(pos_ref[...], (64, count))
    ).astype(BF)
    table = table_ref[...]
    t0, t_rest = halves(table)
    t1, t2 = halves(table - t0.astype(F32))
    stream_in = tok_ref[...].astype(F32) + ((dot_tn(hits, t2) + dot_tn(hits, t1)) + dot_tn(hits, t0))
    g1, s1, g2, s2 = (norms_ref[k : k + 1, :] for k in range(4))
    n1, r1 = norm_parts(stream_in)
    y1 = (n1 * g1 + s1).astype(BF)
    qkv = 0.0
    for s in range(2):
        pad = dot_nt(y1, wat[s * 768 : (s + 1) * 768, :]).astype(BF)
        qkv = qkv + dot(pad, places_ref[place(s), :, :1152])
    qkv_ref[...] = qkv.astype(BF)

    def segments(shape, dim):
        at = lax.broadcasted_iota(jnp.int32, shape, dim)
        seg = at + 8
        for k in range(5):
            res = res_ref[k]
            off = off_ref[k]
            length = jnp.where(res == 0, SMALL_LEN, jnp.where(res == 1, BIG_LEN, 0))
            seg = jnp.where((at >= off) & (at < off + length), k, seg)
        return seg

    allowed = segments((count, count), 0) == segments((count, count), 1)
    lane = lax.broadcasted_iota(jnp.int32, (1, 128), 1)
    masks = ((lane < HD).astype(F32).astype(BF), (lane >= HD).astype(F32).astype(BF))
    scale = HD**-0.5
    for p in range(HEADS // 2):
        lo = p * 128
        q = qkv_ref[:, lo : lo + 128]
        k = qkv_ref[:, 384 + lo : 512 + lo]
        v = qkv_ref[:, 768 + lo : 896 + lo]
        ctx = 0.0
        for hh in range(2):
            scores = dot_nt(q * masks[hh], k) * scale
            scores = jnp.where(allowed, scores, -1e30)
            expo = jnp.exp(scores - jnp.max(scores, axis=-1, keepdims=True))
            probs = expo / jnp.sum(expo, axis=-1, keepdims=True)
            probs_ref[2 * p + hh] = probs
            ctx = ctx + dot(probs.astype(BF), v * masks[hh])
        ctx_ref[:, lo : lo + 128] = ctx.astype(BF)
    ctx_pads = [
        dot_nt(ctx_ref[...], places_ref[place(s), :, 1152:]).astype(BF) for s in range(2)
    ]
    stream_mid = stream_in + (dot(ctx_pads[0], wat[:768, :]) + dot(ctx_pads[1], wat[768:, :]))
    n2, r2 = norm_parts(stream_mid)
    y2 = (n2 * g2 + s2).astype(BF)

    cot = cot_ref[...]
    right = jnp.where(half == 0, y2, cot)
    out = stream_mid
    d_y2 = 0.0
    for k in range(4):
        wu = wup[k * 384 : (k + 1) * 384, :]
        wd = wdn[k * 384 : (k + 1) * 384, :]
        pre = dot_nt(y2, wu)
        cdf = 0.5 * (1.0 + lax.erf(pre * (2.0**-0.5)))
        hidden = (pre * cdf).astype(BF)
        slope = cdf + pre * (jnp.exp(-0.5 * pre * pre) * ((2.0 * math.pi) ** -0.5))
        d_pre = (slope * dot_nt(cot, wd)).astype(BF)
        out = out + dot(hidden, wd)
        d_y2 = d_y2 + dot(d_pre, wu)
        grad = dot_tn(jnp.where(half == 0, d_pre, hidden), right).reshape(8, GROUP, 384)
        at = (k % 2) * 8
        if k < 2:
            keep_ref[at : at + 8] = grad
        else:
            send_ref[at : at + 8] = grad.astype(BF)
    result_ref[...] = out.astype(BF)
    gain2 = jnp.sum(d_y2 * n2, axis=0, keepdims=True)
    shift2 = jnp.sum(d_y2, axis=0, keepdims=True)
    d_mid = cot.astype(F32) + norm_back(d_y2, n2, r2, g2)

    d_attn = d_mid.astype(BF)
    d_ctx = 0.0
    for s in range(2):
        pad = dot_nt(d_attn, wat[s * 768 : (s + 1) * 768, :]).astype(BF)
        d_ctx = d_ctx + dot(pad, places_ref[place(s), :, 1152:])
    d_ctx = d_ctx.astype(BF)
    for p in range(HEADS // 2):
        lo = p * 128
        q = qkv_ref[:, lo : lo + 128]
        k = qkv_ref[:, 384 + lo : 512 + lo]
        v = qkv_ref[:, 768 + lo : 896 + lo]
        dc = d_ctx[:, lo : lo + 128]
        dq, dk, dv = 0.0, 0.0, 0.0
        for hh in range(2):
            probs = probs_ref[2 * p + hh]
            dcm = dc * masks[hh]
            d_probs = dot_nt(dcm, v)
            inner = jnp.sum(probs * d_probs, axis=-1, keepdims=True)
            d_scores = (probs * (d_probs - inner)).astype(BF)
            dq = dq + dot(d_scores, k * masks[hh])
            dk = dk + dot_tn(d_scores, q * masks[hh])
            dv = dv + dot_tn(probs.astype(BF), dcm)
        dqkv_ref[:, lo : lo + 128] = (dq * scale).astype(BF)
        dqkv_ref[:, 384 + lo : 512 + lo] = (dk * scale).astype(BF)
        dqkv_ref[:, 768 + lo : 896 + lo] = dv.astype(BF)
    d_pads = [
        dot_nt(dqkv_ref[...], places_ref[place(s), :, :1152]).astype(BF) for s in range(2)
    ]
    d_y1 = dot(d_pads[0], wat[:768, :]) + dot(d_pads[1], wat[768:, :])
    in_grad = d_mid + norm_back(d_y1, n1, r1, g1)
    in_grad_ref[...] = in_grad

    i0, i1 = halves(in_grad)
    pos_grad = dot(hits, i0) + dot(hits, i1)
    gain1 = jnp.sum(d_y1 * n1, axis=0, keepdims=True)
    shift1 = jnp.sum(d_y1, axis=0, keepdims=True)
    row = lax.broadcasted_iota(jnp.int32, (64, 384), 0)
    for at, value in ((50, gain1), (51, shift1), (52, gain2), (53, shift2)):
        pos_grad = jnp.where(row == at, jnp.broadcast_to(value, (64, 384)), pos_grad)
    small = dot(small_ref[...], jnp.where(half == 0, pos_grad, 0.0).astype(BF))
    right = jnp.where(half == 0, d_attn, y1)
    for s in range(2):
        left = jnp.where(half == 0, ctx_pads[s], d_pads[s])
        grad = (dot_tn(left, right) + small).reshape(16, GROUP, 384)
        if s == 0:
            keep_ref[16:] = grad
        else:
            send_ref[16:] = grad.astype(BF)


def run_layer(where, res_ids, offsets, tokens, cotangent, table, norms, pos, own, other):
    count = tokens.shape[0]
    places = jnp.asarray(unit_places(), BF)
    small = jnp.asarray(small_places(), BF)
    smem = pl.BlockSpec(memory_space=pltpu.SMEM)
    vmem = pl.BlockSpec(memory_space=pltpu.VMEM)
    return pl.pallas_call(
        layer_kernel,
        out_shape=(
            jax.ShapeDtypeStruct((count, D), BF),
            jax.ShapeDtypeStruct((count, D), F32),
            jax.ShapeDtypeStruct((32, GROUP, D), F32),
            jax.ShapeDtypeStruct((32, GROUP, D), BF),
        ),
        in_specs=[smem] * 3 + [vmem] * 9,
        out_specs=(vmem,) * 4,
        scratch_shapes=[
            pltpu.VMEM((1536, D), BF),
            pltpu.VMEM((1536, D), BF),
            pltpu.VMEM((1536, D), BF),
            pltpu.VMEM((HEADS, count, count), F32),
            pltpu.VMEM((count, 1152), BF),
            pltpu.VMEM((count, D), BF),
            pltpu.VMEM((count, 1152), BF),
        ],
        compiler_params=pltpu.CompilerParams(vmem_limit_bytes=VMEM),
        cost_estimate=pl.CostEstimate(
            flops=6_000_000_000, bytes_accessed=16_000_000, transcendentals=2_000_000
        ),
        name="layer",
    )(where, res_ids, offsets, tokens, cotangent, table, norms, pos, own, other, places, small)


def product(a, b):
    (ah, al), (bh, bl) = a, b
    return dot(ah, bh) + (dot(ah, bl) + dot(al, bh))


def orth_kernel(
    where_ref, factor_ref, g_own_ref, g_oth_ref, o_own_ref, o_oth_ref, piece_ref, out_ref, grad_ref, m_ref
):
    xy = where_ref[2]
    is_out = where_ref[3]
    factor = factor_ref[0]
    row = lax.broadcasted_iota(jnp.int32, (GROUP, D), 0) % BLOCK
    valid = ((is_out == 0) | (row >= 9)).astype(F32)

    def fill(at, total):
        for s, (g, o) in enumerate(((g_own_ref, o_own_ref), (g_oth_ref, o_oth_ref))):
            m = MOMENTUM * group_rows(o, 0, at) + factor * (g[at].astype(F32) * valid)
            total = total + m * m
            m_ref[pl.ds(pl.multiple_of(s * 768 + at * GROUP, 16), GROUP), :] = m.astype(BF)
        return total

    total = lax.fori_loop(0, 16, fill, jnp.zeros((GROUP, D), F32))
    inv = 1.0 / (jnp.sqrt(jnp.sum(total)) + 1e-07)
    whole = m_ref[...]
    gram = dot_tn(whole, whole) * (inv * inv)
    eye = (
        lax.broadcasted_iota(jnp.int32, (D, D), 0) == lax.broadcasted_iota(jnp.int32, (D, D), 1)
    ).astype(F32)
    run = None
    for step in range(NS_STEPS):
        parts = halves(gram)
        poly = COEF_A * eye + COEF_B * gram + COEF_C * product(parts, parts)
        poly_parts = halves(poly)
        run = poly if run is None else product(poly_parts, halves(run))
        if step < NS_STEPS - 1:
            gram = product(halves(product(poly_parts, parts)), poly_parts)
    mine = MOMENTUM * group_rows(o_own_ref, 0, xy) + factor * (piece_ref[...] * valid)
    out_ref[...] = product(halves(mine * inv), halves(run))
    grad_ref[...] = piece_ref[...] * valid


def run_orth(where, factor, g_own, g_oth, o_own, o_oth, piece):
    smem = pl.BlockSpec(memory_space=pltpu.SMEM)
    vmem = pl.BlockSpec(memory_space=pltpu.VMEM)
    return pl.pallas_call(
        orth_kernel,
        out_shape=(jax.ShapeDtypeStruct((GROUP, D), F32), jax.ShapeDtypeStruct((GROUP, D), F32)),
        in_specs=[smem] * 2 + [vmem] * 5,
        out_specs=(vmem, vmem),
        scratch_shapes=[pltpu.VMEM((1536, D), BF)],
        compiler_params=pltpu.CompilerParams(vmem_limit_bytes=VMEM),
        cost_estimate=pl.CostEstimate(
            flops=8_000_000_000, bytes_accessed=4_000_000, transcendentals=0
        ),
        name="orth",
    )(where, factor, g_own, g_oth, o_own, o_oth, piece)


def swapped(value):
    return lax.ppermute(value, "c", [(0, 1), (1, 0)])


def exchanged(value, axes):
    return lax.all_to_all(value, axes, 0, 0, tiled=True)


def everywhere(value, axes):
    peers = lax.axis_size(axes)
    return exchanged(jnp.broadcast_to(value[None], (peers, *value.shape)), axes)


def step_rate(rows_count, cols_count):
    return math.sqrt(max(rows_count, cols_count) / rows_count)


def padded(rows, before, total):
    return jnp.pad(rows, ((before, total - before - rows.shape[0]), (0, 0)))


def shards(
    tokens,
    cotangent,
    pos_table,
    norm_params,
    qkv_weight,
    out_weight,
    up_weight,
    down_weight,
    qkv_moment,
    out_moment,
    up_moment,
    down_moment,
    norm_moment,
    pos_moment,
    res_ids,
    offsets,
    pos_index,
):
    z = lax.axis_index(COLUMN)
    xy = lax.axis_index(PLANE)
    zh = lax.axis_index("zh")
    is_out = (z == 1).astype(jnp.int32)
    where = jnp.stack([lax.axis_index("c"), zh, xy, is_out]).astype(jnp.int32)

    rows = jnp.concatenate([up_weight.T, down_weight, qkv_weight.T, out_weight], axis=0).astype(BF)
    own = everywhere(padded(rows, 0, SENT), CHIPS)
    other = swapped(own)

    old = jnp.stack(
        [
            padded(up_moment.T, 0, 16),
            padded(out_moment, 9, 16),
            padded(down_moment, 0, 16),
            padded(qkv_moment.T, 0, 16),
        ]
    ).astype(BF)
    old = exchanged(
        jnp.broadcast_to(old[:, None], (4, 16, 16, D)).reshape(64, 16, D), CHIPS
    )
    old_other = swapped(old)

    result, in_grad, keep, send = run_layer(
        where,
        res_ids,
        offsets,
        tokens,
        cotangent,
        padded(pos_table, 0, 64),
        norm_params,
        pos_index.reshape(1, -1),
        own,
        other,
    )
    pair = (keep + swapped(send).astype(F32)).astype(BF)
    piece = jnp.sum(exchanged(pair, HALF).astype(F32), axis=0)
    grads = everywhere(piece.astype(BF), PLANE)
    grads_other = swapped(grads)

    small = grads.reshape(16, 4, BLOCK, D)[:, :, 0].reshape(64, D).astype(F32)
    valid = (is_out == 0) | (jnp.arange(GROUP)[None, :, None] % BLOCK >= 9)
    wide = jnp.where(valid, grads.astype(F32), 0.0)
    wide_other = jnp.where(valid, grads_other.astype(F32), 0.0)
    squares = jnp.sum(wide * wide) + jnp.sum(wide_other * wide_other)
    squares = squares + jnp.where(is_out == 1, jnp.sum(small * small), 0.0)
    message = jnp.concatenate([small, jnp.broadcast_to(squares, (8, D))], axis=0)
    told = everywhere(message, COLUMN)
    grad_norm = jnp.sqrt(jnp.sum(told[:, 64, 0]))
    factor = jnp.minimum(1.0, CLIP_LIMIT / (grad_norm + 1e-06))
    pos_sum, norm_sum = told[1, :50], told[1, 50:54]

    orth, grad = run_orth(
        where, factor.reshape(1), grads, grads_other, old, old_other, piece
    )
    back = exchanged(
        jnp.concatenate([orth.reshape(4, BLOCK, D), grad.reshape(4, BLOCK, D)], axis=1), COLUMN
    )

    def fresh(moment, z_from, first, last, turn):
        block = back[z_from, BLOCK + first : BLOCK + last]
        return MOMENTUM * moment + factor * (block.T if turn else block)

    def stepped(weight, z_from, first, last, turn, rate):
        block = back[z_from, first:last]
        return weight - rate * (block.T if turn else block)

    norm_fresh = MOMENTUM * norm_moment + factor * norm_sum
    pos_fresh = MOMENTUM * pos_moment + factor * pos_sum
    return (
        result,
        in_grad,
        grad_norm,
        fresh(qkv_moment, 3, 0, 9, True),
        stepped(qkv_weight, 3, 0, 9, True, step_rate(D, 3 * D)),
        fresh(out_moment, 1, 9, 12, False),
        stepped(out_weight, 1, 9, 12, False, step_rate(D, D)),
        fresh(up_moment, 0, 0, 12, True),
        stepped(up_weight, 0, 0, 12, True, step_rate(D, FF)),
        fresh(down_moment, 2, 0, 12, False),
        stepped(down_weight, 2, 0, 12, False, step_rate(FF, D)),
        norm_fresh,
        norm_params - NORM_RATE * norm_fresh,
        pos_fresh,
        pos_table - SMALL_RATE * pos_fresh,
    )


def solution(mesh):
    finer = Mesh(
        mesh.devices.reshape(2, 4, 4, 2, mesh.shape["tensor"]), ("zl", "x", "y", "c", "zh")
    )
    columns = P(None, ROWS)
    rows = P(ROWS, None)
    return jax.shard_map(
        shards,
        mesh=finer,
        in_specs=(
            P(DP, None),
            P(DP, None),
            P(),
            P(),
            columns,
            rows,
            columns,
            rows,
            columns,
            rows,
            columns,
            rows,
            P(),
            P(),
            P(DP),
            P(DP),
            P(DP),
        ),
        out_specs=(
            P(DP, None),
            P(DP, None),
            P(),
            columns,
            columns,
            rows,
            rows,
            columns,
            columns,
            rows,
            rows,
            P(),
            P(),
            P(),
            P(),
        ),
        check_vma=False,
    )
```

profile of v0, /device:TPU:0, one launch (start us, length us, event | category | flops | bytes accessed | tf_op | source)
XLA Modules:
  0.0 180.8 jit_solution(2657468599940110953)
XLA Ops:
  0.6 0.7 convert.42
  1.4 0.7 convert_bitcast_fusion.2
  2.1 0.7 convert_bitcast_fusion.3
  2.9 0.7 convert.44
  3.8 39.7 %all_to_all.30.own_ref = bf16[64,40,384]{2,1,0:T(8,128)(2,1)S(1)} all-to-all(bf16[64,40,384]{2,1,0:T(8,128)(2,1)S(1)} %broadcast_in_dim.24), channel_id=1, replica_groups=mesh['zl'=2,'x'=4,'y'=4,'c'=2,'zh'=2] {'zh','zl','x','y'}, dimensions={0} | all-to-all | bytes 3932160 | tf_op jit(solution)/shard_map/all_to_all | solution.py:368
  43.5 0.7 pad.28.table_ref
  44.7 2.8 %collective-permute-done.oth_ref = bf16[64,40,384]{2,1,0:T(8,128)(2,1)} collective-permute-done((bf16[64,40,384]{2,1,0:T(8,128)(2,1)S(1)}, bf16[64,40,384]{2,1,0:T(8,128)(2,1)}, u32[]{:S(2)}, u32[]{:S(2)}) %collective-permute-start) | collective-permute-done | bytes 1966112 | tf_op jit(solution)/shard_map/ppermute | solution.py:364
  47.6 18.3 %layer.1 = (bf16[256,384]{1,0:T(8,128)(2,1)}, f32[256,384]{1,0:T(8,128)}, f32[32,48,384]{2,1,0:T(8,128)}, bf16[32,48,384]{2,1,0:T(8,128)(2,1)}) custom-call(s32[4]{0:T(128)} %pad_add_fusion.where_ref, s32[5]{0:T(128)} %res_ref.1, s32[5]{0:T(128)} %off_ref.1, bf16[256,384]{1,0:T(8,128)(2,1)} %tok_ref.1, bf16[256,384]{1,0:T(8,128)(2,1)} %cot_ref.1, ...), custom_call_target="tpu_custom_call" | custom-call | flops 6000000000 | bytes 16000000 | tf_op jit(solution)/shard_map/layer/pallas_call | solution.py:278
  66.0 2.9 %collective-permute-done.1 = bf16[32,48,384]{2,1,0:T(8,128)(2,1)S(1)} collective-permute-done((bf16[32,48,384]{2,1,0:T(8,128)(2,1)}, bf16[32,48,384]{2,1,0:T(8,128)(2,1)S(1)}, u32[]{:S(2)}, u32[]{:S(2)}) %collective-permute-start.1) | collective-permute-done | bytes 1179680 | tf_op jit(solution)/shard_map/ppermute | solution.py:364
  68.9 3.0 %add_convert_fusion = bf16[32,48,384]{2,1,0:T(8,128)(2,1)} fusion(f32[32,48,384]{2,1,0:T(8,128)} %get-tuple-element.23, bf16[32,48,384]{2,1,0:T(8,128)(2,1)S(1)} %collective-permute-done.1), kind=kLoop, calls=%fused_computation.1 | loop fusion | flops 1769472 | bytes 4718592 | tf_op jit(solution)/shard_map/convert_element_type | solution.py:438
  71.9 4.8 %all-to-all-start.1 = ((bf16[32,48,384]{2,1,0:T(8,128)(2,1)}), bf16[32,48,384]{2,1,0:T(8,128)(2,1)S(1)}, u32[]{:S(2)}, u32[]{:S(2)}) async-start(bf16[32,48,384]{2,1,0:T(8,128)(2,1)} %add_convert_fusion), calls=%async_computation.1 | async-start | bytes 2359296 | tf_op jit(solution)/shard_map/all_to_all | solution.py:368
  76.8 18.4 %all-to-all-done.1 = bf16[32,48,384]{2,1,0:T(8,128)(2,1)S(1)} async-done(((bf16[32,48,384]{2,1,0:T(8,128)(2,1)}), bf16[32,48,384]{2,1,0:T(8,128)(2,1)S(1)}, u32[]{:S(2)}, u32[]{:S(2)}) %all-to-all-start.1) | async-done | bytes 1179680 | tf_op jit(solution)/shard_map/all_to_all | solution.py:368
  95.4 0.9 broadcast_in_dim.25
  96.3 4.5 %all-to-all-start.2 = ((bf16[16,48,384]{2,1,0:T(8,128)(2,1)}), bf16[16,48,384]{2,1,0:T(8,128)(2,1)S(1)}, u32[]{:S(2)}, u32[]{:S(2)}) async-start(bf16[16,48,384]{2,1,0:T(8,128)(2,1)} %broadcast_in_dim.25), calls=%async_computation.2 | async-start | bytes 1179648 | tf_op jit(solution)/shard_map/all_to_all | solution.py:368
  100.8 11.0 %all-to-all-done.2.g_own_ref = bf16[16,48,384]{2,1,0:T(8,128)(2,1)S(1)} async-done(((bf16[16,48,384]{2,1,0:T(8,128)(2,1)}), bf16[16,48,384]{2,1,0:T(8,128)(2,1)S(1)}, u32[]{:S(2)}, u32[]{:S(2)}) %all-to-all-start.2) | async-done | bytes 589856 | tf_op jit(solution)/shard_map/all_to_all | solution.py:368
  111.8 1.0 broadcast_in_dim.47
  112.8 5.6 %all-to-all-start.4 = ((bf16[64,16,384]{2,1,0:T(8,128)(2,1)}), bf16[64,16,384]{2,1,0:T(8,128)(2,1)S(1)}, u32[]{:S(2)}, u32[]{:S(2)}) async-start(bf16[64,16,384]{2,1,0:T(8,128)(2,1)} %bitcast.15), calls=%async_computation.4 | async-start | bytes 1572864 | tf_op jit(solution)/shard_map/all_to_all | solution.py:368
  118.6 13.5 %all-to-all-done.4.o_own_ref = bf16[64,16,384]{2,1,0:T(8,128)(2,1)S(1)} async-done(((bf16[64,16,384]{2,1,0:T(8,128)(2,1)}), bf16[64,16,384]{2,1,0:T(8,128)(2,1)S(1)}, u32[]{:S(2)}, u32[]{:S(2)}) %all-to-all-start.4) | async-done | bytes 786464 | tf_op jit(solution)/shard_map/all_to_all | solution.py:368
  132.4 0.6 multiply_reduce_fusion.2
  133.7 1.1 multiply_reduce_fusion
  136.1 11.9 %all_to_all.31 = f32[4,72,384]{2,1,0:T(8,128)S(1)} all-to-all(f32[4,72,384]{2,1,0:T(8,128)S(1)} %broadcast_in_dim.46), channel_id=1, replica_groups=mesh['zl'=2,'x'=4,'y'=4,'c'=2,'zh'=2] {'zh','zl'}, dimensions={0} | all-to-all | bytes 884736 | tf_op jit(solution)/shard_map/all_to_all | solution.py:368
  149.4 15.8 %orth.1 = (f32[48,384]{1,0:T(8,128)}, f32[48,384]{1,0:T(8,128)}) custom-call(s32[4]{0:T(128)} %pad_add_fusion.where_ref, f32[1]{0:T(128)} %bitcast.8.factor_ref, bf16[16,48,384]{2,1,0:T(8,128)(2,1)} %copy-done, bf16[16,48,384]{2,1,0:T(8,128)(2,1)} %copy-done.3, bf16[64,16,384]{2,1,0:T(8,128)(2,1)} %copy-done.2, ...), custom_call_target="tpu_custom_call" | custom-call | flops 8000000000 | bytes 4000000 | tf_op jit(solution)/shard_map/orth/pallas_call | solution.py:349
  165.3 0.9 reshape.131
  166.2 0.9 reshape.132
  167.1 0.7 pad_maximum_fusion
  167.8 3.3 %all-to-all-start.5 = ((f32[4,24,384]{2,1,0:T(8,128)}), f32[4,24,384]{2,1,0:T(8,128)S(1)}, u32[]{:S(2)}, u32[]{:S(2)}) async-start(f32[4,24,384]{2,1,0:T(8,128)} %pad_maximum_fusion), calls=%async_computation.5 | async-start | bytes 294912 | tf_op jit(solution)/shard_map/all_to_all | solution.py:368
  171.2 0.7 multiply_subtract_fusion
  172.5 4.7 %all-to-all-done.5 = f32[4,24,384]{2,1,0:T(8,128)S(1)} async-done(((f32[4,24,384]{2,1,0:T(8,128)}), f32[4,24,384]{2,1,0:T(8,128)S(1)}, u32[]{:S(2)}, u32[]{:S(2)}) %all-to-all-start.5) | async-done | bytes 147488 | tf_op jit(solution)/shard_map/all_to_all | solution.py:368
  177.2 0.6 fusion.9
  177.8 0.6 fusion.13
  178.4 0.6 fusion.22
  179.0 0.6 fusion.17
  (61 shorter events, 2.8 us)
Async XLA Ops:
  3.8 39.7 %copy-start.4 = (f32[50,384]{1,0:T(8,128)S(1)}, f32[50,384]{1,0:T(8,128)}, u32[]{:S(2)}) copy-start(f32[50,384]{1,0:T(8,128)} %param.21) | copy-start | bytes 230404
  43.4 4.1 %copy-start.1 = (bf16[64,40,384]{2,1,0:T(8,128)(2,1)}, bf16[64,40,384]{2,1,0:T(8,128)(2,1)S(1)}, u32[]{:S(2)}) copy-start(bf16[64,40,384]{2,1,0:T(8,128)(2,1)S(1)} %all_to_all.30.own_ref) | copy-start | bytes 5898244
  43.4 4.1 %collective-permute-start = (bf16[64,40,384]{2,1,0:T(8,128)(2,1)S(1)}, bf16[64,40,384]{2,1,0:T(8,128)(2,1)}, u32[]{:S(2)}, u32[]{:S(2)}) collective-permute-start(bf16[64,40,384]{2,1,0:T(8,128)(2,1)S(1)} %all_to_all.30.own_ref), channel_id=1, source_target_pairs={{0,2},{2,0},{1,3},{3,1},{4,6},{6,4},{5,7},{7,5},{8,10},{10,8},{9,1... | collective-permute-start | bytes 5898248 | tf_op jit(solution)/shard_map/ppermute | solution.py:364
  65.8 3.1 %collective-permute-start.1 = (bf16[32,48,384]{2,1,0:T(8,128)(2,1)}, bf16[32,48,384]{2,1,0:T(8,128)(2,1)S(1)}, u32[]{:S(2)}, u32[]{:S(2)}) collective-permute-start(bf16[32,48,384]{2,1,0:T(8,128)(2,1)} %get-tuple-element.24), channel_id=1, source_target_pairs={{0,2},{2,0},{1,3},{3,1},{4,6},{6,4},{5,7},{7,5},{8,10},{10,8},{9,1... | collective-permute-start | bytes 3538952 | tf_op jit(solution)/shard_map/ppermute | solution.py:364
  71.9 4.8 %copy-start.7 = (f32[12,384]{1,0:T(8,128)S(1)}, f32[12,384]{1,0:T(8,128)}, u32[]{:S(2)}) copy-start(f32[12,384]{1,0:T(8,128)} %param.30) | copy-start | bytes 55300
  71.9 4.9 %copy-start.14 = (f32[3,384]{1,0:T(4,128)S(1)}, f32[3,384]{1,0:T(4,128)}, u32[]{:S(2)}) copy-start(f32[3,384]{1,0:T(4,128)} %param.28) | copy-start | bytes 13828
  71.9 4.9 %copy-start.11 = (f32[384,9]{0,1:T(8,128)S(1)}, f32[384,9]{0,1:T(8,128)}, u32[]{:S(2)}) copy-start(f32[384,9]{0,1:T(8,128)} %param.27) | copy-start | bytes 41476
  71.9 23.3 %all-to-all-start.1 = ((bf16[32,48,384]{2,1,0:T(8,128)(2,1)}), bf16[32,48,384]{2,1,0:T(8,128)(2,1)S(1)}, u32[]{:S(2)}, u32[]{:S(2)}) async-start(bf16[32,48,384]{2,1,0:T(8,128)(2,1)} %add_convert_fusion), calls=%async_computation.1 | async-start | bytes 2359296 | tf_op jit(solution)/shard_map/all_to_all | solution.py:368
  95.3 17.5 %copy-start.5 = (f32[48,384]{1,0:T(8,128)}, f32[48,384]{1,0:T(8,128)S(1)}, u32[]{:S(2)}) copy-start(f32[48,384]{1,0:T(8,128)S(1)} %convert_reduce_fusion.piece_ref) | copy-start | bytes 221188
  95.3 5.4 %copy-start.9 = (f32[384,12]{0,1:T(8,128)S(1)}, f32[384,12]{0,1:T(8,128)}, u32[]{:S(2)}) copy-start(f32[384,12]{0,1:T(8,128)} %param.29) | copy-start | bytes 55300
  96.3 15.5 %all-to-all-start.2 = ((bf16[16,48,384]{2,1,0:T(8,128)(2,1)}), bf16[16,48,384]{2,1,0:T(8,128)(2,1)S(1)}, u32[]{:S(2)}, u32[]{:S(2)}) async-start(bf16[16,48,384]{2,1,0:T(8,128)(2,1)} %broadcast_in_dim.25), calls=%async_computation.2 | async-start | bytes 1179648 | tf_op jit(solution)/shard_map/all_to_all | solution.py:368
  111.8 21.9 %copy-start = (bf16[16,48,384]{2,1,0:T(8,128)(2,1)}, bf16[16,48,384]{2,1,0:T(8,128)(2,1)S(1)}, u32[]{:S(2)}) copy-start(bf16[16,48,384]{2,1,0:T(8,128)(2,1)S(1)} %all-to-all-done.2.g_own_ref) | copy-start | bytes 1769476
  112.8 19.3 %all-to-all-start.4 = ((bf16[64,16,384]{2,1,0:T(8,128)(2,1)}), bf16[64,16,384]{2,1,0:T(8,128)(2,1)S(1)}, u32[]{:S(2)}, u32[]{:S(2)}) async-start(bf16[64,16,384]{2,1,0:T(8,128)(2,1)} %bitcast.15), calls=%async_computation.4 | async-start | bytes 1572864 | tf_op jit(solution)/shard_map/all_to_all | solution.py:368
  118.5 15.2 %collective-permute-start.2 = (bf16[16,48,384]{2,1,0:T(8,128)(2,1)S(1)}, bf16[16,48,384]{2,1,0:T(8,128)(2,1)S(1)}, u32[]{:S(2)}, u32[]{:S(2)}) collective-permute-start(bf16[16,48,384]{2,1,0:T(8,128)(2,1)S(1)} %all-to-all-done.2.g_own_ref), channel_id=1, source_target_pairs={{0,2},{2,0},{1,3},{3,1},{4,6},{6,4},{5,7},{7,5},{8,10},{10,8},{9,1... | collective-permute-start | bytes 1769480 | tf_op jit(solution)/shard_map/ppermute | solution.py:364
  132.1 2.6 %copy-start.2 = (bf16[64,16,384]{2,1,0:T(8,128)(2,1)}, bf16[64,16,384]{2,1,0:T(8,128)(2,1)S(1)}, u32[]{:S(2)}) copy-start(bf16[64,16,384]{2,1,0:T(8,128)(2,1)S(1)} %all-to-all-done.4.o_own_ref) | copy-start | bytes 2359300
  132.1 17.3 %collective-permute-start.3 = (bf16[64,16,384]{2,1,0:T(8,128)(2,1)S(1)}, bf16[64,16,384]{2,1,0:T(8,128)(2,1)}, u32[]{:S(2)}, u32[]{:S(2)}) collective-permute-start(bf16[64,16,384]{2,1,0:T(8,128)(2,1)S(1)} %all-to-all-done.4.o_own_ref), channel_id=1, source_target_pairs={{0,2},{2,0},{1,3},{3,1},{4,6},{6,4},{5,7},{7,5},{8,10},{10,8},{9,1... | collective-permute-start | bytes 2359304 | tf_op jit(solution)/shard_map/ppermute | solution.py:364
  133.6 14.4 %copy-start.3 = (bf16[16,48,384]{2,1,0:T(8,128)(2,1)}, bf16[16,48,384]{2,1,0:T(8,128)(2,1)S(1)}, u32[]{:S(2)}) copy-start(bf16[16,48,384]{2,1,0:T(8,128)(2,1)S(1)} %collective-permute-done.2.g_oth_ref) | copy-start | bytes 1769476
  149.4 21.8 %copy-start.12 = (f32[50,384]{1,0:T(8,128)S(1)}, f32[50,384]{1,0:T(8,128)}, u32[]{:S(2)}) copy-start(f32[50,384]{1,0:T(8,128)} %param.32) | copy-start | bytes 230404
  165.2 6.6 %copy-start.15 = (f32[4,384]{1,0:T(4,128)S(1)}, f32[4,384]{1,0:T(4,128)}, u32[]{:S(2)}) copy-start(f32[4,384]{1,0:T(4,128)} %norms_ref.1) | copy-start | bytes 18436
  165.2 6.6 %copy-start.16 = (f32[4,384]{1,0:T(4,128)S(1)}, f32[4,384]{1,0:T(4,128)}, u32[]{:S(2)}) copy-start(f32[4,384]{1,0:T(4,128)} %param.31) | copy-start | bytes 18436
  165.3 11.9 %copy-start.6 = (f32[12,384]{1,0:T(8,128)S(1)}, f32[12,384]{1,0:T(8,128)}, u32[]{:S(2)}) copy-start(f32[12,384]{1,0:T(8,128)} %param.26) | copy-start | bytes 55300
  165.3 12.5 %copy-start.8 = (f32[384,12]{0,1:T(8,128)S(1)}, f32[384,12]{0,1:T(8,128)}, u32[]{:S(2)}) copy-start(f32[384,12]{0,1:T(8,128)} %param.25) | copy-start | bytes 55300
  165.3 13.2 %copy-start.13 = (f32[3,384]{1,0:T(4,128)S(1)}, f32[3,384]{1,0:T(4,128)}, u32[]{:S(2)}) copy-start(f32[3,384]{1,0:T(4,128)} %param.24) | copy-start | bytes 13828
  165.3 13.8 %copy-start.10 = (f32[384,9]{0,1:T(8,128)S(1)}, f32[384,9]{0,1:T(8,128)}, u32[]{:S(2)}) copy-start(f32[384,9]{0,1:T(8,128)} %param.23) | copy-start | bytes 41476
  167.8 9.4 %all-to-all-start.5 = ((f32[4,24,384]{2,1,0:T(8,128)}), f32[4,24,384]{2,1,0:T(8,128)S(1)}, u32[]{:S(2)}, u32[]{:S(2)}) async-start(f32[4,24,384]{2,1,0:T(8,128)} %pad_maximum_fusion), calls=%async_computation.5 | async-start | bytes 294912 | tf_op jit(solution)/shard_map/all_to_all | solution.py:368
where the time goes:
time: 182 us; the launch traced here: 181 us
  waiting for transfers between devices  53.4 us (29%)
  blocking collectives  51.6 us (28%)
  Pallas kernels  34.1 us (19%)
  starting transfers between devices  18.5 us (10%)
  other arithmetic  13.5 us (7%)
  local copies, waits for them, and re-layouts  4.94 us (3%)
  between operations  4.79 us (3%)
    all_to_all x2, blocking collectives, exchanged(): return lax.all_to_all(value, axes, 0, 0, tiled=True)  51.6 us
    all_to_all x4, waiting for transfers between devices, exchanged(): return lax.all_to_all(value, axes, 0, 0, tiled=True)  47.6 us
    pallas_call x1, Pallas kernels, run_layer(): pl.pallas_call(layer_kernel, out_shape=(jax.ShapeDtypeStruct((count, D),...  18.3 us
    all_to_all x4, starting transfers between devices, exchanged(): return lax.all_to_all(value, axes, 0, 0, tiled=True)  18.2 us
    pallas_call x1, Pallas kernels, run_orth(): pl.pallas_call(orth_kernel, out_shape=(jax.ShapeDtypeStruct((GROUP, D), F...  15.8 us
    ppermute x4, waiting for transfers between devices, swapped(): return lax.ppermute(value, 'c', [(0, 1), (1, 0)])  5.75 us
  transfers between devices with their start and end apart: 8, of which 6 were waited for; matrix products, arithmetic and copies ran while one was open for 3% of the time, Pallas kernels for 0%

commit v1 on v0

--- a/solution.py
+++ b/solution.py
@@ -211,7 +211,7 @@
         grad = dot_tn(jnp.where(half == 0, d_pre, hidden), right).reshape(8, GROUP, 384)
         at = (k % 2) * 8
         if k < 2:
-            keep_ref[at : at + 8] = grad
+            keep_ref[at : at + 8] = grad.astype(BF)
         else:
             send_ref[at : at + 8] = grad.astype(BF)
     result_ref[...] = out.astype(BF)
@@ -264,7 +264,7 @@
         left = jnp.where(half == 0, ctx_pads[s], d_pads[s])
         grad = (dot_tn(left, right) + small).reshape(16, GROUP, 384)
         if s == 0:
-            keep_ref[16:] = grad
+            keep_ref[16:] = grad.astype(BF)
         else:
             send_ref[16:] = grad.astype(BF)
 
@@ -280,7 +280,7 @@
         out_shape=(
             jax.ShapeDtypeStruct((count, D), BF),
             jax.ShapeDtypeStruct((count, D), F32),
-            jax.ShapeDtypeStruct((32, GROUP, D), F32),
+            jax.ShapeDtypeStruct((32, GROUP, D), BF),
             jax.ShapeDtypeStruct((32, GROUP, D), BF),
         ),
         in_specs=[smem] * 3 + [vmem] * 9,
@@ -307,29 +307,101 @@
     return dot(ah, bh) + (dot(ah, bl) + dot(al, bh))
 
 
-def orth_kernel(
-    where_ref, factor_ref, g_own_ref, g_oth_ref, o_own_ref, o_oth_ref, piece_ref, out_ref, grad_ref, m_ref
-):
+def call(kernel, name, outs, args, scalars=0, scratch=(), flops=0, moved=0):
+    smem = pl.BlockSpec(memory_space=pltpu.SMEM)
+    vmem = pl.BlockSpec(memory_space=pltpu.VMEM)
+    return pl.pallas_call(
+        kernel,
+        out_shape=tuple(jax.ShapeDtypeStruct(shape, dtype) for shape, dtype in outs),
+        in_specs=[smem] * scalars + [vmem] * (len(args) - scalars),
+        out_specs=(vmem,) * len(outs),
+        scratch_shapes=scratch,
+        compiler_params=pltpu.CompilerParams(vmem_limit_bytes=VMEM),
+        cost_estimate=pl.CostEstimate(flops=flops, bytes_accessed=moved, transcendentals=0),
+        name=name,
+    )(*args)
+
+
+def prepare_kernel(qkv_ref, out_ref, up_ref, down_ref, qkv_m_ref, out_m_ref, up_m_ref, down_m_ref, rows_ref, old_ref):
+    zeros = jnp.zeros((16, D), F32)
+    rows = jnp.concatenate(
+        [up_ref[...], down_ref[...], qkv_ref[...], out_ref[...], zeros[: SENT - 36]], axis=0
+    ).astype(BF)
+    rows_ref[...] = jnp.broadcast_to(rows[None], rows_ref.shape)
+    old = (
+        jnp.concatenate([up_m_ref[...], zeros[:4]], axis=0),
+        jnp.concatenate([zeros[:9], out_m_ref[...], zeros[:4]], axis=0),
+        jnp.concatenate([down_m_ref[...], zeros[:4]], axis=0),
+        jnp.concatenate([qkv_m_ref[...], zeros[:7]], axis=0),
+    )
+    for z in range(4):
+        old_ref[z * 16 : (z + 1) * 16] = jnp.broadcast_to(old[z].astype(BF)[None], (16, 16, D))
+
+
+def valid_rows(is_out):
+    row = lax.broadcasted_iota(jnp.int32, (GROUP, D), 0) % BLOCK
+    return ((is_out == 0) | (row >= 9)).astype(F32)
+
+
+def tell_kernel(where_ref, own_ref, oth_ref, piece_ref, small_ref, told_ref):
+    is_out = where_ref[3]
+    valid = valid_rows(is_out)
+    total = jnp.zeros((GROUP, D), F32)
+    for xy in range(16):
+        for ref in (own_ref, oth_ref):
+            g = ref[xy].astype(F32) * valid
+            total = total + g * g
+    small = dot_tn(small_ref[...], own_ref[...].reshape(768, D))
+    squares = jnp.sum(total) + jnp.where(is_out == 1, jnp.sum(small * small), 0.0)
+    squares = jnp.full((1, D), squares, F32)
+    high = squares.astype(BF).astype(F32)
+    mid = (squares - high).astype(BF).astype(F32)
+    low = squares - high - mid
+    for z in range(4):
+        told_ref[z] = jnp.concatenate(
+            [small, piece_ref[z * BLOCK : (z + 1) * BLOCK, :], high, mid, low, jnp.zeros((1, D), F32)],
+            axis=0,
+        ).astype(BF)
+
+
+def clip(told_ref):
+    total = jnp.zeros((1, 1), F32)
+    for z in range(4):
+        for k in range(3):
+            total = total + told_ref[z, 76 + k : 77 + k, :].astype(F32)[:, :1]
+    grad_norm = jnp.sqrt(total)
+    return grad_norm, jnp.minimum(1.0, CLIP_LIMIT / (grad_norm + 1e-06))
+
+
+def gram_kernel(where_ref, g_own_ref, g_oth_ref, o_own_ref, o_oth_ref, gram_ref, both_ref):
+    valid = valid_rows(where_ref[3])
+
+    def fill(xy, _):
+        for s, (g, o) in enumerate(((g_own_ref, o_own_ref), (g_oth_ref, o_oth_ref))):
+            at = pl.ds(pl.multiple_of(s * 768 + xy * GROUP, 16), GROUP)
+            both_ref[at, :D] = group_rows(o, 0, xy).astype(BF)
+            both_ref[at, D:] = (g[xy].astype(F32) * valid).astype(BF)
+        return 0
+
+    lax.fori_loop(0, 16, fill, 0)
+    both = both_ref[...]
+    gram_ref[...] = dot_tn(both, both)
+
+
+def orth_kernel(where_ref, told_ref, gram_ref, o_own_ref, piece_ref, out_ref):
     xy = where_ref[2]
-    is_out = where_ref[3]
-    factor = factor_ref[0]
-    row = lax.broadcasted_iota(jnp.int32, (GROUP, D), 0) % BLOCK
-    valid = ((is_out == 0) | (row >= 9)).astype(F32)
-
-    def fill(at, total):
-        for s, (g, o) in enumerate(((g_own_ref, o_own_ref), (g_oth_ref, o_oth_ref))):
-            m = MOMENTUM * group_rows(o, 0, at) + factor * (g[at].astype(F32) * valid)
-            total = total + m * m
-            m_ref[pl.ds(pl.multiple_of(s * 768 + at * GROUP, 16), GROUP), :] = m.astype(BF)
-        return total
-
-    total = lax.fori_loop(0, 16, fill, jnp.zeros((GROUP, D), F32))
-    inv = 1.0 / (jnp.sqrt(jnp.sum(total)) + 1e-07)
-    whole = m_ref[...]
-    gram = dot_tn(whole, whole) * (inv * inv)
+    valid = valid_rows(where_ref[3])
+    factor = clip(told_ref)[1]
+    gram = (
+        (MOMENTUM * MOMENTUM) * gram_ref[:D, :D]
+        + (MOMENTUM * factor) * (gram_ref[:D, D:] + gram_ref[D:, :D])
+        + (factor * factor) * gram_ref[D:, D:]
+    )
     eye = (
         lax.broadcasted_iota(jnp.int32, (D, D), 0) == lax.broadcasted_iota(jnp.int32, (D, D), 1)
     ).astype(F32)
+    inv = 1.0 / (jnp.sqrt(jnp.sum(gram * eye)) + 1e-07)
+    gram = gram * (inv * inv)
     run = None
     for step in range(NS_STEPS):
         parts = halves(gram)
@@ -339,25 +411,65 @@
         if step < NS_STEPS - 1:
             gram = product(halves(product(poly_parts, parts)), poly_parts)
     mine = MOMENTUM * group_rows(o_own_ref, 0, xy) + factor * (piece_ref[...] * valid)
-    out_ref[...] = product(halves(mine * inv), halves(run))
-    grad_ref[...] = piece_ref[...] * valid
-
-
-def run_orth(where, factor, g_own, g_oth, o_own, o_oth, piece):
-    smem = pl.BlockSpec(memory_space=pltpu.SMEM)
-    vmem = pl.BlockSpec(memory_space=pltpu.VMEM)
-    return pl.pallas_call(
-        orth_kernel,
-        out_shape=(jax.ShapeDtypeStruct((GROUP, D), F32), jax.ShapeDtypeStruct((GROUP, D), F32)),
-        in_specs=[smem] * 2 + [vmem] * 5,
-        out_specs=(vmem, vmem),
-        scratch_shapes=[pltpu.VMEM((1536, D), BF)],
-        compiler_params=pltpu.CompilerParams(vmem_limit_bytes=VMEM),
-        cost_estimate=pl.CostEstimate(
-            flops=8_000_000_000, bytes_accessed=4_000_000, transcendentals=0
-        ),
-        name="orth",
-    )(where, factor, g_own, g_oth, o_own, o_oth, piece)
+    orth = product(halves(mine * inv), halves(run))
+    for z in range(4):
+        out_ref[z] = jnp.concatenate(
+            [orth[z * BLOCK : (z + 1) * BLOCK], jnp.zeros((4, D), F32)], axis=0
+        ).astype(BF)
+
+
+def step_rate(rows_count, cols_count):
+    return math.sqrt(max(rows_count, cols_count) / rows_count)
+
+
+def update_kernel(
+    told_ref,
+    back_ref,
+    qkv_ref,
+    out_ref,
+    up_ref,
+    down_ref,
+    qkv_m_ref,
+    out_m_ref,
+    up_m_ref,
+    down_m_ref,
+    norms_ref,
+    norm_m_ref,
+    table_ref,
+    pos_m_ref,
+    grad_norm_ref,
+    qkv_m_next,
+    qkv_next,
+    out_m_next,
+    out_next,
+    up_m_next,
+    up_next,
+    down_m_next,
+    down_next,
+    norm_m_next,
+    norms_next,
+    pos_m_next,
+    table_next,
+):
+    grad_norm, factor = clip(told_ref)
+    grad_norm_ref[...] = grad_norm
+    for z, first, last, rate, w_ref, m_ref, w_next, m_next in (
+        (3, 0, 9, step_rate(D, 3 * D), qkv_ref, qkv_m_ref, qkv_next, qkv_m_next),
+        (1, 9, 12, step_rate(D, D), out_ref, out_m_ref, out_next, out_m_next),
+        (0, 0, 12, step_rate(D, FF), up_ref, up_m_ref, up_next, up_m_next),
+        (2, 0, 12, step_rate(FF, D), down_ref, down_m_ref, down_next, down_m_next),
+    ):
+        grad = told_ref[z].astype(F32)[64 + first : 64 + last]
+        orth = back_ref[z].astype(F32)[first:last]
+        m_next[...] = MOMENTUM * m_ref[...] + factor * grad
+        w_next[...] = w_ref[...] - rate * orth
+    small = told_ref[1].astype(F32)
+    norm_fresh = MOMENTUM * norm_m_ref[...] + factor * small[50:54]
+    norm_m_next[...] = norm_fresh
+    norms_next[...] = norms_ref[...] - NORM_RATE * norm_fresh
+    pos_fresh = MOMENTUM * pos_m_ref[...] + factor * small[:50]
+    pos_m_next[...] = pos_fresh
+    table_next[...] = table_ref[...] - SMALL_RATE * pos_fresh
 
 
 def swapped(value):
@@ -371,14 +483,6 @@
 def everywhere(value, axes):
     peers = lax.axis_size(axes)
     return exchanged(jnp.broadcast_to(value[None], (peers, *value.shape)), axes)
-
-
-def step_rate(rows_count, cols_count):
-    return math.sqrt(max(rows_count, cols_count) / rows_count)
-
-
-def padded(rows, before, total):
-    return jnp.pad(rows, ((before, total - before - rows.shape[0]), (0, 0)))
 
 
 def shards(
@@ -400,28 +504,24 @@
     offsets,
     pos_index,
 ):
-    z = lax.axis_index(COLUMN)
-    xy = lax.axis_index(PLANE)
-    zh = lax.axis_index("zh")
-    is_out = (z == 1).astype(jnp.int32)
-    where = jnp.stack([lax.axis_index("c"), zh, xy, is_out]).astype(jnp.int32)
-
-    rows = jnp.concatenate([up_weight.T, down_weight, qkv_weight.T, out_weight], axis=0).astype(BF)
-    own = everywhere(padded(rows, 0, SENT), CHIPS)
+    is_out = (lax.axis_index(COLUMN) == 1).astype(jnp.int32)
+    where = jnp.stack(
+        [lax.axis_index("c"), lax.axis_index("zh"), lax.axis_index(PLANE), is_out]
+    ).astype(jnp.int32)
+    weights = (qkv_weight.T, out_weight, up_weight.T, down_weight)
+    moments = (qkv_moment.T, out_moment, up_moment.T, down_moment)
+
+    rows, old = call(
+        prepare_kernel,
+        "prepare",
+        (((64, SENT, D), BF), ((64, 16, D), BF)),
+        weights + moments,
+        moved=4_000_000,
+    )
+    own = exchanged(rows, CHIPS)
+    own, old = lax.optimization_barrier((own, old))
     other = swapped(own)
-
-    old = jnp.stack(
-        [
-            padded(up_moment.T, 0, 16),
-            padded(out_moment, 9, 16),
-            padded(down_moment, 0, 16),
-            padded(qkv_moment.T, 0, 16),
-        ]
-    ).astype(BF)
-    old = exchanged(
-        jnp.broadcast_to(old[:, None], (4, 16, 16, D)).reshape(64, 16, D), CHIPS
-    )
-    old_other = swapped(old)
+    old = exchanged(old, CHIPS)
 
     result, in_grad, keep, send = run_layer(
         where,
@@ -429,63 +529,67 @@
         offsets,
         tokens,
         cotangent,
-        padded(pos_table, 0, 64),
+        jnp.pad(pos_table, ((0, 14), (0, 0))),
         norm_params,
         pos_index.reshape(1, -1),
         own,
         other,
     )
-    pair = (keep + swapped(send).astype(F32)).astype(BF)
+    keep, send, old = lax.optimization_barrier((keep, send, old))
+    old_other = swapped(old)
+    pair = (keep.astype(F32) + swapped(send).astype(F32)).astype(BF)
     piece = jnp.sum(exchanged(pair, HALF).astype(F32), axis=0)
     grads = everywhere(piece.astype(BF), PLANE)
     grads_other = swapped(grads)
 
-    small = grads.reshape(16, 4, BLOCK, D)[:, :, 0].reshape(64, D).astype(F32)
-    valid = (is_out == 0) | (jnp.arange(GROUP)[None, :, None] % BLOCK >= 9)
-    wide = jnp.where(valid, grads.astype(F32), 0.0)
-    wide_other = jnp.where(valid, grads_other.astype(F32), 0.0)
-    squares = jnp.sum(wide * wide) + jnp.sum(wide_other * wide_other)
-    squares = squares + jnp.where(is_out == 1, jnp.sum(small * small), 0.0)
-    message = jnp.concatenate([small, jnp.broadcast_to(squares, (8, D))], axis=0)
-    told = everywhere(message, COLUMN)
-    grad_norm = jnp.sqrt(jnp.sum(told[:, 64, 0]))
-    factor = jnp.minimum(1.0, CLIP_LIMIT / (grad_norm + 1e-06))
-    pos_sum, norm_sum = told[1, :50], told[1, 50:54]
-
-    orth, grad = run_orth(
-        where, factor.reshape(1), grads, grads_other, old, old_other, piece
-    )
-    back = exchanged(
-        jnp.concatenate([orth.reshape(4, BLOCK, D), grad.reshape(4, BLOCK, D)], axis=1), COLUMN
-    )
-
-    def fresh(moment, z_from, first, last, turn):
-        block = back[z_from, BLOCK + first : BLOCK + last]
-        return MOMENTUM * moment + factor * (block.T if turn else block)
-
-    def stepped(weight, z_from, first, last, turn, rate):
-        block = back[z_from, first:last]
-        return weight - rate * (block.T if turn else block)
-
-    norm_fresh = MOMENTUM * norm_moment + factor * norm_sum
-    pos_fresh = MOMENTUM * pos_moment + factor * pos_sum
-    return (
-        result,
-        in_grad,
-        grad_norm,
-        fresh(qkv_moment, 3, 0, 9, True),
-        stepped(qkv_weight, 3, 0, 9, True, step_rate(D, 3 * D)),
-        fresh(out_moment, 1, 9, 12, False),
-        stepped(out_weight, 1, 9, 12, False, step_rate(D, D)),
-        fresh(up_moment, 0, 0, 12, True),
-        stepped(up_weight, 0, 0, 12, True, step_rate(D, FF)),
-        fresh(down_moment, 2, 0, 12, False),
-        stepped(down_weight, 2, 0, 12, False, step_rate(FF, D)),
-        norm_fresh,
-        norm_params - NORM_RATE * norm_fresh,
-        pos_fresh,
-        pos_table - SMALL_RATE * pos_fresh,
-    )
+    small = jnp.asarray(small_places(), BF)
+    (told,) = call(
+        tell_kernel,
+        "tell",
+        (((4, 80, D), BF),),
+        (where, grads, grads_other, piece, small),
+        scalars=1,
+        moved=2_000_000,
+    )
+    told = exchanged(told, COLUMN)
+    (gram,) = call(
+        gram_kernel,
+        "gram",
+        (((2 * D, 2 * D), F32),),
+        (where, grads, grads_other, old, old_other),
+        scalars=1,
+        scratch=[pltpu.VMEM((1536, 2 * D), BF)],
+        flops=3_000_000_000,
+        moved=5_000_000,
+    )
+    (orth,) = call(
+        orth_kernel,
+        "orth",
+        (((4, 16, D), BF),),
+        (where, told, gram, old, piece),
+        scalars=1,
+        flops=8_000_000_000,
+        moved=4_000_000,
+    )
+    back = exchanged(orth, COLUMN)
+    like = lambda a: (a.shape, F32)
+    grad_norm, *news = call(
+        update_kernel,
+        "update",
+        (
+            ((1, 1), F32),
+            *(like(a) for pair_of in zip(moments, weights) for a in pair_of),
+            like(norm_moment),
+            like(norm_params),
+            like(pos_moment),
+            like(pos_table),
+        ),
+        (told, back, *weights, *moments, norm_params, norm_moment, pos_table, pos_moment),
+        moved=2_000_000,
+    )
+    for k in (0, 1, 4, 5):
+        news[k] = news[k].T
+    return (result, in_grad, grad_norm.reshape(()), *news)
 
 
 def solution(mesh):

time: 182 us -> 162 us (0.89)
  waiting for transfers between devices: 53.4 us -> 16.6 us
  blocking collectives: 51.6 us -> 77.3 us
  Pallas kernels: 34.1 us -> 45.8 us
  other arithmetic: 13.5 us -> 2.36 us
  starting transfers between devices: 18.5 us -> 14.5 us
  between operations: 4.79 us -> 0.9 us
    all_to_all x4 -> x3, waiting for transfers between devices: 47.6 us -> 11.7 us  [exchanged(): return lax.all_to_all(value, axes, 0, 0, tiled=True)]
    all_to_all x2 -> x3, blocking collectives: 51.6 us -> 77.3 us  [exchanged(): return lax.all_to_all(value, axes, 0, 0, tiled=True)]
    pallas_call x1 -> x5, Pallas kernels: 15.8 us -> 27.9 us  [call(): pl.pallas_call(kernel, out_shape=tuple((jax.ShapeDtypeStruct(shape, dtype...]
    all_to_all x4 -> x3, starting transfers between devices: 18.2 us -> 14.1 us  [exchanged(): return lax.all_to_all(value, axes, 0, 0, tiled=True)]
    sub x6 -> x0, other arithmetic: 3.77 us -> none  [the longest x4 2.48 us: stepped(): return weight - rate * (block.T if turn else block)]
    unnamed x34 -> x16, local copies, waits for them, and re-layouts: 0.08 us -> 2.43 us
    reduce_sum x3 -> x0, other arithmetic: 2.32 us -> none  [the longest x1 1.09 us: shards(): squares = jnp.sum(wide * wide) + jnp.sum(wide_other * wide_other)]
    reshape x2 -> x0, local copies, waits for them, and re-layouts: 1.83 us -> none  [the longest x1 0.94 us: shards(): orth.reshape(4, BLOCK, D)]
  transfers between devices with their start and end apart: 8 -> 7, of which waited for: 6 -> 4; matrix products, arithmetic and copies ran while one was open for 3% -> 1% of each run, Pallas kernels for 0% -> 16%
where the time goes in v1:
time: 162 us; the launch traced here: 161 us
  blocking collectives  77.3 us (48%)
  Pallas kernels  45.8 us (28%)
  waiting for transfers between devices  16.6 us (10%)
  starting transfers between devices  14.5 us (9%)
  local copies, waits for them, and re-layouts  3.96 us (2%)
  other arithmetic  2.36 us (1%)
    all_to_all x3, blocking collectives, exchanged(): return lax.all_to_all(value, axes, 0, 0, tiled=True)  77.3 us
    pallas_call x5, Pallas kernels, call(): pl.pallas_call(kernel, out_shape=tuple((jax.ShapeDtypeStruct(shape, dtype...  27.9 us
    pallas_call x1, Pallas kernels, run_layer(): pl.pallas_call(layer_kernel, out_shape=(jax.ShapeDtypeStruct((count, D),...  17.9 us
    all_to_all x3, starting transfers between devices, exchanged(): return lax.all_to_all(value, axes, 0, 0, tiled=True)  14.1 us
    all_to_all x3, waiting for transfers between devices, exchanged(): return lax.all_to_all(value, axes, 0, 0, tiled=True)  11.7 us
    ppermute x4, waiting for transfers between devices, swapped(): return lax.ppermute(value, 'c', [(0, 1), (1, 0)])  4.83 us
  transfers between devices with their start and end apart: 7, of which 4 were waited for; matrix products, arithmetic and copies ran while one was open for 1% of the time, Pallas kernels for 16%

profile of v1, /device:TPU:0, one launch (start us, length us, event | category | flops | bytes accessed | tf_op | source)
XLA Modules:
  0.0 161.4 jit_solution(1914759664868572428)
XLA Ops:
  0.6 2.6 %prepare.1 = (bf16[64,40,384]{2,1,0:T(8,128)(2,1)}, bf16[64,16,384]{2,1,0:T(8,128)(2,1)}) custom-call(f32[9,384]{1,0:T(8,128)} %bitcast.14, f32[3,384]{1,0:T(4,128)} %out_ref.3, f32[12,384]{1,0:T(8,128)} %bitcast.16, f32[12,384]{1,0:T(8,128)} %down_ref.3, f32[9,384]{1,0:T(8,128)} %bitcast.18, f32[3,384]{1,0:T(4,128)} %out_m_ref.3, f32[12,384]{1,0:T(8,128)} %bitcast.20, ...), custom_call_target="tpu_custom_call" | custom-call | bytes 4000000 | tf_op jit(solution)/shard_map/prepare/pallas_call | solution.py:313
  3.3 39.9 %all_to_all.30.own_ref = bf16[64,40,384]{2,1,0:T(8,128)(2,1)S(1)} all-to-all(bf16[64,40,384]{2,1,0:T(8,128)(2,1)} %get-tuple-element.39), channel_id=1, replica_groups=mesh['zl'=2,'x'=4,'y'=4,'c'=2,'zh'=2] {'zh','zl','x','y'}, dimensions={0} | all-to-all | bytes 3932160 | tf_op jit(solution)/shard_map/all_to_all | solution.py:480
  43.1 0.0 collective-permute-start
  43.2 6.2 %all-to-all-start.1 = ((bf16[64,16,384]{2,1,0:T(8,128)(2,1)}), bf16[64,16,384]{2,1,0:T(8,128)(2,1)S(1)}, u32[]{:S(2)}, u32[]{:S(2)}) async-start(bf16[64,16,384]{2,1,0:T(8,128)(2,1)} %get-tuple-element.46), calls=%async_computation.1 | async-start | bytes 1572864 | tf_op jit(solution)/shard_map/all_to_all | solution.py:480
  49.3 0.0 copy-done.6
  49.3 0.6 pad.4.table_ref
  50.0 0.6 pad_add_fusion.where_ref
  50.6 0.0 collective-permute-done.oth_ref
  50.6 17.9 %layer.1 = (bf16[256,384]{1,0:T(8,128)(2,1)}, f32[256,384]{1,0:T(8,128)}, bf16[32,48,384]{2,1,0:T(8,128)(2,1)}, bf16[32,48,384]{2,1,0:T(8,128)(2,1)}) custom-call(s32[4]{0:T(128)} %pad_add_fusion.where_ref, s32[5]{0:T(128)} %res_ref.1, s32[5]{0:T(128)} %off_ref.1, bf16[256,384]{1,0:T(8,128)(2,1)} %tok_ref.1, bf16[256,384]{1,0:T(8,128)(2,1)} %cot_ref.1, ...), custom_call_target="tpu_custom_call" | custom-call | flops 6000000000 | bytes 16000000 | tf_op jit(solution)/shard_map/layer/pallas_call | solution.py:278
  68.5 0.0 all-to-all-done.1.o_own_ref
  68.5 0.3 collective-permute-start.1
  68.8 2.8 %collective-permute-done.1 = bf16[32,48,384]{2,1,0:T(8,128)(2,1)S(1)} collective-permute-done((bf16[32,48,384]{2,1,0:T(8,128)(2,1)}, bf16[32,48,384]{2,1,0:T(8,128)(2,1)S(1)}, u32[]{:S(2)}, u32[]{:S(2)}) %collective-permute-start.1) | collective-permute-done | bytes 1179680 | tf_op jit(solution)/shard_map/ppermute | solution.py:476
  71.6 1.6 add_convert_fusion
  73.2 27.1 %all_to_all.31 = bf16[32,48,384]{2,1,0:T(8,128)(2,1)S(1)} all-to-all(bf16[32,48,384]{2,1,0:T(8,128)(2,1)S(1)} %add_convert_fusion), channel_id=1, replica_groups=mesh['zl'=2,'x'=4,'y'=4,'c'=2,'zh'=2] {'zl','x','y'}, dimensions={0} | all-to-all | bytes 2359296 | tf_op jit(solution)/shard_map/all_to_all | solution.py:480
  100.3 0.2 convert_reduce_fusion.piece_ref
  100.5 0.9 broadcast_in_dim.2
  101.4 3.8 %all-to-all-start.3 = ((bf16[16,48,384]{2,1,0:T(8,128)(2,1)}), bf16[16,48,384]{2,1,0:T(8,128)(2,1)S(1)}, u32[]{:S(2)}, u32[]{:S(2)}) async-start(bf16[16,48,384]{2,1,0:T(8,128)(2,1)} %broadcast_in_dim.2), calls=%async_computation.3 | async-start | bytes 1179648 | tf_op jit(solution)/shard_map/all_to_all | solution.py:480
  105.2 0.1 collective-permute-start.3
  105.3 11.6 %all-to-all-done.3.own_ref.g_own_ref = bf16[16,48,384]{2,1,0:T(8,128)(2,1)S(1)} async-done(((bf16[16,48,384]{2,1,0:T(8,128)(2,1)}), bf16[16,48,384]{2,1,0:T(8,128)(2,1)S(1)}, u32[]{:S(2)}, u32[]{:S(2)}) %all-to-all-start.3) | async-done | bytes 589856 | tf_op jit(solution)/shard_map/all_to_all | solution.py:480
  116.9 0.0 collective-permute-start.2
  116.9 2.0 %collective-permute-done.2.oth_ref.g_oth_ref = bf16[16,48,384]{2,1,0:T(8,128)(2,1)S(1)} collective-permute-done((bf16[16,48,384]{2,1,0:T(8,128)(2,1)S(1)}, bf16[16,48,384]{2,1,0:T(8,128)(2,1)S(1)}, u32[]{:S(2)}, u32[]{:S(2)}) %collective-permute-start.2) | collective-permute-done | bytes 589856 | tf_op jit(solution)/shard_map/ppermute | solution.py:476
  118.9 0.8 copy-done.5
  119.8 2.6 %tell.1 = bf16[4,80,384]{2,1,0:T(8,128)(2,1)} custom-call(s32[4]{0:T(128)} %pad_add_fusion.where_ref, bf16[16,48,384]{2,1,0:T(8,128)(2,1)} %copy-done, bf16[16,48,384]{2,1,0:T(8,128)(2,1)} %copy-done.5, f32[48,384]{1,0:T(8,128)} %copy-done.4, bf16[768,64]{1,0:T(8,128)(2,1)} %constant.34.clone.small_ref), custom_call_target="tpu_custom_call" | custom-call | bytes 2000000 | tf_op jit(solution)/shard_map/tell/pallas_call | solution.py:313
  122.4 4.2 %all-to-all-start.4 = ((bf16[4,80,384]{2,1,0:T(8,128)(2,1)}), bf16[4,80,384]{2,1,0:T(8,128)(2,1)S(1)}, u32[]{:S(2)}, u32[]{:S(2)}) async-start(bf16[4,80,384]{2,1,0:T(8,128)(2,1)} %tell.1), calls=%async_computation.4 | async-start | bytes 491520 | tf_op jit(solution)/shard_map/all_to_all | solution.py:480
  126.6 0.0 collective-permute-done.3.o_oth_ref
  126.6 0.9 copy-done.7
  127.5 5.8 %gram.1.gram_ref = f32[768,768]{1,0:T(8,128)} custom-call(s32[4]{0:T(128)} %pad_add_fusion.where_ref, bf16[16,48,384]{2,1,0:T(8,128)(2,1)} %copy-done, bf16[16,48,384]{2,1,0:T(8,128)(2,1)} %copy-done.5, bf16[64,16,384]{2,1,0:T(8,128)(2,1)} %copy-done.3, bf16[64,16,384]{2,1,0:T(8,128)(2,1)} %copy-done.7), custom_call_target="tpu_custom_call" | custom-call | flops 3000000000 | bytes 5000000 | tf_op jit(solution)/shard_map/gram/pallas_call | solution.py:313
  133.2 0.1 all-to-all-done.4.told_ref
  133.4 0.7 copy-done.2
  134.1 14.9 %orth.1 = bf16[4,16,384]{2,1,0:T(8,128)(2,1)} custom-call(s32[4]{0:T(128)} %pad_add_fusion.where_ref, bf16[4,80,384]{2,1,0:T(8,128)(2,1)} %copy-done.2, f32[768,768]{1,0:T(8,128)} %gram.1.gram_ref, bf16[64,16,384]{2,1,0:T(8,128)(2,1)} %copy-done.3, f32[48,384]{1,0:T(8,128)} %copy-done.4), custom_call_target="tpu_custom_call" | custom-call | flops 8000000000 | bytes 4000000 | tf_op jit(solution)/shard_map/orth/pallas_call | solution.py:313
  148.9 10.3 %all_to_all.32.back_ref = bf16[4,16,384]{2,1,0:T(8,128)(2,1)} all-to-all(bf16[4,16,384]{2,1,0:T(8,128)(2,1)} %orth.1), channel_id=1, replica_groups=mesh['zl'=2,'x'=4,'y'=4,'c'=2,'zh'=2] {'zh','zl'}, dimensions={0} | all-to-all | bytes 98304 | tf_op jit(solution)/shard_map/all_to_all | solution.py:480
  159.3 2.0 %update.1 = (f32[1,1]{1,0:T(1,128)}, f32[9,384]{1,0:T(8,128)}, f32[9,384]{1,0:T(8,128)}, f32[3,384]{1,0:T(4,128)}, f32[3,384]{1,0:T(4,128)}, /*index=5*/f32[12,3...) custom-call(bf16[4,80,384]{2,1,0:T(8,128)(2,1)} %copy-done.2, ...), custom_call_target="tpu_custom_call" | custom-call | bytes 2000000 | tf_op jit(solution)/shard_map/update/pallas_call | solution.py:313
  (13 shorter events, 0.0 us)
Async XLA Ops:
  3.3 46.1 %copy-start.6 = (f32[50,384]{1,0:T(8,128)S(1)}, f32[50,384]{1,0:T(8,128)}, u32[]{:S(2)}) copy-start(f32[50,384]{1,0:T(8,128)} %table_ref.1) | copy-start | bytes 230404
  43.1 7.4 %copy-start.1 = (bf16[64,40,384]{2,1,0:T(8,128)(2,1)}, bf16[64,40,384]{2,1,0:T(8,128)(2,1)S(1)}, u32[]{:S(2)}) copy-start(bf16[64,40,384]{2,1,0:T(8,128)(2,1)S(1)} %all_to_all.30.own_ref) | copy-start | bytes 5898244
  43.1 7.4 %collective-permute-start = (bf16[64,40,384]{2,1,0:T(8,128)(2,1)S(1)}, bf16[64,40,384]{2,1,0:T(8,128)(2,1)}, u32[]{:S(2)}, u32[]{:S(2)}) collective-permute-start(bf16[64,40,384]{2,1,0:T(8,128)(2,1)S(1)} %all_to_all.30.own_ref), channel_id=1, source_target_pairs={{0,2},{2,0},{1,3},{3,1},{4,6},{6,4},{5,7},{7,5},{8,10},{10,8},{9,1... | collective-permute-start | bytes 5898248 | tf_op jit(solution)/shard_map/ppermute | solution.py:476
  43.2 25.3 %all-to-all-start.1 = ((bf16[64,16,384]{2,1,0:T(8,128)(2,1)}), bf16[64,16,384]{2,1,0:T(8,128)(2,1)S(1)}, u32[]{:S(2)}, u32[]{:S(2)}) async-start(bf16[64,16,384]{2,1,0:T(8,128)(2,1)} %get-tuple-element.46), calls=%async_computation.1 | async-start | bytes 1572864 | tf_op jit(solution)/shard_map/all_to_all | solution.py:480
  68.5 36.7 %copy-start.3 = (bf16[64,16,384]{2,1,0:T(8,128)(2,1)}, bf16[64,16,384]{2,1,0:T(8,128)(2,1)S(1)}, u32[]{:S(2)}) copy-start(bf16[64,16,384]{2,1,0:T(8,128)(2,1)S(1)} %all-to-all-done.1.o_own_ref) | copy-start | bytes 2359300
  68.5 3.1 %collective-permute-start.1 = (bf16[32,48,384]{2,1,0:T(8,128)(2,1)}, bf16[32,48,384]{2,1,0:T(8,128)(2,1)S(1)}, u32[]{:S(2)}, u32[]{:S(2)}) collective-permute-start(bf16[32,48,384]{2,1,0:T(8,128)(2,1)} %get-tuple-element.48), channel_id=1, source_target_pairs={{0,2},{2,0},{1,3},{3,1},{4,6},{6,4},{5,7},{7,5},{8,10},{10,8},{9,1... | collective-permute-start | bytes 3538952 | tf_op jit(solution)/shard_map/ppermute | solution.py:476
  100.5 18.4 %copy-start.4 = (f32[48,384]{1,0:T(8,128)}, f32[48,384]{1,0:T(8,128)S(1)}, u32[]{:S(2)}) copy-start(f32[48,384]{1,0:T(8,128)S(1)} %convert_reduce_fusion.piece_ref) | copy-start | bytes 221188
  101.4 15.5 %all-to-all-start.3 = ((bf16[16,48,384]{2,1,0:T(8,128)(2,1)}), bf16[16,48,384]{2,1,0:T(8,128)(2,1)S(1)}, u32[]{:S(2)}, u32[]{:S(2)}) async-start(bf16[16,48,384]{2,1,0:T(8,128)(2,1)} %broadcast_in_dim.2), calls=%async_computation.3 | async-start | bytes 1179648 | tf_op jit(solution)/shard_map/all_to_all | solution.py:480
  105.2 21.3 %collective-permute-start.3 = (bf16[64,16,384]{2,1,0:T(8,128)(2,1)S(1)}, bf16[64,16,384]{2,1,0:T(8,128)(2,1)S(1)}, u32[]{:S(2)}, u32[]{:S(2)}) collective-permute-start(bf16[64,16,384]{2,1,0:T(8,128)(2,1)S(1)} %all-to-all-done.1.o_own_ref), channel_id=1, source_target_pairs={{0,2},{2,0},{1,3},{3,1},{4,6},{6,4},{5,7},{7,5},{8,10},{10,8},{9,1... | collective-permute-start | bytes 2359304 | tf_op jit(solution)/shard_map/ppermute | solution.py:476
  116.9 2.0 %copy-start = (bf16[16,48,384]{2,1,0:T(8,128)(2,1)}, bf16[16,48,384]{2,1,0:T(8,128)(2,1)S(1)}, u32[]{:S(2)}) copy-start(bf16[16,48,384]{2,1,0:T(8,128)(2,1)S(1)} %all-to-all-done.3.own_ref.g_own_ref) | copy-start | bytes 1769476
  116.9 2.0 %collective-permute-start.2 = (bf16[16,48,384]{2,1,0:T(8,128)(2,1)S(1)}, bf16[16,48,384]{2,1,0:T(8,128)(2,1)S(1)}, u32[]{:S(2)}, u32[]{:S(2)}) collective-permute-start(bf16[16,48,384]{2,1,0:T(8,128)(2,1)S(1)} %all-to-all-done.3.own_ref.g_own_ref), channel_id=1, source_target_pairs={{0,2},{2,0},{1,3},{3,1},{4,6},{6,4},{5,7},{7,5},{8,10},{10,8},{9,1... | collective-permute-start | bytes 1769480 | tf_op jit(solution)/shard_map/ppermute | solution.py:476
  118.9 0.8 copy-start.5
  122.4 10.9 %all-to-all-start.4 = ((bf16[4,80,384]{2,1,0:T(8,128)(2,1)}), bf16[4,80,384]{2,1,0:T(8,128)(2,1)S(1)}, u32[]{:S(2)}, u32[]{:S(2)}) async-start(bf16[4,80,384]{2,1,0:T(8,128)(2,1)} %tell.1), calls=%async_computation.4 | async-start | bytes 491520 | tf_op jit(solution)/shard_map/all_to_all | solution.py:480
  126.6 0.9 copy-start.7
  133.4 0.7 copy-start.2

commit v2 on v1

--- a/solution.py
+++ b/solution.py
@@ -30,7 +30,8 @@
 COLUMN = ("zh", "zl")
 PLANE = ("x", "y")
 HALF = ("zl", "x", "y")
-CHIPS = ("zh", "zl", "x", "y")
+COLUMN_CORES = ("zh", "zl", "c")
+AXES = ("zl", "x", "y", "c", "zh")
 
 BF = jnp.bfloat16
 F32 = jnp.float32
@@ -38,6 +39,7 @@
 GROUP = 48
 SENT = 40
 VMEM = 60 << 20
+LAYER_VMEM = 60 << 20
 
 
 def unit_places():
@@ -95,24 +97,57 @@
     )
 
 
-def group_rows(source, first, xy):
-    return jnp.concatenate(
-        [source[z * 16 + xy].astype(F32)[first : first + BLOCK] for z in range(4)], axis=0
-    )
+def device(x, y, z, core):
+    x, y, z = x % 4, y % 4, z % 4
+    return ((((z % 2) * 4 + x) * 4 + y) * 2 + core) * 2 + z // 2
+
+
+def devices():
+    return [(x, y, z, c) for x in range(4) for y in range(4) for z in range(4) for c in range(2)]
+
+
+def column_step(step):
+    return [(device(x, y, z + step, c), device(x, y, z, c)) for x, y, z, c in devices()]
+
+
+def colour_groups():
+    return [
+        [device(x, y, x + 2 * y - colour, core) for x in range(4) for y in range(4)]
+        for colour in range(4)
+        for core in range(2)
+    ]
+
+
+def colour_step(step):
+    sources = {
+        1: ((1, 0, 0), (0, 0, -1)),
+        2: ((0, 1, 0), (0, -1, 0)),
+        3: ((-1, 0, 0), (0, 0, 1)),
+    }[step]
+    return [
+        (device(x + sources[c][0], y + sources[c][1], z + sources[c][2], c), device(x, y, z, c))
+        for x, y, z, c in devices()
+    ]
 
 
 def layer_kernel(
     where_ref,
     res_ref,
     off_ref,
-    tok_ref,
-    cot_ref,
-    table_ref,
+    tok_hbm,
+    cot_hbm,
+    table_hbm,
     norms_ref,
     pos_ref,
-    own_ref,
-    oth_ref,
-    places_ref,
+    own0,
+    own1,
+    own2,
+    own3,
+    oth0,
+    oth1,
+    oth2,
+    oth3,
+    places_hbm,
     small_ref,
     result_ref,
     in_grad_ref,
@@ -125,20 +160,43 @@
     qkv_ref,
     ctx_ref,
     dqkv_ref,
+    places_ref,
+    tok_ref,
+    cot_ref,
+    table_ref,
+    sems,
 ):
     core = where_ref[0]
     half = where_ref[1]
+    colour = where_ref[4]
     count = tok_ref.shape[0]
-
-    for s, src in enumerate((own_ref, oth_ref)):
-
-        def regroup(xy, _, s=s, src=src):
-            at = pl.multiple_of(s * 768 + xy * GROUP, 16)
-            for first, dst in ((0, wup), (12, wdn), (24, wat)):
-                dst[pl.ds(at, GROUP), :] = group_rows(src, first, xy).astype(BF)
-            return 0
-
-        lax.fori_loop(0, 16, regroup, 0)
+    loads = [
+        pltpu.make_async_copy(src, dst, sems.at[k])
+        for k, (src, dst) in enumerate(
+            ((tok_hbm, tok_ref), (places_hbm, places_ref), (cot_hbm, cot_ref))
+        )
+    ]
+    for load in loads:
+        load.start()
+    table_ref[...] = jnp.zeros(table_ref.shape, F32)
+    table_ref[: table_hbm.shape[0]] = table_hbm[...]
+
+    for here in range(4):
+
+        @pl.when(colour == here)
+        def _(here=here):
+            for s, refs in enumerate(((own0, own1, own2, own3), (oth0, oth1, oth2, oth3))):
+                for xy in range(16):
+                    ahead = xy // 4 + 2 * (xy % 4) - here
+                    blocks = [refs[(ahead - z) % 4][xy].astype(F32) for z in range(4)]
+                    at = s * 768 + xy * GROUP
+                    for first, dst in ((0, wup), (12, wdn), (24, wat)):
+                        dst[at : at + GROUP] = jnp.concatenate(
+                            [block[first : first + BLOCK] for block in blocks], axis=0
+                        ).astype(BF)
+
+    for load in loads:
+        load.wait()
 
     def place(s):
         return core if s == 0 else 1 - core
@@ -269,12 +327,13 @@
             send_ref[16:] = grad.astype(BF)
 
 
-def run_layer(where, res_ids, offsets, tokens, cotangent, table, norms, pos, own, other):
+def run_layer(where, res_ids, offsets, tokens, cotangent, table, norms, pos, weights):
     count = tokens.shape[0]
     places = jnp.asarray(unit_places(), BF)
     small = jnp.asarray(small_places(), BF)
     smem = pl.BlockSpec(memory_space=pltpu.SMEM)
     vmem = pl.BlockSpec(memory_space=pltpu.VMEM)
+    hbm = pl.BlockSpec(memory_space=pl.ANY)
     return pl.pallas_call(
         layer_kernel,
         out_shape=(
@@ -283,7 +342,7 @@
             jax.ShapeDtypeStruct((32, GROUP, D), BF),
             jax.ShapeDtypeStruct((32, GROUP, D), BF),
         ),
-        in_specs=[smem] * 3 + [vmem] * 9,
+        in_specs=[smem] * 3 + [hbm] * 2 + [vmem] * 11 + [hbm, vmem],
         out_specs=(vmem,) * 4,
         scratch_shapes=[
             pltpu.VMEM((1536, D), BF),
@@ -293,13 +352,20 @@
             pltpu.VMEM((count, 1152), BF),
             pltpu.VMEM((count, D), BF),
             pltpu.VMEM((count, 1152), BF),
+            pltpu.VMEM((2, 768, 1536), BF),
+            pltpu.VMEM((count, D), BF),
+            pltpu.VMEM((count, D), BF),
+            pltpu.VMEM((64, D), F32),
+            pltpu.SemaphoreType.DMA((3,)),
         ],
-        compiler_params=pltpu.CompilerParams(vmem_limit_bytes=VMEM),
+        compiler_params=pltpu.CompilerParams(vmem_limit_bytes=LAYER_VMEM),
         cost_estimate=pl.CostEstimate(
-            flops=6_000_000_000, bytes_accessed=16_000_000, transcendentals=2_000_000
+            flops=0, bytes_accessed=0, transcendentals=0
         ),
         name="layer",
-    )(where, res_ids, offsets, tokens, cotangent, table, norms, pos, own, other, places, small)
+    )(
+        where, res_ids, offsets, tokens, cotangent, table, norms, pos, *weights, places, small
+    )
 
 
 def product(a, b):
@@ -322,99 +388,137 @@
     )(*args)
 
 
-def prepare_kernel(qkv_ref, out_ref, up_ref, down_ref, qkv_m_ref, out_m_ref, up_m_ref, down_m_ref, rows_ref, old_ref):
+def prepare_kernel(
+    where_ref,
+    qkv_ref,
+    out_ref,
+    up_ref,
+    down_ref,
+    qkv_m_ref,
+    out_m_ref,
+    up_m_ref,
+    down_m_ref,
+    rows_ref,
+    *old_refs,
+):
     zeros = jnp.zeros((16, D), F32)
     rows = jnp.concatenate(
         [up_ref[...], down_ref[...], qkv_ref[...], out_ref[...], zeros[: SENT - 36]], axis=0
     ).astype(BF)
     rows_ref[...] = jnp.broadcast_to(rows[None], rows_ref.shape)
     old = (
-        jnp.concatenate([up_m_ref[...], zeros[:4]], axis=0),
-        jnp.concatenate([zeros[:9], out_m_ref[...], zeros[:4]], axis=0),
-        jnp.concatenate([down_m_ref[...], zeros[:4]], axis=0),
-        jnp.concatenate([qkv_m_ref[...], zeros[:7]], axis=0),
+        up_m_ref[...],
+        jnp.concatenate([zeros[:9], out_m_ref[...]], axis=0),
+        down_m_ref[...],
+        jnp.concatenate([qkv_m_ref[...], zeros[:3]], axis=0),
     )
     for z in range(4):
-        old_ref[z * 16 : (z + 1) * 16] = jnp.broadcast_to(old[z].astype(BF)[None], (16, 16, D))
+
+        @pl.when(where_ref[3] == z)
+        def _(z=z):
+            for step, ref in enumerate(old_refs):
+                ref[...] = old[(z - step) % 4].astype(BF)
+
+
+def join_kernel(where_ref, *refs):
+    *sources, joined_ref = refs
+    for z in range(4):
+
+        @pl.when(where_ref[3] == z)
+        def _(z=z):
+            joined_ref[...] = jnp.concatenate(
+                [sources[(at - z) % 4][...].astype(F32) for at in range(4)], axis=0
+            ).astype(BF)
 
 
 def valid_rows(is_out):
     row = lax.broadcasted_iota(jnp.int32, (GROUP, D), 0) % BLOCK
-    return ((is_out == 0) | (row >= 9)).astype(F32)
-
-
-def tell_kernel(where_ref, own_ref, oth_ref, piece_ref, small_ref, told_ref):
-    is_out = where_ref[3]
+    return (jnp.logical_not(is_out) | (row >= 9)).astype(F32)
+
+
+def tell_kernel(where_ref, own_ref, piece_ref, small_ref, told_ref):
+    is_out = where_ref[3] == 1
     valid = valid_rows(is_out)
     total = jnp.zeros((GROUP, D), F32)
     for xy in range(16):
-        for ref in (own_ref, oth_ref):
-            g = ref[xy].astype(F32) * valid
-            total = total + g * g
-    small = dot_tn(small_ref[...], own_ref[...].reshape(768, D))
-    squares = jnp.sum(total) + jnp.where(is_out == 1, jnp.sum(small * small), 0.0)
+        g = own_ref[xy].astype(F32) * valid
+        total = total + g * g
+    small = dot(small_ref[...], own_ref[...].reshape(768, D))
+    counted = jnp.where(is_out & (where_ref[0] == 0), 1.0, 0.0)
+    squares = jnp.sum(total) + counted * jnp.sum(small * small)
     squares = jnp.full((1, D), squares, F32)
     high = squares.astype(BF).astype(F32)
     mid = (squares - high).astype(BF).astype(F32)
     low = squares - high - mid
     for z in range(4):
-        told_ref[z] = jnp.concatenate(
+        rows = jnp.concatenate(
             [small, piece_ref[z * BLOCK : (z + 1) * BLOCK, :], high, mid, low, jnp.zeros((1, D), F32)],
             axis=0,
         ).astype(BF)
+        told_ref[2 * z] = rows
+        told_ref[2 * z + 1] = rows
 
 
 def clip(told_ref):
     total = jnp.zeros((1, 1), F32)
-    for z in range(4):
-        for k in range(3):
-            total = total + told_ref[z, 76 + k : 77 + k, :].astype(F32)[:, :1]
+    for k in range(8):
+        last = told_ref[k, 64:, :].astype(F32)
+        total = total + (last[12:13, :1] + last[13:14, :1] + last[14:15, :1])
     grad_norm = jnp.sqrt(total)
     return grad_norm, jnp.minimum(1.0, CLIP_LIMIT / (grad_norm + 1e-06))
 
 
-def gram_kernel(where_ref, g_own_ref, g_oth_ref, o_own_ref, o_oth_ref, gram_ref, both_ref):
-    valid = valid_rows(where_ref[3])
-
-    def fill(xy, _):
-        for s, (g, o) in enumerate(((g_own_ref, o_own_ref), (g_oth_ref, o_oth_ref))):
-            at = pl.ds(pl.multiple_of(s * 768 + xy * GROUP, 16), GROUP)
-            both_ref[at, :D] = group_rows(o, 0, xy).astype(BF)
-            both_ref[at, D:] = (g[xy].astype(F32) * valid).astype(BF)
-        return 0
-
-    lax.fori_loop(0, 16, fill, 0)
-    both = both_ref[...]
-    gram_ref[...] = dot_tn(both, both)
-
-
-def orth_kernel(where_ref, told_ref, gram_ref, o_own_ref, piece_ref, out_ref):
-    xy = where_ref[2]
-    valid = valid_rows(where_ref[3])
+def gram_kernel(where_ref, own_ref, oth_ref, old_own_ref, old_oth_ref, gram_ref, grad_ref, old_ref):
+    valid = valid_rows(where_ref[3] == 1)
+    for s, (g_ref, o_ref) in enumerate(((own_ref, old_own_ref), (oth_ref, old_oth_ref))):
+        for xy in range(16):
+            at = s * 768 + xy * GROUP
+            grad_ref[at : at + GROUP] = (g_ref[xy].astype(F32) * valid).astype(BF)
+        old_ref[s * 768 : (s + 1) * 768] = o_ref[...].reshape(768, D)
+    grad = grad_ref[...]
+    old = old_ref[...]
+    cross = dot_tn(grad, old)
+    gram_ref[0] = dot_tn(old, old)
+    gram_ref[1] = cross + cross.T
+    gram_ref[2] = dot_tn(grad, grad)
+
+
+def left_parts(parts):
+    return jnp.concatenate([parts[0], parts[0], parts[1]], axis=1)
+
+
+def right_parts(parts):
+    return jnp.concatenate([parts[0], parts[1], parts[0]], axis=0)
+
+
+def orth_kernel(where_ref, told_ref, gram_ref, old_ref, piece_ref, out_ref):
+    valid = valid_rows(where_ref[3] == 1)
     factor = clip(told_ref)[1]
     gram = (
-        (MOMENTUM * MOMENTUM) * gram_ref[:D, :D]
-        + (MOMENTUM * factor) * (gram_ref[:D, D:] + gram_ref[D:, :D])
-        + (factor * factor) * gram_ref[D:, D:]
+        (MOMENTUM * MOMENTUM) * gram_ref[0]
+        + (MOMENTUM * factor) * gram_ref[1]
+        + (factor * factor) * gram_ref[2]
     )
     eye = (
         lax.broadcasted_iota(jnp.int32, (D, D), 0) == lax.broadcasted_iota(jnp.int32, (D, D), 1)
     ).astype(F32)
     inv = 1.0 / (jnp.sqrt(jnp.sum(gram * eye)) + 1e-07)
     gram = gram * (inv * inv)
-    run = None
+    mine = (MOMENTUM * old_ref[...].astype(F32) + factor * (piece_ref[...] * valid)) * inv
     for step in range(NS_STEPS):
         parts = halves(gram)
-        poly = COEF_A * eye + COEF_B * gram + COEF_C * product(parts, parts)
-        poly_parts = halves(poly)
-        run = poly if run is None else product(poly_parts, halves(run))
+        right = right_parts(parts)
+        poly = halves(COEF_A * eye + COEF_B * gram + COEF_C * dot(left_parts(parts), right))
         if step < NS_STEPS - 1:
-            gram = product(halves(product(poly_parts, parts)), poly_parts)
-    mine = MOMENTUM * group_rows(o_own_ref, 0, xy) + factor * (piece_ref[...] * valid)
-    orth = product(halves(mine * inv), halves(run))
+            turned = halves(dot(left_parts(poly), right))
+            left = jnp.concatenate([left_parts(turned), left_parts(halves(mine))], axis=0)
+            both = dot(left, right_parts(poly))
+            gram, mine = both[:D], both[D:]
+        else:
+            mine = dot(left_parts(halves(mine)), right_parts(poly))
     for z in range(4):
         out_ref[z] = jnp.concatenate(
-            [orth[z * BLOCK : (z + 1) * BLOCK], jnp.zeros((4, D), F32)], axis=0
+            [mine[z * BLOCK : (z + 1) * BLOCK], jnp.zeros((4, D), F32)], axis=0
         ).astype(BF)
 
 
@@ -423,6 +527,7 @@
 
 
 def update_kernel(
+    where_ref,
     told_ref,
     back_ref,
     qkv_ref,
@@ -459,11 +564,11 @@
         (0, 0, 12, step_rate(D, FF), up_ref, up_m_ref, up_next, up_m_next),
         (2, 0, 12, step_rate(FF, D), down_ref, down_m_ref, down_next, down_m_next),
     ):
-        grad = told_ref[z].astype(F32)[64 + first : 64 + last]
+        grad = told_ref[2 * z + where_ref[0], 64:, :].astype(F32)[first:last]
         orth = back_ref[z].astype(F32)[first:last]
         m_next[...] = MOMENTUM * m_ref[...] + factor * grad
         w_next[...] = w_ref[...] - rate * orth
-    small = told_ref[1].astype(F32)
+    small = told_ref[2, :64, :].astype(F32)
     norm_fresh = MOMENTUM * norm_m_ref[...] + factor * small[50:54]
     norm_m_next[...] = norm_fresh
     norms_next[...] = norms_ref[...] - NORM_RATE * norm_fresh
@@ -504,24 +609,30 @@
     offsets,
     pos_index,
 ):
-    is_out = (lax.axis_index(COLUMN) == 1).astype(jnp.int32)
+    z = lax.axis_index(COLUMN)
+    colour = (lax.axis_index("x") + 2 * lax.axis_index("y") - z) % 4
     where = jnp.stack(
-        [lax.axis_index("c"), lax.axis_index("zh"), lax.axis_index(PLANE), is_out]
+        [lax.axis_index("c"), lax.axis_index("zh"), lax.axis_index(PLANE), z, colour]
     ).astype(jnp.int32)
     weights = (qkv_weight.T, out_weight, up_weight.T, down_weight)
     moments = (qkv_moment.T, out_moment, up_moment.T, down_moment)
 
-    rows, old = call(
+    rows, *old = call(
         prepare_kernel,
         "prepare",
-        (((64, SENT, D), BF), ((64, 16, D), BF)),
-        weights + moments,
+        (((16, SENT, D), BF), *(((BLOCK, D), BF) for _ in range(4))),
+        (where, *weights, *moments),
+        scalars=1,
         moved=4_000_000,
     )
-    own = exchanged(rows, CHIPS)
-    own, old = lax.optimization_barrier((own, old))
-    other = swapped(own)
-    old = exchanged(old, CHIPS)
+    old = [old[0]] + [lax.ppermute(old[k], AXES, column_step(k)) for k in (1, 2, 3)]
+    (old,) = call(join_kernel, "join", (((GROUP, D), BF),), (where, *old), scalars=1)
+
+    own = [lax.all_to_all(rows, AXES, 0, 0, axis_index_groups=colour_groups(), tiled=True)]
+    own[0], old = lax.optimization_barrier((own[0], old))
+    own += [lax.ppermute(own[0], AXES, colour_step(step)) for step in (1, 2, 3)]
+    other = [swapped(value) for value in own]
+    old_own = everywhere(old, PLANE)
 
     result, in_grad, keep, send = run_layer(
         where,
@@ -529,36 +640,34 @@
         offsets,
         tokens,
         cotangent,
-        jnp.pad(pos_table, ((0, 14), (0, 0))),
+        pos_table,
         norm_params,
         pos_index.reshape(1, -1),
-        own,
-        other,
-    )
-    keep, send, old = lax.optimization_barrier((keep, send, old))
-    old_other = swapped(old)
+        (*own, *other),
+    )
+    keep, send, old_own = lax.optimization_barrier((keep, send, old_own))
+    old_other = swapped(old_own)
     pair = (keep.astype(F32) + swapped(send).astype(F32)).astype(BF)
     piece = jnp.sum(exchanged(pair, HALF).astype(F32), axis=0)
     grads = everywhere(piece.astype(BF), PLANE)
     grads_other = swapped(grads)
 
-    small = jnp.asarray(small_places(), BF)
     (told,) = call(
         tell_kernel,
         "tell",
-        (((4, 80, D), BF),),
-        (where, grads, grads_other, piece, small),
+        (((8, 80, D), BF),),
+        (where, grads, piece, jnp.asarray(small_places().T, BF)),
         scalars=1,
         moved=2_000_000,
     )
-    told = exchanged(told, COLUMN)
+    told = exchanged(told, COLUMN_CORES)
     (gram,) = call(
         gram_kernel,
         "gram",
-        (((2 * D, 2 * D), F32),),
-        (where, grads, grads_other, old, old_other),
+        (((3, D, D), F32),),
+        (where, grads, grads_other, old_own, old_other),
         scalars=1,
-        scratch=[pltpu.VMEM((1536, 2 * D), BF)],
+        scratch=[pltpu.VMEM((1536, D), BF), pltpu.VMEM((1536, D), BF)],
         flops=3_000_000_000,
         moved=5_000_000,
     )
@@ -584,7 +693,8 @@
             like(pos_moment),
             like(pos_table),
         ),
-        (told, back, *weights, *moments, norm_params, norm_moment, pos_table, pos_moment),
+        (where, told, back, *weights, *moments, norm_params, norm_moment, pos_table, pos_moment),
+        scalars=1,
         moved=2_000_000,
     )
     for k in (0, 1, 4, 5):

time: 162 us -> 150 us (0.926)
  blocking collectives: 77.3 us -> 34.9 us
  starting transfers between devices: 14.5 us -> 30.4 us
  waiting for transfers between devices: 16.6 us -> 31.5 us
  Pallas kernels: 45.8 us -> 41.4 us
  local copies, waits for them, and re-layouts: 3.96 us -> 7.83 us
    all_to_all x3 -> x2, blocking collectives: 77.3 us -> 34.9 us  [exchanged(): return lax.all_to_all(value, axes, 0, 0, tiled=True)]
    all_to_all x0 -> x1, starting transfers between devices: none -> 10.4 us  [shards(): lax.all_to_all(rows, AXES, 0, 0, axis_index_groups=colour_groups(), tiled...]
    ppermute x0 -> x6, waiting for transfers between devices: none -> 9.98 us  [the longest x3 5.58 us: shards(): lax.ppermute(old[k], AXES, column_step(k))]
    ppermute x0 -> x6, starting transfers between devices: none -> 8.13 us  [the longest x3 4.97 us: shards(): own += [lax.ppermute(own[0], AXES, colour_step(step)) for step in (1, 2, 3)]]
    pallas_call x5 -> x6, Pallas kernels: 27.9 us -> 23.3 us  [call(): pl.pallas_call(kernel, out_shape=tuple((jax.ShapeDtypeStruct(shape, dtype...]
    all_to_all x3, starting transfers between devices: 14.1 us -> 10.9 us  [exchanged(): return lax.all_to_all(value, axes, 0, 0, tiled=True)]
    all_to_all x3, waiting for transfers between devices: 11.7 us -> 15 us  [exchanged(): return lax.all_to_all(value, axes, 0, 0, tiled=True)]
    unnamed x16 -> x34, local copies, waits for them, and re-layouts: 2.43 us -> 4.66 us
  transfers between devices with their start and end apart: 7 -> 17, of which waited for: 4 -> 9; matrix products, arithmetic and copies ran while one was open for 1% -> 1% of each run, Pallas kernels for 16% -> 18%
where the time goes in v2:
time: 150 us; the launch traced here: 149 us
  Pallas kernels  41.4 us (28%)
  blocking collectives  34.9 us (23%)
  waiting for transfers between devices  31.5 us (21%)
  starting transfers between devices  30.4 us (20%)
  local copies, waits for them, and re-layouts  7.83 us (5%)
  other arithmetic  1.78 us (1%)
    all_to_all x2, blocking collectives, exchanged(): return lax.all_to_all(value, axes, 0, 0, tiled=True)  34.9 us
    pallas_call x6, Pallas kernels, call(): pl.pallas_call(kernel, out_shape=tuple((jax.ShapeDtypeStruct(shape, dtype...  23.3 us
    pallas_call x1, Pallas kernels, run_layer(): pl.pallas_call(layer_kernel, out_shape=(jax.ShapeDtypeStruct((count, D),...  18 us
    all_to_all x3, waiting for transfers between devices, exchanged(): return lax.all_to_all(value, axes, 0, 0, tiled=True)  15 us
    all_to_all x3, starting transfers between devices, exchanged(): return lax.all_to_all(value, axes, 0, 0, tiled=True)  10.9 us
    all_to_all x1, starting transfers between devices, shards(): lax.all_to_all(rows, AXES, 0, 0, axis_index_groups=colour_groups(), tiled...  10.4 us
    ppermute x3, waiting for transfers between devices, shards(): lax.ppermute(old[k], AXES, column_step(k))  5.58 us
    ppermute x3, starting transfers between devices, shards(): own += [lax.ppermute(own[0], AXES, colour_step(step)) for step in (1, 2, 3)]  4.97 us
  transfers between devices with their start and end apart: 17, of which 9 were waited for; matrix products, arithmetic and copies ran while one was open for 1% of the time, Pallas kernels for 18%

profile of v2, /device:TPU:0, one launch (start us, length us, event | category | flops | bytes accessed | tf_op | source)
XLA Modules:
  0.0 148.9 jit_solution(9075060586949702625)
XLA Ops:
  1.3 1.7 %prepare.1 = (bf16[16,40,384]{2,1,0:T(8,128)(2,1)}, bf16[12,384]{1,0:T(8,128)(2,1)}, bf16[12,384]{1,0:T(8,128)(2,1)}, bf16[12,384]{1,0:T(8,128)(2,1)}, bf16[12,384]{1,0:T(8,128)(2,1)}) custom-call(s32[5]{0:T(128)} %stack.23.where_ref, f32[9,384]{1,0:T(8,128)} %bitcast.15, f32[3,384]{1,0:T(4,128)} %out_ref.3, f32[12,384]{1,0:T(8,128)} %bitcast.17, ...), custom_call_target="tpu_custom_call" | custom-call | bytes 4000000 | tf_op jit(solution)/shard_map/prepare/pallas_call | solution.py:379
  3.1 10.4 %all-to-all-start = ((bf16[16,40,384]{2,1,0:T(8,128)(2,1)}), bf16[16,40,384]{2,1,0:T(8,128)(2,1)S(1)}, u32[]{:S(2)}, u32[]{:S(2)}) async-start(bf16[16,40,384]{2,1,0:T(8,128)(2,1)} %get-tuple-element.42), calls=%async_computation | async-start | bytes 983040 | tf_op jit(solution)/shard_map/all_to_all | solution.py:631
  14.3 2.4 %collective-permute-start.1 = (bf16[12,384]{1,0:T(8,128)(2,1)}, bf16[12,384]{1,0:T(8,128)(2,1)S(1)}, u32[]{:S(2)}, u32[]{:S(2)}) collective-permute-start(bf16[12,384]{1,0:T(8,128)(2,1)} %get-tuple-element.45), channel_id=1, source_target_pairs={{1,0},{3,2},{65,64},{67,66},{0,1},{2,3},{64,65},{66,67},{5,4},{7,6... | collective-permute-start | bytes 27656 | tf_op jit(solution)/shard_map/ppermute | solution.py:628
  16.7 2.0 %collective-permute-done.refs_1_ = bf16[12,384]{1,0:T(8,128)(2,1)S(1)} collective-permute-done((bf16[12,384]{1,0:T(8,128)(2,1)}, bf16[12,384]{1,0:T(8,128)(2,1)S(1)}, u32[]{:S(2)}, u32[]{:S(2)}) %collective-permute-start) | collective-permute-done | bytes 9248 | tf_op jit(solution)/shard_map/ppermute | solution.py:628
  18.7 3.4 %collective-permute-done.1.refs_2_ = bf16[12,384]{1,0:T(8,128)(2,1)S(1)} collective-permute-done((bf16[12,384]{1,0:T(8,128)(2,1)}, bf16[12,384]{1,0:T(8,128)(2,1)S(1)}, u32[]{:S(2)}, u32[]{:S(2)}) %collective-permute-start.1) | collective-permute-done | bytes 9248 | tf_op jit(solution)/shard_map/ppermute | solution.py:628
  22.9 1.5 join.1.old_ref
  24.3 1.8 %all-to-all-done.own0 = bf16[16,40,384]{2,1,0:T(8,128)(2,1)S(1)} async-done(((bf16[16,40,384]{2,1,0:T(8,128)(2,1)}), bf16[16,40,384]{2,1,0:T(8,128)(2,1)S(1)}, u32[]{:S(2)}, u32[]{:S(2)}) %all-to-all-start) | async-done | bytes 491552 | tf_op jit(solution)/shard_map/all_to_all | solution.py:631
  26.7 2.7 %collective-permute-start.4 = (bf16[16,40,384]{2,1,0:T(8,128)(2,1)S(1)}, bf16[16,40,384]{2,1,0:T(8,128)(2,1)S(1)}, u32[]{:S(2)}, u32[]{:S(2)}) collective-permute-start(bf16[16,40,384]{2,1,0:T(8,128)(2,1)S(1)} %all-to-all-done.own0), channel_id=1, source_target_pairs={{4,0},{14,2},{68,64},{78,66},{5,1},{15,3},{69,65},{79,67},{8,4},{2... | collective-permute-start | bytes 1474568 | tf_op jit(solution)/shard_map/ppermute | solution.py:633
  29.4 1.7 %collective-permute-start.3 = (bf16[16,40,384]{2,1,0:T(8,128)(2,1)S(1)}, bf16[16,40,384]{2,1,0:T(8,128)(2,1)S(1)}, u32[]{:S(2)}, u32[]{:S(2)}) collective-permute-start(bf16[16,40,384]{2,1,0:T(8,128)(2,1)S(1)} %all-to-all-done.own0), channel_id=1, source_target_pairs={{16,0},{67,2},{80,64},{2,66},{17,1},{66,3},{81,65},{3,67},{20,4},{... | collective-permute-start | bytes 1474568 | tf_op jit(solution)/shard_map/ppermute | solution.py:633
  31.1 1.6 %broadcast_in_dim.4 = bf16[16,48,384]{2,1,0:T(8,128)(2,1)} broadcast(bf16[48,384]{1,0:T(8,128)(2,1)} %join.1.old_ref), dimensions={1,2} | broadcast | bytes 626688 | tf_op jit(solution)/shard_map/broadcast_in_dim | solution.py:590
  32.7 3.6 %all-to-all-start.1 = ((bf16[16,48,384]{2,1,0:T(8,128)(2,1)}), bf16[16,48,384]{2,1,0:T(8,128)(2,1)S(1)}, u32[]{:S(2)}, u32[]{:S(2)}) async-start(bf16[16,48,384]{2,1,0:T(8,128)(2,1)} %broadcast_in_dim.4), calls=%async_computation.1 | async-start | bytes 1179648 | tf_op jit(solution)/shard_map/all_to_all | solution.py:585
  37.0 4.4 %collective-permute-done.3.own1 = bf16[16,40,384]{2,1,0:T(8,128)(2,1)S(1)} collective-permute-done((bf16[16,40,384]{2,1,0:T(8,128)(2,1)S(1)}, bf16[16,40,384]{2,1,0:T(8,128)(2,1)S(1)}, u32[]{:S(2)}, u32[]{:S(2)}) %collective-permute-start.3) | collective-permute-done | bytes 491552 | tf_op jit(solution)/shard_map/ppermute | solution.py:633
  41.5 1.8 %collective-permute-done.7.oth1 = bf16[16,40,384]{2,1,0:T(8,128)(2,1)S(1)} collective-permute-done((bf16[16,40,384]{2,1,0:T(8,128)(2,1)S(1)}, bf16[16,40,384]{2,1,0:T(8,128)(2,1)S(1)}, u32[]{:S(2)}, u32[]{:S(2)}) %collective-permute-start.7) | collective-permute-done | bytes 491552 | tf_op jit(solution)/shard_map/ppermute | solution.py:581
  43.3 0.8 copy-done.11
  44.1 18.0 %layer.1 = (bf16[256,384]{1,0:T(8,128)(2,1)}, f32[256,384]{1,0:T(8,128)}, bf16[32,48,384]{2,1,0:T(8,128)(2,1)}, bf16[32,48,384]{2,1,0:T(8,128)(2,1)}) custom-call(s32[5]{0:T(128)} %stack.23.where_ref, s32[5]{0:T(128)} %res_ref.1, s32[5]{0:T(128)} %off_ref.1, bf16[256,384]{1,0:T(8,128)(2,1)} %tok_hbm.1, bf16[256,384]{1,0:T(8,128)(2,1)} %cot_hbm.1, ...), custom_call_target="tpu_custom_call" | custom-call | tf_op jit(solution)/shard_map/layer/pallas_call | solution.py:337
  62.4 2.9 %collective-permute-done.10 = bf16[32,48,384]{2,1,0:T(8,128)(2,1)S(1)} collective-permute-done((bf16[32,48,384]{2,1,0:T(8,128)(2,1)}, bf16[32,48,384]{2,1,0:T(8,128)(2,1)S(1)}, u32[]{:S(2)}, u32[]{:S(2)}) %collective-permute-start.10) | collective-permute-done | bytes 1179680 | tf_op jit(solution)/shard_map/ppermute | solution.py:581
  65.3 1.6 %add_convert_fusion = bf16[32,48,384]{2,1,0:T(8,128)(2,1)S(1)} fusion(bf16[32,48,384]{2,1,0:T(8,128)(2,1)S(1)} %collective-permute-done.10, bf16[32,48,384]{2,1,0:T(8,128)(2,1)} %get-tuple-element.53), kind=kLoop, calls=%fused_computation.1 | loop fusion | flops 2359296 | bytes 3538944 | tf_op jit(solution)/shard_map/convert_element_type | solution.py:650
  66.9 25.5 %all_to_all.30 = bf16[32,48,384]{2,1,0:T(8,128)(2,1)S(1)} all-to-all(bf16[32,48,384]{2,1,0:T(8,128)(2,1)S(1)} %add_convert_fusion), channel_id=1, replica_groups=mesh['zl'=2,'x'=4,'y'=4,'c'=2,'zh'=2] {'zl','x','y'}, dimensions={0} | all-to-all | bytes 2359296 | tf_op jit(solution)/shard_map/all_to_all | solution.py:585
  92.6 0.9 broadcast_in_dim.5
  93.4 3.8 %all-to-all-start.3 = ((bf16[16,48,384]{2,1,0:T(8,128)(2,1)}), bf16[16,48,384]{2,1,0:T(8,128)(2,1)S(1)}, u32[]{:S(2)}, u32[]{:S(2)}) async-start(bf16[16,48,384]{2,1,0:T(8,128)(2,1)} %broadcast_in_dim.5), calls=%async_computation.3 | async-start | bytes 1179648 | tf_op jit(solution)/shard_map/all_to_all | solution.py:585
  97.4 11.6 %all-to-all-done.3.own_ref = bf16[16,48,384]{2,1,0:T(8,128)(2,1)S(1)} async-done(((bf16[16,48,384]{2,1,0:T(8,128)(2,1)}), bf16[16,48,384]{2,1,0:T(8,128)(2,1)S(1)}, u32[]{:S(2)}, u32[]{:S(2)}) %all-to-all-start.3) | async-done | bytes 589856 | tf_op jit(solution)/shard_map/all_to_all | solution.py:585
  109.0 0.8 copy-done
  109.8 2.4 %tell.1 = bf16[8,80,384]{2,1,0:T(8,128)(2,1)} custom-call(s32[5]{0:T(128)} %stack.23.where_ref, bf16[16,48,384]{2,1,0:T(8,128)(2,1)} %copy-done, f32[48,384]{1,0:T(8,128)} %copy-done.3, bf16[64,768]{1,0:T(8,128)(2,1)} %constant.44.clone.small_ref), custom_call_target="tpu_custom_call" | custom-call | bytes 2000000 | tf_op jit(solution)/shard_map/tell/pallas_call | solution.py:379
  112.1 3.5 %all-to-all-start.4 = ((bf16[8,80,384]{2,1,0:T(8,128)(2,1)}), bf16[8,80,384]{2,1,0:T(8,128)(2,1)S(1)}, u32[]{:S(2)}, u32[]{:S(2)}) async-start(bf16[8,80,384]{2,1,0:T(8,128)(2,1)} %tell.1), calls=%async_computation.4 | async-start | bytes 983040 | tf_op jit(solution)/shard_map/all_to_all | solution.py:585
  115.7 0.8 copy-done.15
  116.5 0.8 copy-done.16
  117.3 4.9 %gram.1.gram_ref = f32[3,384,384]{2,1,0:T(8,128)} custom-call(s32[5]{0:T(128)} %stack.23.where_ref, bf16[16,48,384]{2,1,0:T(8,128)(2,1)} %copy-done, bf16[16,48,384]{2,1,0:T(8,128)(2,1)} %copy-done.16, bf16[16,48,384]{2,1,0:T(8,128)(2,1)} %copy-done.4, bf16[16,48,384]{2,1,0:T(8,128)(2,1)} %copy-done.15), custom_call_target="tpu_custom_call" | custom-call | flops 3000000000 | bytes 5000000 | tf_op jit(solution)/shard_map/gram/pallas_call | solution.py:379
  122.2 3.3 %all-to-all-done.4.told_ref = bf16[8,80,384]{2,1,0:T(8,128)(2,1)S(1)} async-done(((bf16[8,80,384]{2,1,0:T(8,128)(2,1)}), bf16[8,80,384]{2,1,0:T(8,128)(2,1)S(1)}, u32[]{:S(2)}, u32[]{:S(2)}) %all-to-all-start.4) | async-done | bytes 491552 | tf_op jit(solution)/shard_map/all_to_all | solution.py:585
  125.6 0.8 copy-done.2
  126.4 10.8 %orth.1 = bf16[4,16,384]{2,1,0:T(8,128)(2,1)} custom-call(s32[5]{0:T(128)} %stack.23.where_ref, bf16[8,80,384]{2,1,0:T(8,128)(2,1)} %copy-done.2, f32[3,384,384]{2,1,0:T(8,128)} %gram.1.gram_ref, bf16[48,384]{1,0:T(8,128)(2,1)} %join.1.old_ref, f32[48,384]{1,0:T(8,128)} %copy-done.3), custom_call_target="tpu_custom_call" | custom-call | flops 8000000000 | bytes 4000000 | tf_op jit(solution)/shard_map/orth/pallas_call | solution.py:379
  137.2 9.5 %all_to_all.31.back_ref = bf16[4,16,384]{2,1,0:T(8,128)(2,1)} all-to-all(bf16[4,16,384]{2,1,0:T(8,128)(2,1)} %orth.1), channel_id=1, replica_groups=mesh['zl'=2,'x'=4,'y'=4,'c'=2,'zh'=2] {'zh','zl'}, dimensions={0} | all-to-all | bytes 98304 | tf_op jit(solution)/shard_map/all_to_all | solution.py:585
  146.7 2.0 %update.1 = (f32[1,1]{1,0:T(1,128)}, f32[9,384]{1,0:T(8,128)}, f32[9,384]{1,0:T(8,128)}, f32[3,384]{1,0:T(4,128)}, f32[3,384]{1,0:T(4,128)}, /*index=5*/f32[12,3...) custom-call(s32[5]{0:T(128)} %stack.23.where_ref, ...), custom_call_target="tpu_custom_call" | custom-call | bytes 2000000 | tf_op jit(solution)/shard_map/update/pallas_call | solution.py:379
  (51 shorter events, 4.0 us)
Async XLA Ops:
  3.1 23.0 %all-to-all-start = ((bf16[16,40,384]{2,1,0:T(8,128)(2,1)}), bf16[16,40,384]{2,1,0:T(8,128)(2,1)S(1)}, u32[]{:S(2)}, u32[]{:S(2)}) async-start(bf16[16,40,384]{2,1,0:T(8,128)(2,1)} %get-tuple-element.42), calls=%async_computation | async-start | bytes 983040 | tf_op jit(solution)/shard_map/all_to_all | solution.py:631
  13.5 5.2 %collective-permute-start = (bf16[12,384]{1,0:T(8,128)(2,1)}, bf16[12,384]{1,0:T(8,128)(2,1)S(1)}, u32[]{:S(2)}, u32[]{:S(2)}) collective-permute-start(bf16[12,384]{1,0:T(8,128)(2,1)} %get-tuple-element.44), channel_id=1, source_target_pairs={{64,0},{66,2},{1,64},{3,66},{65,1},{67,3},{0,65},{2,67},{68,4},{70... | collective-permute-start | bytes 27656 | tf_op jit(solution)/shard_map/ppermute | solution.py:628
  14.3 7.8 %collective-permute-start.1 = (bf16[12,384]{1,0:T(8,128)(2,1)}, bf16[12,384]{1,0:T(8,128)(2,1)S(1)}, u32[]{:S(2)}, u32[]{:S(2)}) collective-permute-start(bf16[12,384]{1,0:T(8,128)(2,1)} %get-tuple-element.45), channel_id=1, source_target_pairs={{1,0},{3,2},{65,64},{67,66},{0,1},{2,3},{64,65},{66,67},{5,4},{7,6... | collective-permute-start | bytes 27656 | tf_op jit(solution)/shard_map/ppermute | solution.py:628
  16.7 5.6 %collective-permute-start.2 = (bf16[12,384]{1,0:T(8,128)(2,1)}, bf16[12,384]{1,0:T(8,128)(2,1)S(1)}, u32[]{:S(2)}, u32[]{:S(2)}) collective-permute-start(bf16[12,384]{1,0:T(8,128)(2,1)} %get-tuple-element.46), channel_id=1, source_target_pairs={{65,0},{67,2},{0,64},{2,66},{64,1},{66,3},{1,65},{3,67},{69,4},{71... | collective-permute-start | bytes 27656 | tf_op jit(solution)/shard_map/ppermute | solution.py:628
  18.7 3.6 %copy-start.12 = (bf16[12,384]{1,0:T(8,128)(2,1)}, bf16[12,384]{1,0:T(8,128)(2,1)S(1)}, u32[]{:S(2)}) copy-start(bf16[12,384]{1,0:T(8,128)(2,1)S(1)} %collective-permute-done.refs_1_) | copy-start | bytes 27652
  26.1 18.0 %copy-start.1 = (bf16[16,40,384]{2,1,0:T(8,128)(2,1)}, bf16[16,40,384]{2,1,0:T(8,128)(2,1)S(1)}, u32[]{:S(2)}) copy-start(bf16[16,40,384]{2,1,0:T(8,128)(2,1)S(1)} %all-to-all-done.own0) | copy-start | bytes 1474564
  26.1 10.3 %collective-permute-start.5 = (bf16[16,40,384]{2,1,0:T(8,128)(2,1)S(1)}, bf16[16,40,384]{2,1,0:T(8,128)(2,1)S(1)}, u32[]{:S(2)}, u32[]{:S(2)}) collective-permute-start(bf16[16,40,384]{2,1,0:T(8,128)(2,1)S(1)} %all-to-all-done.own0), channel_id=1, source_target_pairs={{48,0},{66,2},{112,64},{3,66},{49,1},{67,3},{113,65},{2,67},{52,4}... | collective-permute-start | bytes 1474568 | tf_op jit(solution)/shard_map/ppermute | solution.py:633
  26.7 10.2 %collective-permute-start.4 = (bf16[16,40,384]{2,1,0:T(8,128)(2,1)S(1)}, bf16[16,40,384]{2,1,0:T(8,128)(2,1)S(1)}, u32[]{:S(2)}, u32[]{:S(2)}) collective-permute-start(bf16[16,40,384]{2,1,0:T(8,128)(2,1)S(1)} %all-to-all-done.own0), channel_id=1, source_target_pairs={{4,0},{14,2},{68,64},{78,66},{5,1},{15,3},{69,65},{79,67},{8,4},{2... | collective-permute-start | bytes 1474568 | tf_op jit(solution)/shard_map/ppermute | solution.py:633
  29.4 12.0 %collective-permute-start.3 = (bf16[16,40,384]{2,1,0:T(8,128)(2,1)S(1)}, bf16[16,40,384]{2,1,0:T(8,128)(2,1)S(1)}, u32[]{:S(2)}, u32[]{:S(2)}) collective-permute-start(bf16[16,40,384]{2,1,0:T(8,128)(2,1)S(1)} %all-to-all-done.own0), channel_id=1, source_target_pairs={{16,0},{67,2},{80,64},{2,66},{17,1},{66,3},{81,65},{3,67},{20,4},{... | collective-permute-start | bytes 1474568 | tf_op jit(solution)/shard_map/ppermute | solution.py:633
  32.7 29.4 %all-to-all-start.1 = ((bf16[16,48,384]{2,1,0:T(8,128)(2,1)}), bf16[16,48,384]{2,1,0:T(8,128)(2,1)S(1)}, u32[]{:S(2)}, u32[]{:S(2)}) async-start(bf16[16,48,384]{2,1,0:T(8,128)(2,1)} %broadcast_in_dim.4), calls=%async_computation.1 | async-start | bytes 1179648 | tf_op jit(solution)/shard_map/all_to_all | solution.py:585
  36.3 5.1 %collective-permute-start.6 = (bf16[16,40,384]{2,1,0:T(8,128)(2,1)S(1)}, bf16[16,40,384]{2,1,0:T(8,128)(2,1)S(1)}, u32[]{:S(2)}, u32[]{:S(2)}) collective-permute-start(bf16[16,40,384]{2,1,0:T(8,128)(2,1)S(1)} %all-to-all-done.own0), channel_id=1, source_target_pairs={{0,2},{2,0},{1,3},{3,1},{4,6},{6,4},{5,7},{7,5},{8,10},{10,8},{9,1... | collective-permute-start | bytes 1474568 | tf_op jit(solution)/shard_map/ppermute | solution.py:581
  36.4 7.7 %copy-start.5 = (bf16[16,40,384]{2,1,0:T(8,128)(2,1)}, bf16[16,40,384]{2,1,0:T(8,128)(2,1)S(1)}, u32[]{:S(2)}) copy-start(bf16[16,40,384]{2,1,0:T(8,128)(2,1)S(1)} %collective-permute-done.5.own3) | copy-start | bytes 1474564
  36.4 5.0 %collective-permute-start.9 = (bf16[16,40,384]{2,1,0:T(8,128)(2,1)S(1)}, bf16[16,40,384]{2,1,0:T(8,128)(2,1)S(1)}, u32[]{:S(2)}, u32[]{:S(2)}) collective-permute-start(bf16[16,40,384]{2,1,0:T(8,128)(2,1)S(1)} %collective-permute-done.5.own3), channel_id=1, source_target_pairs={{0,2},{2,0},{1,3},{3,1},{4,6},{6,4},{5,7},{7,5},{8,10},{10,8},{9,1... | collective-permute-start | bytes 1474568 | tf_op jit(solution)/shard_map/ppermute | solution.py:581
  36.9 7.2 %copy-start.6 = (bf16[16,40,384]{2,1,0:T(8,128)(2,1)}, bf16[16,40,384]{2,1,0:T(8,128)(2,1)S(1)}, u32[]{:S(2)}) copy-start(bf16[16,40,384]{2,1,0:T(8,128)(2,1)S(1)} %collective-permute-done.4.own2) | copy-start | bytes 1474564
  36.9 4.5 %collective-permute-start.8 = (bf16[16,40,384]{2,1,0:T(8,128)(2,1)S(1)}, bf16[16,40,384]{2,1,0:T(8,128)(2,1)S(1)}, u32[]{:S(2)}, u32[]{:S(2)}) collective-permute-start(bf16[16,40,384]{2,1,0:T(8,128)(2,1)S(1)} %collective-permute-done.4.own2), channel_id=1, source_target_pairs={{0,2},{2,0},{1,3},{3,1},{4,6},{6,4},{5,7},{7,5},{8,10},{10,8},{9,1... | collective-permute-start | bytes 1474568 | tf_op jit(solution)/shard_map/ppermute | solution.py:581
  41.4 2.7 %copy-start.7 = (bf16[16,40,384]{2,1,0:T(8,128)(2,1)}, bf16[16,40,384]{2,1,0:T(8,128)(2,1)S(1)}, u32[]{:S(2)}) copy-start(bf16[16,40,384]{2,1,0:T(8,128)(2,1)S(1)} %collective-permute-done.3.own1) | copy-start | bytes 1474564
  41.4 1.9 %collective-permute-start.7 = (bf16[16,40,384]{2,1,0:T(8,128)(2,1)S(1)}, bf16[16,40,384]{2,1,0:T(8,128)(2,1)S(1)}, u32[]{:S(2)}, u32[]{:S(2)}) collective-permute-start(bf16[16,40,384]{2,1,0:T(8,128)(2,1)S(1)} %collective-permute-done.3.own1), channel_id=1, source_target_pairs={{0,2},{2,0},{1,3},{3,1},{4,6},{6,4},{5,7},{7,5},{8,10},{10,8},{9,1... | collective-permute-start | bytes 1474568 | tf_op jit(solution)/shard_map/ppermute | solution.py:581
  41.4 2.7 %copy-start.8 = (bf16[16,40,384]{2,1,0:T(8,128)(2,1)}, bf16[16,40,384]{2,1,0:T(8,128)(2,1)S(1)}, u32[]{:S(2)}) copy-start(bf16[16,40,384]{2,1,0:T(8,128)(2,1)S(1)} %collective-permute-done.6.oth0) | copy-start | bytes 1474564
  41.4 2.7 %copy-start.9 = (bf16[16,40,384]{2,1,0:T(8,128)(2,1)}, bf16[16,40,384]{2,1,0:T(8,128)(2,1)S(1)}, u32[]{:S(2)}) copy-start(bf16[16,40,384]{2,1,0:T(8,128)(2,1)S(1)} %collective-permute-done.9.oth3) | copy-start | bytes 1474564
  41.5 2.7 %copy-start.10 = (bf16[16,40,384]{2,1,0:T(8,128)(2,1)}, bf16[16,40,384]{2,1,0:T(8,128)(2,1)S(1)}, u32[]{:S(2)}) copy-start(bf16[16,40,384]{2,1,0:T(8,128)(2,1)S(1)} %collective-permute-done.8.oth2) | copy-start | bytes 1474564
  43.3 0.8 copy-start.11
  62.2 35.1 %copy-start.4 = (bf16[16,48,384]{2,1,0:T(8,128)(2,1)}, bf16[16,48,384]{2,1,0:T(8,128)(2,1)S(1)}, u32[]{:S(2)}) copy-start(bf16[16,48,384]{2,1,0:T(8,128)(2,1)S(1)} %all-to-all-done.1.old_own_ref) | copy-start | bytes 1769476
  62.2 3.1 %collective-permute-start.10 = (bf16[32,48,384]{2,1,0:T(8,128)(2,1)}, bf16[32,48,384]{2,1,0:T(8,128)(2,1)S(1)}, u32[]{:S(2)}, u32[]{:S(2)}) collective-permute-start(bf16[32,48,384]{2,1,0:T(8,128)(2,1)} %get-tuple-element.54), channel_id=1, source_target_pairs={{0,2},{2,0},{1,3},{3,1},{4,6},{6,4},{5,7},{7,5},{8,10},{10,8},{9,1... | collective-permute-start | bytes 3538952 | tf_op jit(solution)/shard_map/ppermute | solution.py:581
  92.6 16.4 %copy-start.3 = (f32[48,384]{1,0:T(8,128)}, f32[48,384]{1,0:T(8,128)S(1)}, u32[]{:S(2)}) copy-start(f32[48,384]{1,0:T(8,128)S(1)} %convert_reduce_fusion.piece_ref) | copy-start | bytes 221188
  93.4 15.5 %all-to-all-start.3 = ((bf16[16,48,384]{2,1,0:T(8,128)(2,1)}), bf16[16,48,384]{2,1,0:T(8,128)(2,1)S(1)}, u32[]{:S(2)}, u32[]{:S(2)}) async-start(bf16[16,48,384]{2,1,0:T(8,128)(2,1)} %broadcast_in_dim.5), calls=%async_computation.3 | async-start | bytes 1179648 | tf_op jit(solution)/shard_map/all_to_all | solution.py:585
  97.3 18.4 %collective-permute-start.12 = (bf16[16,48,384]{2,1,0:T(8,128)(2,1)S(1)}, bf16[16,48,384]{2,1,0:T(8,128)(2,1)S(1)}, u32[]{:S(2)}, u32[]{:S(2)}) collective-permute-start(bf16[16,48,384]{2,1,0:T(8,128)(2,1)S(1)} %all-to-all-done.1.old_own_ref), channel_id=1, source_target_pairs={{0,2},{2,0},{1,3},{3,1},{4,6},{6,4},{5,7},{7,5},{8,10},{10,8},{9,1... | collective-permute-start | bytes 1769480 | tf_op jit(solution)/shard_map/ppermute | solution.py:581
  109.0 0.8 copy-start
  109.0 6.7 %collective-permute-start.11 = (bf16[16,48,384]{2,1,0:T(8,128)(2,1)S(1)}, bf16[16,48,384]{2,1,0:T(8,128)(2,1)S(1)}, u32[]{:S(2)}, u32[]{:S(2)}) collective-permute-start(bf16[16,48,384]{2,1,0:T(8,128)(2,1)S(1)} %all-to-all-done.3.own_ref), channel_id=1, source_target_pairs={{0,2},{2,0},{1,3},{3,1},{4,6},{6,4},{5,7},{7,5},{8,10},{10,8},{9,1... | collective-permute-start | bytes 1769480 | tf_op jit(solution)/shard_map/ppermute | solution.py:581
  112.1 13.4 %all-to-all-start.4 = ((bf16[8,80,384]{2,1,0:T(8,128)(2,1)}), bf16[8,80,384]{2,1,0:T(8,128)(2,1)S(1)}, u32[]{:S(2)}, u32[]{:S(2)}) async-start(bf16[8,80,384]{2,1,0:T(8,128)(2,1)} %tell.1), calls=%async_computation.4 | async-start | bytes 983040 | tf_op jit(solution)/shard_map/all_to_all | solution.py:585
  115.6 0.8 copy-start.15
  116.5 0.8 copy-start.16
  125.5 0.8 copy-start.2
  (2 other events, 1.2 us)

commit v3 on v2

--- a/solution.py
+++ b/solution.py
@@ -38,31 +38,38 @@
 BLOCK = 12
 GROUP = 48
 SENT = 40
-VMEM = 60 << 20
+VMEM = 24 << 20
+ALL_VMEM = 60 << 20
 LAYER_VMEM = 60 << 20
 
 
-def unit_places():
-    places = np.zeros((2, 768, 1536), np.float32)
-    for core in range(2):
-        for xy in range(16):
-            for z in range(4):
-                block = (z * 16 + xy) * 2 + core
-                for r in range(BLOCK):
-                    row = xy * GROUP + z * BLOCK + r
-                    if r < 9:
-                        head, rest = divmod(block * 9 + r, 192)
-                        part, e = divmod(rest, 64)
-                        places[core, row, part * 384 + head * 64 + e] = 1
-                    else:
-                        places[core, row, 1152 + block * 3 + r - 9] = 1
-    return places
+def qkv_pieces(block):
+    pieces = []
+    row = block * 9
+    while row < block * 9 + 9:
+        head, rest = divmod(row, 3 * HD)
+        part, e = divmod(rest, HD)
+        count = min(HD - e, block * 9 + 9 - row)
+        pieces.append((row - block * 9, count, part * HEADS * HD + head * HD + e))
+        row += count
+    return pieces
+
+
+def blocks_of_rows():
+    return [
+        (core, xy * GROUP + z * BLOCK, (z * 16 + xy) * 2 + core)
+        for core in range(2)
+        for xy in range(16)
+        for z in range(4)
+    ]
 
 
 def small_places():
-    places = np.zeros((768, 64), np.float32)
+    places = np.zeros((2, 64, 768), np.float32)
     for n in range(64):
-        places[(n // 4) * GROUP + (n % 4) * BLOCK, n] = 1
+        at = (n // 4) * GROUP + (n % 4) * BLOCK
+        places[0, n, at] = 1
+        places[1, n, at + 9] = 1
     return places
 
 
@@ -130,15 +137,33 @@
     ]
 
 
+def embed_kernel(tok_ref, cot_ref, table_ref, pos_ref, stream_ref, cot_out_ref, padded_ref):
+    count = tok_ref.shape[0]
+    padded_ref[...] = jnp.zeros(padded_ref.shape, F32)
+    padded_ref[: table_ref.shape[0]] = table_ref[...]
+    t0, t_rest = halves(padded_ref[...])
+    t1, t2 = halves(padded_ref[...] - t0.astype(F32))
+    hits = hits_of(pos_ref, count)
+    stream_ref[...] = tok_ref[...].astype(F32) + (
+        (dot_tn(hits, t2) + dot_tn(hits, t1)) + dot_tn(hits, t0)
+    )
+    cot_out_ref[...] = cot_ref[...]
+
+
+def hits_of(pos_ref, count):
+    return (
+        lax.broadcasted_iota(jnp.int32, (64, count), 0) == jnp.broadcast_to(pos_ref[...], (64, count))
+    ).astype(BF)
+
+
 def layer_kernel(
     where_ref,
     res_ref,
     off_ref,
-    tok_hbm,
-    cot_hbm,
-    table_hbm,
     norms_ref,
     pos_ref,
+    stream_hbm,
+    cot_hbm,
     own0,
     own1,
     own2,
@@ -147,75 +172,81 @@
     oth1,
     oth2,
     oth3,
-    places_hbm,
-    small_ref,
-    result_ref,
-    in_grad_ref,
-    keep_ref,
-    send_ref,
+    result_hbm,
+    in_grad_hbm,
+    keep_hbm,
+    send_hbm,
     wup,
     wdn,
-    wat,
+    wqkv,
+    wout,
+    mixed,
+    sorted_qkv,
+    sorted_out,
+    message,
     probs_ref,
     qkv_ref,
     ctx_ref,
     dqkv_ref,
-    places_ref,
-    tok_ref,
+    small_ref,
+    weights_ref,
+    stream_ref,
     cot_ref,
-    table_ref,
-    sems,
+    result_ref,
+    in_grad_ref,
+    kept,
+    sent,
+    in_sems,
+    out_sems,
 ):
     core = where_ref[0]
     half = where_ref[1]
     colour = where_ref[4]
-    count = tok_ref.shape[0]
+    count = cot_ref.shape[0]
     loads = [
-        pltpu.make_async_copy(src, dst, sems.at[k])
-        for k, (src, dst) in enumerate(
-            ((tok_hbm, tok_ref), (places_hbm, places_ref), (cot_hbm, cot_ref))
-        )
+        pltpu.make_async_copy(source, weights_ref.at[k], in_sems.at[k])
+        for k, source in enumerate((own0, own1, own2, own3, oth0, oth1, oth2, oth3))
     ]
+    loads.append(pltpu.make_async_copy(stream_hbm, stream_ref, in_sems.at[8]))
+    loads.append(pltpu.make_async_copy(cot_hbm, cot_ref, in_sems.at[9]))
     for load in loads:
         load.start()
-    table_ref[...] = jnp.zeros(table_ref.shape, F32)
-    table_ref[: table_hbm.shape[0]] = table_hbm[...]
-
-    for here in range(4):
-
-        @pl.when(colour == here)
-        def _(here=here):
-            for s, refs in enumerate(((own0, own1, own2, own3), (oth0, oth1, oth2, oth3))):
+
+    for s in range(2):
+        for load in loads[4 * s : 4 * s + 4]:
+            load.wait()
+        for here in range(4):
+
+            @pl.when(colour == here)
+            def _(s=s, here=here):
                 for xy in range(16):
                     ahead = xy // 4 + 2 * (xy % 4) - here
-                    blocks = [refs[(ahead - z) % 4][xy].astype(F32) for z in range(4)]
+                    blocks = [weights_ref[4 * s + (ahead - z) % 4, xy].astype(F32) for z in range(4)]
                     at = s * 768 + xy * GROUP
-                    for first, dst in ((0, wup), (12, wdn), (24, wat)):
-                        dst[at : at + GROUP] = jnp.concatenate(
-                            [block[first : first + BLOCK] for block in blocks], axis=0
-                        ).astype(BF)
-
-    for load in loads:
+                    groups = [
+                        jnp.concatenate([block[k : k + BLOCK] for block in blocks], axis=0)
+                        for k in (0, 12, 24)
+                    ]
+                    wup[at : at + GROUP] = groups[0].astype(BF)
+                    wdn[at : at + GROUP] = groups[1].astype(BF)
+                    mixed[core if s == 0 else 1 - core, xy * GROUP : (xy + 1) * GROUP] = groups[2]
+
+    for load in loads[8:]:
         load.wait()
 
-    def place(s):
-        return core if s == 0 else 1 - core
-
-    hits = (
-        lax.broadcasted_iota(jnp.int32, (64, count), 0) == jnp.broadcast_to(pos_ref[...], (64, count))
-    ).astype(BF)
-    table = table_ref[...]
-    t0, t_rest = halves(table)
-    t1, t2 = halves(table - t0.astype(F32))
-    stream_in = tok_ref[...].astype(F32) + ((dot_tn(hits, t2) + dot_tn(hits, t1)) + dot_tn(hits, t0))
+    for at_core, at, block in blocks_of_rows():
+        for first, length, to in qkv_pieces(block):
+            sorted_qkv[to : to + length] = mixed[at_core, at + first : at + first + length]
+        sorted_out[block * 3 : block * 3 + 3] = mixed[at_core, at + 9 : at + 12]
+    wqkv[...] = sorted_qkv[...].astype(BF)
+    wout[...] = sorted_out[...].astype(BF)
+
+
+    stream_in = stream_ref[...]
     g1, s1, g2, s2 = (norms_ref[k : k + 1, :] for k in range(4))
     n1, r1 = norm_parts(stream_in)
     y1 = (n1 * g1 + s1).astype(BF)
-    qkv = 0.0
-    for s in range(2):
-        pad = dot_nt(y1, wat[s * 768 : (s + 1) * 768, :]).astype(BF)
-        qkv = qkv + dot(pad, places_ref[place(s), :, :1152])
-    qkv_ref[...] = qkv.astype(BF)
+    qkv_ref[...] = dot_nt(y1, wqkv[...]).astype(BF)
 
     def segments(shape, dim):
         at = lax.broadcasted_iota(jnp.int32, shape, dim)
@@ -245,10 +276,7 @@
             probs_ref[2 * p + hh] = probs
             ctx = ctx + dot(probs.astype(BF), v * masks[hh])
         ctx_ref[:, lo : lo + 128] = ctx.astype(BF)
-    ctx_pads = [
-        dot_nt(ctx_ref[...], places_ref[place(s), :, 1152:]).astype(BF) for s in range(2)
-    ]
-    stream_mid = stream_in + (dot(ctx_pads[0], wat[:768, :]) + dot(ctx_pads[1], wat[768:, :]))
+    stream_mid = stream_in + dot(ctx_ref[...], wout[...])
     n2, r2 = norm_parts(stream_mid)
     y2 = (n2 * g2 + s2).astype(BF)
 
@@ -269,20 +297,27 @@
         grad = dot_tn(jnp.where(half == 0, d_pre, hidden), right).reshape(8, GROUP, 384)
         at = (k % 2) * 8
         if k < 2:
-            keep_ref[at : at + 8] = grad.astype(BF)
+            kept[at : at + 8] = grad.astype(BF)
         else:
-            send_ref[at : at + 8] = grad.astype(BF)
+            sent[at : at + 8] = grad.astype(BF)
     result_ref[...] = out.astype(BF)
+    stores = [
+        pltpu.make_async_copy(
+            source.at[pl.ds(16 * k, 16)], target.at[pl.ds(16 * k, 16)], out_sems.at[2 * k + j]
+        )
+        for k in range(2)
+        for j, (source, target) in enumerate(((sent, send_hbm), (kept, keep_hbm)))
+    ]
+    stores.append(pltpu.make_async_copy(result_ref, result_hbm, out_sems.at[4]))
+    stores.append(pltpu.make_async_copy(in_grad_ref, in_grad_hbm, out_sems.at[5]))
+    for k in (0, 1, 4):
+        stores[k].start()
     gain2 = jnp.sum(d_y2 * n2, axis=0, keepdims=True)
     shift2 = jnp.sum(d_y2, axis=0, keepdims=True)
     d_mid = cot.astype(F32) + norm_back(d_y2, n2, r2, g2)
 
     d_attn = d_mid.astype(BF)
-    d_ctx = 0.0
-    for s in range(2):
-        pad = dot_nt(d_attn, wat[s * 768 : (s + 1) * 768, :]).astype(BF)
-        d_ctx = d_ctx + dot(pad, places_ref[place(s), :, 1152:])
-    d_ctx = d_ctx.astype(BF)
+    d_ctx = dot_nt(d_attn, wout[...]).astype(BF)
     for p in range(HEADS // 2):
         lo = p * 128
         q = qkv_ref[:, lo : lo + 128]
@@ -302,13 +337,12 @@
         dqkv_ref[:, lo : lo + 128] = (dq * scale).astype(BF)
         dqkv_ref[:, 384 + lo : 512 + lo] = (dk * scale).astype(BF)
         dqkv_ref[:, 768 + lo : 896 + lo] = dv.astype(BF)
-    d_pads = [
-        dot_nt(dqkv_ref[...], places_ref[place(s), :, :1152]).astype(BF) for s in range(2)
-    ]
-    d_y1 = dot(d_pads[0], wat[:768, :]) + dot(d_pads[1], wat[768:, :])
+    d_y1 = dot(dqkv_ref[...], wqkv[...])
     in_grad = d_mid + norm_back(d_y1, n1, r1, g1)
     in_grad_ref[...] = in_grad
-
+    stores[5].start()
+
+    hits = hits_of(pos_ref, count)
     i0, i1 = halves(in_grad)
     pos_grad = dot(hits, i0) + dot(hits, i1)
     gain1 = jnp.sum(d_y1 * n1, axis=0, keepdims=True)
@@ -316,21 +350,49 @@
     row = lax.broadcasted_iota(jnp.int32, (64, 384), 0)
     for at, value in ((50, gain1), (51, shift1), (52, gain2), (53, shift2)):
         pos_grad = jnp.where(row == at, jnp.broadcast_to(value, (64, 384)), pos_grad)
-    small = dot(small_ref[...], jnp.where(half == 0, pos_grad, 0.0).astype(BF))
-    right = jnp.where(half == 0, d_attn, y1)
-    for s in range(2):
-        left = jnp.where(half == 0, ctx_pads[s], d_pads[s])
-        grad = (dot_tn(left, right) + small).reshape(16, GROUP, 384)
-        if s == 0:
-            keep_ref[16:] = grad.astype(BF)
-        else:
-            send_ref[16:] = grad.astype(BF)
-
-
-def run_layer(where, res_ids, offsets, tokens, cotangent, table, norms, pos, weights):
-    count = tokens.shape[0]
-    places = jnp.asarray(unit_places(), BF)
-    small = jnp.asarray(small_places(), BF)
+    sorted_out[...] = dot_tn(ctx_ref[...], d_attn)
+    sorted_qkv[...] = dot_tn(dqkv_ref[...], y1)
+    small_ref[...] = pos_grad
+
+    @pl.when(half == 0)
+    def _():
+        zeros = jnp.zeros((8, D), F32)
+        for at_core in range(2):
+            for xy in range(16):
+                rows = []
+                for z in range(4):
+                    block = (z * 16 + xy) * 2 + at_core
+                    rows += [
+                        small_ref[xy * 4 + z : xy * 4 + z + 1],
+                        zeros,
+                        sorted_out[block * 3 : block * 3 + 3],
+                    ]
+                message[at_core, xy] = jnp.concatenate(rows, axis=0).astype(BF)
+
+    @pl.when(half == 1)
+    def _():
+        zeros = jnp.zeros((2, D), F32)
+        for at_core in range(2):
+            for xy in range(16):
+                rows = []
+                for z in range(4):
+                    rows += [
+                        sorted_qkv[to : to + length]
+                        for _, length, to in qkv_pieces((z * 16 + xy) * 2 + at_core)
+                    ]
+                    rows += [small_ref[xy * 4 + z : xy * 4 + z + 1], zeros]
+                message[at_core, xy] = jnp.concatenate(rows, axis=0).astype(BF)
+
+    sent[16:] = message[1 - core]
+    stores[2].start()
+    kept[16:] = message[core]
+    stores[3].start()
+    for store in stores:
+        store.wait()
+
+
+def run_layer(where, res_ids, offsets, stream, cotangent, norms, pos, weights):
+    count = stream.shape[0]
     smem = pl.BlockSpec(memory_space=pltpu.SMEM)
     vmem = pl.BlockSpec(memory_space=pltpu.VMEM)
     hbm = pl.BlockSpec(memory_space=pl.ANY)
@@ -342,21 +404,31 @@
             jax.ShapeDtypeStruct((32, GROUP, D), BF),
             jax.ShapeDtypeStruct((32, GROUP, D), BF),
         ),
-        in_specs=[smem] * 3 + [hbm] * 2 + [vmem] * 11 + [hbm, vmem],
-        out_specs=(vmem,) * 4,
+        in_specs=[smem] * 3 + [vmem] * 2 + [hbm] * 10,
+        out_specs=(hbm,) * 4,
         scratch_shapes=[
             pltpu.VMEM((1536, D), BF),
             pltpu.VMEM((1536, D), BF),
-            pltpu.VMEM((1536, D), BF),
+            pltpu.VMEM((1152, D), BF),
+            pltpu.VMEM((D, D), BF),
+            pltpu.VMEM((2, 768, D), F32),
+            pltpu.VMEM((1152, D), F32),
+            pltpu.VMEM((D, D), F32),
+            pltpu.VMEM((2, 16, GROUP, D), BF),
             pltpu.VMEM((HEADS, count, count), F32),
             pltpu.VMEM((count, 1152), BF),
             pltpu.VMEM((count, D), BF),
             pltpu.VMEM((count, 1152), BF),
-            pltpu.VMEM((2, 768, 1536), BF),
+            pltpu.VMEM((64, D), F32),
+            pltpu.VMEM((8, 16, SENT, D), BF),
+            pltpu.VMEM((count, D), F32),
             pltpu.VMEM((count, D), BF),
             pltpu.VMEM((count, D), BF),
-            pltpu.VMEM((64, D), F32),
-            pltpu.SemaphoreType.DMA((3,)),
+            pltpu.VMEM((count, D), F32),
+            pltpu.VMEM((32, GROUP, D), BF),
+            pltpu.VMEM((32, GROUP, D), BF),
+            pltpu.SemaphoreType.DMA((10,)),
+            pltpu.SemaphoreType.DMA((6,)),
         ],
         compiler_params=pltpu.CompilerParams(vmem_limit_bytes=LAYER_VMEM),
         cost_estimate=pl.CostEstimate(
@@ -364,16 +436,17 @@
         ),
         name="layer",
     )(
-        where, res_ids, offsets, tokens, cotangent, table, norms, pos, *weights, places, small
+        where, res_ids, offsets, norms, pos, stream, cotangent, *weights
     )
 
 
 def product(a, b):
     (ah, al), (bh, bl) = a, b
-    return dot(ah, bh) + (dot(ah, bl) + dot(al, bh))
-
-
-def call(kernel, name, outs, args, scalars=0, scratch=(), flops=0, moved=0):
+    first = jnp.concatenate([ah, al], axis=1)
+    return dot(first, jnp.concatenate([bh, bh], axis=0)) + dot(ah, bl)
+
+
+def call(kernel, name, outs, args, scalars=0, scratch=(), flops=0, moved=0, vmem_bytes=VMEM):
     smem = pl.BlockSpec(memory_space=pltpu.SMEM)
     vmem = pl.BlockSpec(memory_space=pltpu.VMEM)
     return pl.pallas_call(
@@ -382,7 +455,7 @@
         in_specs=[smem] * scalars + [vmem] * (len(args) - scalars),
         out_specs=(vmem,) * len(outs),
         scratch_shapes=scratch,
-        compiler_params=pltpu.CompilerParams(vmem_limit_bytes=VMEM),
+        compiler_params=pltpu.CompilerParams(vmem_limit_bytes=vmem_bytes),
         cost_estimate=pl.CostEstimate(flops=flops, bytes_accessed=moved, transcendentals=0),
         name=name,
     )(*args)
@@ -421,101 +494,106 @@
 
 
 def join_kernel(where_ref, *refs):
-    *sources, joined_ref = refs
+    *sources, joined_ref, sent_ref = refs
     for z in range(4):
 
         @pl.when(where_ref[3] == z)
         def _(z=z):
-            joined_ref[...] = jnp.concatenate(
+            joined = jnp.concatenate(
                 [sources[(at - z) % 4][...].astype(F32) for at in range(4)], axis=0
             ).astype(BF)
-
-
-def valid_rows(is_out):
+            joined_ref[...] = joined
+            sent_ref[...] = jnp.broadcast_to(joined[None], sent_ref.shape)
+
+
+def sum_kernel(parts_ref, piece_ref, sent_ref):
+    total = parts_ref[0].astype(F32)
+    for k in range(1, parts_ref.shape[0]):
+        total = total + parts_ref[k].astype(F32)
+    piece_ref[...] = total
+    sent_ref[...] = jnp.broadcast_to(total.astype(BF)[None], sent_ref.shape)
+
+
+def valid_rows(z):
     row = lax.broadcasted_iota(jnp.int32, (GROUP, D), 0) % BLOCK
-    return (jnp.logical_not(is_out) | (row >= 9)).astype(F32)
-
-
-def tell_kernel(where_ref, own_ref, piece_ref, small_ref, told_ref):
-    is_out = where_ref[3] == 1
-    valid = valid_rows(is_out)
+    return jnp.where(z == 1, (row >= 9).astype(F32), jnp.where(z == 3, (row < 9).astype(F32), 1.0))
+
+
+def tell_kernel(where_ref, own_ref, piece_ref, places_ref, told_ref, small_ref):
+    z = where_ref[3]
+    valid = valid_rows(z)
     total = jnp.zeros((GROUP, D), F32)
     for xy in range(16):
         g = own_ref[xy].astype(F32) * valid
         total = total + g * g
-    small = dot(small_ref[...], own_ref[...].reshape(768, D))
-    counted = jnp.where(is_out & (where_ref[0] == 0), 1.0, 0.0)
+    small = dot(places_ref[where_ref[1]], own_ref[...].reshape(768, D))
+    small_ref[...] = small.astype(BF)
+    counted = jnp.where((z == 1) & (where_ref[0] == 0), 1.0, 0.0)
     squares = jnp.sum(total) + counted * jnp.sum(small * small)
     squares = jnp.full((1, D), squares, F32)
     high = squares.astype(BF).astype(F32)
     mid = (squares - high).astype(BF).astype(F32)
     low = squares - high - mid
-    for z in range(4):
+    for to in range(4):
         rows = jnp.concatenate(
-            [small, piece_ref[z * BLOCK : (z + 1) * BLOCK, :], high, mid, low, jnp.zeros((1, D), F32)],
+            [piece_ref[to * BLOCK : (to + 1) * BLOCK, :], high, mid, low, jnp.zeros((1, D), F32)],
             axis=0,
         ).astype(BF)
-        told_ref[2 * z] = rows
-        told_ref[2 * z + 1] = rows
+        told_ref[2 * to] = rows
+        told_ref[2 * to + 1] = rows
 
 
 def clip(told_ref):
     total = jnp.zeros((1, 1), F32)
     for k in range(8):
-        last = told_ref[k, 64:, :].astype(F32)
+        last = told_ref[k].astype(F32)
         total = total + (last[12:13, :1] + last[13:14, :1] + last[14:15, :1])
     grad_norm = jnp.sqrt(total)
     return grad_norm, jnp.minimum(1.0, CLIP_LIMIT / (grad_norm + 1e-06))
 
 
-def gram_kernel(where_ref, own_ref, oth_ref, old_own_ref, old_oth_ref, gram_ref, grad_ref, old_ref):
-    valid = valid_rows(where_ref[3] == 1)
-    for s, (g_ref, o_ref) in enumerate(((own_ref, old_own_ref), (oth_ref, old_oth_ref))):
+def orth_kernel(
+    where_ref,
+    told_ref,
+    own_ref,
+    oth_ref,
+    old_own_ref,
+    old_oth_ref,
+    old_ref,
+    piece_ref,
+    out_ref,
+    whole_ref,
+):
+    valid = valid_rows(where_ref[3])
+    factor = clip(told_ref)[1]
+    scaled = factor * valid
+    for s, (grad_ref, before_ref) in enumerate(((own_ref, old_own_ref), (oth_ref, old_oth_ref))):
         for xy in range(16):
             at = s * 768 + xy * GROUP
-            grad_ref[at : at + GROUP] = (g_ref[xy].astype(F32) * valid).astype(BF)
-        old_ref[s * 768 : (s + 1) * 768] = o_ref[...].reshape(768, D)
-    grad = grad_ref[...]
-    old = old_ref[...]
-    cross = dot_tn(grad, old)
-    gram_ref[0] = dot_tn(old, old)
-    gram_ref[1] = cross + cross.T
-    gram_ref[2] = dot_tn(grad, grad)
-
-
-def left_parts(parts):
-    return jnp.concatenate([parts[0], parts[0], parts[1]], axis=1)
-
-
-def right_parts(parts):
-    return jnp.concatenate([parts[0], parts[1], parts[0]], axis=0)
-
-
-def orth_kernel(where_ref, told_ref, gram_ref, old_ref, piece_ref, out_ref):
-    valid = valid_rows(where_ref[3] == 1)
-    factor = clip(told_ref)[1]
-    gram = (
-        (MOMENTUM * MOMENTUM) * gram_ref[0]
-        + (MOMENTUM * factor) * gram_ref[1]
-        + (factor * factor) * gram_ref[2]
-    )
+            whole_ref[at : at + GROUP] = (
+                MOMENTUM * before_ref[xy].astype(F32) + scaled * grad_ref[xy].astype(F32)
+            ).astype(BF)
+    whole = whole_ref[...]
+    gram = dot_tn(whole, whole)
     eye = (
         lax.broadcasted_iota(jnp.int32, (D, D), 0) == lax.broadcasted_iota(jnp.int32, (D, D), 1)
     ).astype(F32)
     inv = 1.0 / (jnp.sqrt(jnp.sum(gram * eye)) + 1e-07)
     gram = gram * (inv * inv)
-    mine = (MOMENTUM * old_ref[...].astype(F32) + factor * (piece_ref[...] * valid)) * inv
+    mine = (MOMENTUM * old_ref[...].astype(F32) + scaled * piece_ref[...]) * inv
     for step in range(NS_STEPS):
         parts = halves(gram)
-        right = right_parts(parts)
-        poly = halves(COEF_A * eye + COEF_B * gram + COEF_C * dot(left_parts(parts), right))
-        if step < NS_STEPS - 1:
-            turned = halves(dot(left_parts(poly), right))
-            left = jnp.concatenate([left_parts(turned), left_parts(halves(mine))], axis=0)
-            both = dot(left, right_parts(poly))
-            gram, mine = both[:D], both[D:]
+        if step in (0, 1, NS_STEPS - 1):
+            square = dot(parts[0], parts[0])
         else:
-            mine = dot(left_parts(halves(mine)), right_parts(poly))
+            square = product(parts, parts)
+        poly = COEF_A * eye + COEF_B * gram + COEF_C * square
+        if step == NS_STEPS - 1:
+            mine = dot(mine.astype(BF), poly.astype(BF))
+        else:
+            poly = halves(poly)
+            gram = product(halves(product(poly, parts)), poly)
+            mine = product(halves(mine), poly)
     for z in range(4):
         out_ref[z] = jnp.concatenate(
             [mine[z * BLOCK : (z + 1) * BLOCK], jnp.zeros((4, D), F32)], axis=0
@@ -529,6 +607,8 @@
 def update_kernel(
     where_ref,
     told_ref,
+    small_own_ref,
+    small_near_ref,
     back_ref,
     qkv_ref,
     out_ref,
@@ -564,11 +644,12 @@
         (0, 0, 12, step_rate(D, FF), up_ref, up_m_ref, up_next, up_m_next),
         (2, 0, 12, step_rate(FF, D), down_ref, down_m_ref, down_next, down_m_next),
     ):
-        grad = told_ref[2 * z + where_ref[0], 64:, :].astype(F32)[first:last]
+        grad = told_ref[2 * z + where_ref[0]].astype(F32)[first:last]
         orth = back_ref[z].astype(F32)[first:last]
         m_next[...] = MOMENTUM * m_ref[...] + factor * grad
         w_next[...] = w_ref[...] - rate * orth
-    small = told_ref[2, :64, :].astype(F32)
+    near = (where_ref[3] % 2 == 0).astype(F32)
+    small = near * small_near_ref[...].astype(F32) + (1.0 - near) * small_own_ref[...].astype(F32)
     norm_fresh = MOMENTUM * norm_m_ref[...] + factor * small[50:54]
     norm_m_next[...] = norm_fresh
     norms_next[...] = norms_ref[...] - NORM_RATE * norm_fresh
@@ -624,59 +705,70 @@
         (where, *weights, *moments),
         scalars=1,
         moved=4_000_000,
+        vmem_bytes=ALL_VMEM,
     )
     old = [old[0]] + [lax.ppermute(old[k], AXES, column_step(k)) for k in (1, 2, 3)]
-    (old,) = call(join_kernel, "join", (((GROUP, D), BF),), (where, *old), scalars=1)
+    pos = pos_index.reshape(1, -1)
+    stream, cotangent = call(
+        embed_kernel,
+        "embed",
+        ((tokens.shape, F32), (tokens.shape, BF)),
+        (tokens, cotangent, pos_table, pos),
+        scratch=[pltpu.VMEM((64, D), F32)],
+        vmem_bytes=ALL_VMEM,
+    )
 
     own = [lax.all_to_all(rows, AXES, 0, 0, axis_index_groups=colour_groups(), tiled=True)]
-    own[0], old = lax.optimization_barrier((own[0], old))
+    own[0], stream, cotangent, *old = lax.optimization_barrier(
+        (own[0], stream, cotangent, *old)
+    )
+    old, old_sent = call(
+        join_kernel,
+        "join",
+        (((GROUP, D), BF), ((16, GROUP, D), BF)),
+        (where, *old),
+        scalars=1,
+    )
     own += [lax.ppermute(own[0], AXES, colour_step(step)) for step in (1, 2, 3)]
     other = [swapped(value) for value in own]
-    old_own = everywhere(old, PLANE)
+    old_own = exchanged(old_sent, PLANE)
 
     result, in_grad, keep, send = run_layer(
         where,
         res_ids,
         offsets,
-        tokens,
+        stream,
         cotangent,
-        pos_table,
         norm_params,
-        pos_index.reshape(1, -1),
+        pos,
         (*own, *other),
     )
     keep, send, old_own = lax.optimization_barrier((keep, send, old_own))
     old_other = swapped(old_own)
     pair = (keep.astype(F32) + swapped(send).astype(F32)).astype(BF)
-    piece = jnp.sum(exchanged(pair, HALF).astype(F32), axis=0)
-    grads = everywhere(piece.astype(BF), PLANE)
+    piece, sent = call(
+        sum_kernel, "sum", (((GROUP, D), F32), ((16, GROUP, D), BF)), (exchanged(pair, HALF),)
+    )
+    grads = exchanged(sent, PLANE)
     grads_other = swapped(grads)
 
-    (told,) = call(
+    told, small = call(
         tell_kernel,
         "tell",
-        (((8, 80, D), BF),),
-        (where, grads, piece, jnp.asarray(small_places().T, BF)),
+        (((8, 16, D), BF), ((64, D), BF)),
+        (where, grads, piece, jnp.asarray(small_places(), BF)),
         scalars=1,
         moved=2_000_000,
     )
     told = exchanged(told, COLUMN_CORES)
-    (gram,) = call(
-        gram_kernel,
-        "gram",
-        (((3, D, D), F32),),
-        (where, grads, grads_other, old_own, old_other),
-        scalars=1,
-        scratch=[pltpu.VMEM((1536, D), BF), pltpu.VMEM((1536, D), BF)],
-        flops=3_000_000_000,
-        moved=5_000_000,
-    )
+    small_near = lax.ppermute(small, "zl", [(1, 0)])
     (orth,) = call(
         orth_kernel,
         "orth",
         (((4, 16, D), BF),),
-        (where, told, gram, old, piece),
+        (where, told, grads, grads_other, old_own, old_other, old, piece),
         scalars=1,
+        scratch=[pltpu.VMEM((1536, D), BF)],
         flops=8_000_000_000,
         moved=4_000_000,
     )
@@ -693,7 +785,7 @@
             like(pos_moment),
             like(pos_table),
         ),
-        (where, told, back, *weights, *moments, norm_params, norm_moment, pos_table, pos_moment),
+        (where, told, small, small_near, back, *weights, *moments, norm_params, norm_moment, pos_table, pos_moment),
         scalars=1,
         moved=2_000_000,
     )

time: 150 us -> 134 us (0.89)
  Pallas kernels: 41.4 us -> 32 us
  blocking collectives: 34.9 us -> 26.7 us
  local copies, waits for them, and re-layouts: 7.83 us -> 1.54 us
  waiting for transfers between devices: 31.5 us -> 37.2 us
  starting transfers between devices: 30.4 us -> 33.4 us
    all_to_all x2 -> x1, blocking collectives: 34.9 us -> 26.7 us  [exchanged(): return lax.all_to_all(value, axes, 0, 0, tiled=True)]
    all_to_all x3 -> x4, waiting for transfers between devices: 15 us -> 21.4 us  [exchanged(): return lax.all_to_all(value, axes, 0, 0, tiled=True)]
    pallas_call x1, Pallas kernels: 18 us -> 13.3 us  [run_layer(): pl.pallas_call(layer_kernel, out_shape=(jax.ShapeDtypeStruct((count, D),...]
    pallas_call x6 -> x7, Pallas kernels: 23.3 us -> 18.7 us  [call(): pl.pallas_call(kernel, out_shape=tuple((jax.ShapeDtypeStruct(shape, dtype...]
    unnamed x34 -> x46, local copies, waits for them, and re-layouts: 4.66 us -> 0.94 us
    all_to_all x3 -> x4, starting transfers between devices: 10.9 us -> 14.2 us  [exchanged(): return lax.all_to_all(value, axes, 0, 0, tiled=True)]
    broadcast_in_dim x2 -> x0, local copies, waits for them, and re-layouts: 2.49 us -> none  [everywhere(): return exchanged(jnp.broadcast_to(value[None], (peers, *value.shape)), axes)]
    ppermute x3, waiting for transfers between devices: 5.58 us -> 3.38 us  [shards(): lax.ppermute(old[k], AXES, column_step(k))]
  transfers between devices with their start and end apart: 17 -> 19, of which waited for: 9 -> 10; matrix products, arithmetic and copies ran while one was open for 1% -> 0% of each run, Pallas kernels for 18% -> 21%
where the time goes in v3:
time: 134 us
  waiting for transfers between devices  37.2 us (28%)
  starting transfers between devices  33.4 us (25%)
  Pallas kernels  32 us (24%)
  blocking collectives  26.7 us (20%)
  other arithmetic  1.6 us (1%)
  local copies, waits for them, and re-layouts  1.54 us (1%)
    all_to_all x1, blocking collectives, exchanged(): return lax.all_to_all(value, axes, 0, 0, tiled=True)  26.7 us
    all_to_all x4, waiting for transfers between devices, exchanged(): return lax.all_to_all(value, axes, 0, 0, tiled=True)  21.4 us
    pallas_call x7, Pallas kernels, call(): pl.pallas_call(kernel, out_shape=tuple((jax.ShapeDtypeStruct(shape, dtype...  18.7 us
    all_to_all x4, starting transfers between devices, exchanged(): return lax.all_to_all(value, axes, 0, 0, tiled=True)  14.2 us
    pallas_call x1, Pallas kernels, run_layer(): pl.pallas_call(layer_kernel, out_shape=(jax.ShapeDtypeStruct((count, D),...  13.3 us
    all_to_all x1, starting transfers between devices, shards(): lax.all_to_all(rows, AXES, 0, 0, axis_index_groups=colour_groups(), tiled...  10.4 us
    ppermute x3, waiting for transfers between devices, shards(): own += [lax.ppermute(own[0], AXES, colour_step(step)) for step in (1, 2, 3)]  4.57 us
    ppermute x7, waiting for transfers between devices, swapped(): return lax.ppermute(value, 'c', [(0, 1), (1, 0)])  4.05 us
  transfers between devices with their start and end apart: 19, of which 10 were waited for; matrix products, arithmetic and copies ran while one was open for 0% of the time, Pallas kernels for 21%

profile of v3, /device:TPU:0, one launch (start us, length us, event | category | flops | bytes accessed | tf_op | source)
XLA Modules:
  0.0 133.6 jit_solution(8656420956123794208)
XLA Ops:
  0.7 0.6 stack.23.where_ref
  1.3 1.7 %prepare.1 = (bf16[16,40,384]{2,1,0:T(8,128)(2,1)}, bf16[12,384]{1,0:T(8,128)(2,1)}, bf16[12,384]{1,0:T(8,128)(2,1)}, bf16[12,384]{1,0:T(8,128)(2,1)}, bf16[12,384]{1,0:T(8,128)(2,1)}) custom-call(s32[5]{0:T(128)} %stack.23.where_ref, f32[9,384]{1,0:T(8,128)} %bitcast.15, f32[3,384]{1,0:T(4,128)} %out_ref.3, f32[12,384]{1,0:T(8,128)} %bitcast.17, ...), custom_call_target="tpu_custom_call" | custom-call | bytes 4000000 | tf_op jit(solution)/shard_map/prepare/pallas_call | solution.py:452
  3.0 10.4 %all-to-all-start = ((bf16[16,40,384]{2,1,0:T(8,128)(2,1)}), bf16[16,40,384]{2,1,0:T(8,128)(2,1)S(1)}, u32[]{:S(2)}, u32[]{:S(2)}) async-start(bf16[16,40,384]{2,1,0:T(8,128)(2,1)} %get-tuple-element.55), calls=%async_computation | async-start | bytes 983040 | tf_op jit(solution)/shard_map/all_to_all | solution.py:721
  13.5 0.8 collective-permute-start
  14.3 2.4 %collective-permute-start.1 = (bf16[12,384]{1,0:T(8,128)(2,1)}, bf16[12,384]{1,0:T(8,128)(2,1)S(1)}, u32[]{:S(2)}, u32[]{:S(2)}) collective-permute-start(bf16[12,384]{1,0:T(8,128)(2,1)} %get-tuple-element.60), channel_id=1, source_target_pairs={{1,0},{3,2},{65,64},{67,66},{0,1},{2,3},{64,65},{66,67},{5,4},{7,6... | collective-permute-start | bytes 27656 | tf_op jit(solution)/shard_map/ppermute | solution.py:710
  16.6 2.2 %embed.1 = (f32[256,384]{1,0:T(8,128)}, bf16[256,384]{1,0:T(8,128)(2,1)}) custom-call(bf16[256,384]{1,0:T(8,128)(2,1)} %tok_ref.1, bf16[256,384]{1,0:T(8,128)(2,1)} %cot_ref.1, f32[50,384]{1,0:T(8,128)} %table_ref.3, s32[1,256]{1,0:T(1,128)} %bitcast.23), custom_call_target="tpu_custom_call" | custom-call | tf_op jit(solution)/shard_map/embed/pallas_call | solution.py:452
  18.8 3.2 %collective-permute-done.1.refs_2_ = bf16[12,384]{1,0:T(8,128)(2,1)S(1)} collective-permute-done((bf16[12,384]{1,0:T(8,128)(2,1)}, bf16[12,384]{1,0:T(8,128)(2,1)S(1)}, u32[]{:S(2)}, u32[]{:S(2)}) %collective-permute-start.1) | collective-permute-done | bytes 9248 | tf_op jit(solution)/shard_map/ppermute | solution.py:710
  22.2 3.8 %all-to-all-done.own0 = bf16[16,40,384]{2,1,0:T(8,128)(2,1)S(1)} async-done(((bf16[16,40,384]{2,1,0:T(8,128)(2,1)}), bf16[16,40,384]{2,1,0:T(8,128)(2,1)S(1)}, u32[]{:S(2)}, u32[]{:S(2)}) %all-to-all-start) | async-done | bytes 491552 | tf_op jit(solution)/shard_map/all_to_all | solution.py:721
  26.1 2.0 %collective-permute-start.4 = (bf16[16,40,384]{2,1,0:T(8,128)(2,1)S(1)}, bf16[16,40,384]{2,1,0:T(8,128)(2,1)S(1)}, u32[]{:S(2)}, u32[]{:S(2)}) collective-permute-start(bf16[16,40,384]{2,1,0:T(8,128)(2,1)S(1)} %all-to-all-done.own0), channel_id=1, source_target_pairs={{4,0},{14,2},{68,64},{78,66},{5,1},{15,3},{69,65},{79,67},{8,4},{2... | collective-permute-start | bytes 1474568 | tf_op jit(solution)/shard_map/ppermute | solution.py:732
  28.0 1.3 collective-permute-start.3
  29.3 1.4 %join.1 = (bf16[48,384]{1,0:T(8,128)(2,1)S(1)}, bf16[16,48,384]{2,1,0:T(8,128)(2,1)}) custom-call(s32[5]{0:T(128)S(1)} %copy-done.12, bf16[12,384]{1,0:T(8,128)(2,1)S(1)} %copy-done.14, bf16[12,384]{1,0:T(8,128)(2,1)S(1)} %collective-permute-done.refs_1_, bf16[12,384]{1,0:T(8,128)(2,1)S(1)} %collective-permute-done.1.refs_2_, ...), custom_call_target="tpu_custom_call" | custom-call | tf_op jit(solution)/shard_map/join/pallas_call | solution.py:452
  30.8 3.7 %all-to-all-start.1 = ((bf16[16,48,384]{2,1,0:T(8,128)(2,1)}), bf16[16,48,384]{2,1,0:T(8,128)(2,1)S(1)}, u32[]{:S(2)}, u32[]{:S(2)}) async-start(bf16[16,48,384]{2,1,0:T(8,128)(2,1)} %get-tuple-element.73), calls=%async_computation.1 | async-start | bytes 1179648 | tf_op jit(solution)/shard_map/all_to_all | solution.py:666
  34.5 1.6 %collective-permute-done.5.own3 = bf16[16,40,384]{2,1,0:T(8,128)(2,1)S(1)} collective-permute-done((bf16[16,40,384]{2,1,0:T(8,128)(2,1)S(1)}, bf16[16,40,384]{2,1,0:T(8,128)(2,1)S(1)}, u32[]{:S(2)}, u32[]{:S(2)}) %collective-permute-start.5) | collective-permute-done | bytes 491552 | tf_op jit(solution)/shard_map/ppermute | solution.py:732
  36.1 0.5 collective-permute-start.8
  36.6 3.0 %collective-permute-done.3.own1 = bf16[16,40,384]{2,1,0:T(8,128)(2,1)S(1)} collective-permute-done((bf16[16,40,384]{2,1,0:T(8,128)(2,1)S(1)}, bf16[16,40,384]{2,1,0:T(8,128)(2,1)S(1)}, u32[]{:S(2)}, u32[]{:S(2)}) %collective-permute-start.3) | collective-permute-done | bytes 491552 | tf_op jit(solution)/shard_map/ppermute | solution.py:732
  39.7 0.8 copy-done.22
  40.5 1.1 collective-permute-done.7.oth1
  41.7 13.3 %layer.1 = (bf16[256,384]{1,0:T(8,128)(2,1)}, f32[256,384]{1,0:T(8,128)}, bf16[32,48,384]{2,1,0:T(8,128)(2,1)}, bf16[32,48,384]{2,1,0:T(8,128)(2,1)}) custom-call(s32[5]{0:T(128)} %stack.23.where_ref, s32[5]{0:T(128)} %res_ref.1, s32[5]{0:T(128)} %off_ref.1, f32[4,384]{1,0:T(4,128)} %norms_ref.3, s32[1,256]{1,0:T(1,128)} %bitcast.24, ...), custom_call_target="tpu_custom_call" | custom-call | tf_op jit(solution)/shard_map/layer/pallas_call | solution.py:399
  55.2 2.9 %collective-permute-done.10 = bf16[32,48,384]{2,1,0:T(8,128)(2,1)S(1)} collective-permute-done((bf16[32,48,384]{2,1,0:T(8,128)(2,1)}, bf16[32,48,384]{2,1,0:T(8,128)(2,1)S(1)}, u32[]{:S(2)}, u32[]{:S(2)}) %collective-permute-start.10) | collective-permute-done | bytes 1179680 | tf_op jit(solution)/shard_map/ppermute | solution.py:662
  58.1 1.6 %add_convert_fusion = bf16[32,48,384]{2,1,0:T(8,128)(2,1)S(1)} fusion(bf16[32,48,384]{2,1,0:T(8,128)(2,1)S(1)} %collective-permute-done.10, bf16[32,48,384]{2,1,0:T(8,128)(2,1)} %get-tuple-element.74), kind=kLoop, calls=%fused_computation | loop fusion | flops 2359296 | bytes 3538944 | tf_op jit(solution)/shard_map/convert_element_type | solution.py:748
  59.7 26.7 %all_to_all.30.parts_ref = bf16[32,48,384]{2,1,0:T(8,128)(2,1)S(1)} all-to-all(bf16[32,48,384]{2,1,0:T(8,128)(2,1)S(1)} %add_convert_fusion), channel_id=1, replica_groups=mesh['zl'=2,'x'=4,'y'=4,'c'=2,'zh'=2] {'zl','x','y'}, dimensions={0} | all-to-all | bytes 2359296 | tf_op jit(solution)/shard_map/all_to_all | solution.py:666
  86.4 1.0 sum.1
  87.4 3.6 %all-to-all-start.3 = ((bf16[16,48,384]{2,1,0:T(8,128)(2,1)}), bf16[16,48,384]{2,1,0:T(8,128)(2,1)S(1)}, u32[]{:S(2)}, u32[]{:S(2)}) async-start(bf16[16,48,384]{2,1,0:T(8,128)(2,1)} %get-tuple-element.76), calls=%async_computation.3 | async-start | bytes 1179648 | tf_op jit(solution)/shard_map/all_to_all | solution.py:666
  91.1 11.6 %all-to-all-done.3.own_ref = bf16[16,48,384]{2,1,0:T(8,128)(2,1)S(1)} async-done(((bf16[16,48,384]{2,1,0:T(8,128)(2,1)}), bf16[16,48,384]{2,1,0:T(8,128)(2,1)S(1)}, u32[]{:S(2)}, u32[]{:S(2)}) %all-to-all-start.3) | async-done | bytes 589856 | tf_op jit(solution)/shard_map/all_to_all | solution.py:666
  102.8 1.6 %tell.1 = (bf16[8,16,384]{2,1,0:T(8,128)(2,1)}, bf16[64,384]{1,0:T(8,128)(2,1)S(1)}) custom-call(s32[5]{0:T(128)S(1)} %copy-done.13, bf16[16,48,384]{2,1,0:T(8,128)(2,1)S(1)} %all-to-all-done.3.own_ref, f32[48,384]{1,0:T(8,128)S(1)} %get-tuple-element.77.piece_ref, bf16[2,64,768]{2,1,0:T(8,128)(2,1)S(1)} %copy-done.1), custom_call_target="tpu_custom_call" | custom-call | bytes 2000000 | tf_op jit(solution)/shard_map/tell/pallas_call | solution.py:452
  104.4 3.6 %all-to-all-start.4 = ((bf16[8,16,384]{2,1,0:T(8,128)(2,1)}), bf16[8,16,384]{2,1,0:T(8,128)(2,1)S(1)}, u32[]{:S(2)}, u32[]{:S(2)}) async-start(bf16[8,16,384]{2,1,0:T(8,128)(2,1)} %get-tuple-element.78), calls=%async_computation.4 | async-start | bytes 196608 | tf_op jit(solution)/shard_map/all_to_all | solution.py:666
  108.0 1.5 %collective-permute-start.11 = (bf16[64,384]{1,0:T(8,128)(2,1)S(1)}, bf16[64,384]{1,0:T(8,128)(2,1)S(1)}, u32[]{:S(2)}, u32[]{:S(2)}) collective-permute-start(bf16[64,384]{1,0:T(8,128)(2,1)S(1)} %get-tuple-element.79.small_own_ref), channel_id=1, source_target_pairs={{64,0},{65,1},{66,2},{67,3},{68,4},{69,5},{70,6},{71,7},{72,8},{73... | collective-permute-start | bytes 147464 | tf_op jit(solution)/shard_map/ppermute | solution.py:764
  109.5 4.3 %all-to-all-done.4.told_ref = bf16[8,16,384]{2,1,0:T(8,128)(2,1)S(1)} async-done(((bf16[8,16,384]{2,1,0:T(8,128)(2,1)}), bf16[8,16,384]{2,1,0:T(8,128)(2,1)S(1)}, u32[]{:S(2)}, u32[]{:S(2)}) %all-to-all-start.4) | async-done | bytes 98336 | tf_op jit(solution)/shard_map/all_to_all | solution.py:666
  113.9 9.3 %orth.1 = bf16[4,16,384]{2,1,0:T(8,128)(2,1)} custom-call(s32[5]{0:T(128)S(1)} %copy-done.13, bf16[8,16,384]{2,1,0:T(8,128)(2,1)S(1)} %all-to-all-done.4.told_ref, bf16[16,48,384]{2,1,0:T(8,128)(2,1)S(1)} %all-to-all-done.3.own_ref, bf16[16,48,384]{2,1,0:T(8,128)(2,1)S(1)} %collective-permute-done.12.oth_ref, ...), custom_call_target="tpu_custom_call" | custom-call | flops 8000000000 | bytes 4000000 | tf_op jit(solution)/shard_map/orth/pallas_call | solution.py:452
  123.2 3.3 %all-to-all-start.5 = ((bf16[4,16,384]{2,1,0:T(8,128)(2,1)}), bf16[4,16,384]{2,1,0:T(8,128)(2,1)S(1)}, u32[]{:S(2)}, u32[]{:S(2)}) async-start(bf16[4,16,384]{2,1,0:T(8,128)(2,1)} %orth.1), calls=%async_computation.5 | async-start | bytes 98304 | tf_op jit(solution)/shard_map/all_to_all | solution.py:666
  126.5 5.5 %all-to-all-done.5.back_ref = bf16[4,16,384]{2,1,0:T(8,128)(2,1)S(1)} async-done(((bf16[4,16,384]{2,1,0:T(8,128)(2,1)}), bf16[4,16,384]{2,1,0:T(8,128)(2,1)S(1)}, u32[]{:S(2)}, u32[]{:S(2)}) %all-to-all-start.5) | async-done | bytes 49184 | tf_op jit(solution)/shard_map/all_to_all | solution.py:666
  132.1 1.4 %update.1 = (f32[1,1]{1,0:T(1,128)}, f32[9,384]{1,0:T(8,128)}, f32[9,384]{1,0:T(8,128)}, f32[3,384]{1,0:T(4,128)}, f32[3,384]{1,0:T(4,128)}, /*index=5*/f32[12,3...) custom-call(s32[5]{0:T(128)S(1)} %copy-done.13, ...), custom_call_target="tpu_custom_call" | custom-call | bytes 2000000 | tf_op jit(solution)/shard_map/update/pallas_call | solution.py:452
  (63 shorter events, 0.7 us)
Async XLA Ops:
  1.3 28.0 %copy-start.12 = (s32[5]{0:T(128)S(1)}, s32[5]{0:T(128)}, u32[]{:S(2)}) copy-start(s32[5]{0:T(128)} %stack.23.where_ref) | copy-start | bytes 64
  3.0 26.3 %copy-start.14 = (bf16[12,384]{1,0:T(8,128)(2,1)S(1)}, bf16[12,384]{1,0:T(8,128)(2,1)}, u32[]{:S(2)}) copy-start(bf16[12,384]{1,0:T(8,128)(2,1)} %get-tuple-element.69.refs_0_) | copy-start | bytes 27652
  3.0 23.0 %all-to-all-start = ((bf16[16,40,384]{2,1,0:T(8,128)(2,1)}), bf16[16,40,384]{2,1,0:T(8,128)(2,1)S(1)}, u32[]{:S(2)}, u32[]{:S(2)}) async-start(bf16[16,40,384]{2,1,0:T(8,128)(2,1)} %get-tuple-element.55), calls=%async_computation | async-start | bytes 983040 | tf_op jit(solution)/shard_map/all_to_all | solution.py:721
  13.5 5.4 %collective-permute-start = (bf16[12,384]{1,0:T(8,128)(2,1)}, bf16[12,384]{1,0:T(8,128)(2,1)S(1)}, u32[]{:S(2)}, u32[]{:S(2)}) collective-permute-start(bf16[12,384]{1,0:T(8,128)(2,1)} %get-tuple-element.59), channel_id=1, source_target_pairs={{64,0},{66,2},{1,64},{3,66},{65,1},{67,3},{0,65},{2,67},{68,4},{70... | collective-permute-start | bytes 27656 | tf_op jit(solution)/shard_map/ppermute | solution.py:710
  14.3 7.8 %collective-permute-start.1 = (bf16[12,384]{1,0:T(8,128)(2,1)}, bf16[12,384]{1,0:T(8,128)(2,1)S(1)}, u32[]{:S(2)}, u32[]{:S(2)}) collective-permute-start(bf16[12,384]{1,0:T(8,128)(2,1)} %get-tuple-element.60), channel_id=1, source_target_pairs={{1,0},{3,2},{65,64},{67,66},{0,1},{2,3},{64,65},{66,67},{5,4},{7,6... | collective-permute-start | bytes 27656 | tf_op jit(solution)/shard_map/ppermute | solution.py:710
  16.6 5.6 %collective-permute-start.2 = (bf16[12,384]{1,0:T(8,128)(2,1)}, bf16[12,384]{1,0:T(8,128)(2,1)S(1)}, u32[]{:S(2)}, u32[]{:S(2)}) collective-permute-start(bf16[12,384]{1,0:T(8,128)(2,1)} %get-tuple-element.61), channel_id=1, source_target_pairs={{65,0},{67,2},{0,64},{2,66},{64,1},{66,3},{1,65},{3,67},{69,4},{71... | collective-permute-start | bytes 27656 | tf_op jit(solution)/shard_map/ppermute | solution.py:710
  26.1 10.0 %collective-permute-start.5 = (bf16[16,40,384]{2,1,0:T(8,128)(2,1)S(1)}, bf16[16,40,384]{2,1,0:T(8,128)(2,1)S(1)}, u32[]{:S(2)}, u32[]{:S(2)}) collective-permute-start(bf16[16,40,384]{2,1,0:T(8,128)(2,1)S(1)} %all-to-all-done.own0), channel_id=1, source_target_pairs={{48,0},{66,2},{112,64},{3,66},{49,1},{67,3},{113,65},{2,67},{52,4}... | collective-permute-start | bytes 1474568 | tf_op jit(solution)/shard_map/ppermute | solution.py:732
  26.1 10.0 %collective-permute-start.4 = (bf16[16,40,384]{2,1,0:T(8,128)(2,1)S(1)}, bf16[16,40,384]{2,1,0:T(8,128)(2,1)S(1)}, u32[]{:S(2)}, u32[]{:S(2)}) collective-permute-start(bf16[16,40,384]{2,1,0:T(8,128)(2,1)S(1)} %all-to-all-done.own0), channel_id=1, source_target_pairs={{4,0},{14,2},{68,64},{78,66},{5,1},{15,3},{69,65},{79,67},{8,4},{2... | collective-permute-start | bytes 1474568 | tf_op jit(solution)/shard_map/ppermute | solution.py:732
  28.0 11.6 %collective-permute-start.3 = (bf16[16,40,384]{2,1,0:T(8,128)(2,1)S(1)}, bf16[16,40,384]{2,1,0:T(8,128)(2,1)S(1)}, u32[]{:S(2)}, u32[]{:S(2)}) collective-permute-start(bf16[16,40,384]{2,1,0:T(8,128)(2,1)S(1)} %all-to-all-done.own0), channel_id=1, source_target_pairs={{16,0},{67,2},{80,64},{2,66},{17,1},{66,3},{81,65},{3,67},{20,4},{... | collective-permute-start | bytes 1474568 | tf_op jit(solution)/shard_map/ppermute | solution.py:732
  30.8 24.2 %all-to-all-start.1 = ((bf16[16,48,384]{2,1,0:T(8,128)(2,1)}), bf16[16,48,384]{2,1,0:T(8,128)(2,1)S(1)}, u32[]{:S(2)}, u32[]{:S(2)}) async-start(bf16[16,48,384]{2,1,0:T(8,128)(2,1)} %get-tuple-element.73), calls=%async_computation.1 | async-start | bytes 1179648 | tf_op jit(solution)/shard_map/all_to_all | solution.py:666
  34.5 5.2 %collective-permute-start.6 = (bf16[16,40,384]{2,1,0:T(8,128)(2,1)S(1)}, bf16[16,40,384]{2,1,0:T(8,128)(2,1)S(1)}, u32[]{:S(2)}, u32[]{:S(2)}) collective-permute-start(bf16[16,40,384]{2,1,0:T(8,128)(2,1)S(1)} %all-to-all-done.own0), channel_id=1, source_target_pairs={{0,2},{2,0},{1,3},{3,1},{4,6},{6,4},{5,7},{7,5},{8,10},{10,8},{9,1... | collective-permute-start | bytes 1474568 | tf_op jit(solution)/shard_map/ppermute | solution.py:662
  36.1 3.5 %collective-permute-start.9 = (bf16[16,40,384]{2,1,0:T(8,128)(2,1)S(1)}, bf16[16,40,384]{2,1,0:T(8,128)(2,1)S(1)}, u32[]{:S(2)}, u32[]{:S(2)}) collective-permute-start(bf16[16,40,384]{2,1,0:T(8,128)(2,1)S(1)} %collective-permute-done.5.own3), channel_id=1, source_target_pairs={{0,2},{2,0},{1,3},{3,1},{4,6},{6,4},{5,7},{7,5},{8,10},{10,8},{9,1... | collective-permute-start | bytes 1474568 | tf_op jit(solution)/shard_map/ppermute | solution.py:662
  36.1 3.5 %collective-permute-start.8 = (bf16[16,40,384]{2,1,0:T(8,128)(2,1)S(1)}, bf16[16,40,384]{2,1,0:T(8,128)(2,1)S(1)}, u32[]{:S(2)}, u32[]{:S(2)}) collective-permute-start(bf16[16,40,384]{2,1,0:T(8,128)(2,1)S(1)} %collective-permute-done.4.own2), channel_id=1, source_target_pairs={{0,2},{2,0},{1,3},{3,1},{4,6},{6,4},{5,7},{7,5},{8,10},{10,8},{9,1... | collective-permute-start | bytes 1474568 | tf_op jit(solution)/shard_map/ppermute | solution.py:662
  39.6 2.0 %collective-permute-start.7 = (bf16[16,40,384]{2,1,0:T(8,128)(2,1)S(1)}, bf16[16,40,384]{2,1,0:T(8,128)(2,1)}, u32[]{:S(2)}, u32[]{:S(2)}) collective-permute-start(bf16[16,40,384]{2,1,0:T(8,128)(2,1)S(1)} %collective-permute-done.3.own1), channel_id=1, source_target_pairs={{0,2},{2,0},{1,3},{3,1},{4,6},{6,4},{5,7},{7,5},{8,10},{10,8},{9,1... | collective-permute-start | bytes 1474568 | tf_op jit(solution)/shard_map/ppermute | solution.py:662
  55.0 3.1 %collective-permute-start.10 = (bf16[32,48,384]{2,1,0:T(8,128)(2,1)}, bf16[32,48,384]{2,1,0:T(8,128)(2,1)S(1)}, u32[]{:S(2)}, u32[]{:S(2)}) collective-permute-start(bf16[32,48,384]{2,1,0:T(8,128)(2,1)} %get-tuple-element.75), channel_id=1, source_target_pairs={{0,2},{2,0},{1,3},{3,1},{4,6},{6,4},{5,7},{7,5},{8,10},{10,8},{9,1... | collective-permute-start | bytes 3538952 | tf_op jit(solution)/shard_map/ppermute | solution.py:662
  87.4 15.3 %all-to-all-start.3 = ((bf16[16,48,384]{2,1,0:T(8,128)(2,1)}), bf16[16,48,384]{2,1,0:T(8,128)(2,1)S(1)}, u32[]{:S(2)}, u32[]{:S(2)}) async-start(bf16[16,48,384]{2,1,0:T(8,128)(2,1)} %get-tuple-element.76), calls=%async_computation.3 | async-start | bytes 1179648 | tf_op jit(solution)/shard_map/all_to_all | solution.py:666
  91.0 18.5 %collective-permute-start.13 = (bf16[16,48,384]{2,1,0:T(8,128)(2,1)S(1)}, bf16[16,48,384]{2,1,0:T(8,128)(2,1)S(1)}, u32[]{:S(2)}, u32[]{:S(2)}) collective-permute-start(bf16[16,48,384]{2,1,0:T(8,128)(2,1)S(1)} %all-to-all-done.1.old_own_ref), channel_id=1, source_target_pairs={{0,2},{2,0},{1,3},{3,1},{4,6},{6,4},{5,7},{7,5},{8,10},{10,8},{9,1... | collective-permute-start | bytes 1769480 | tf_op jit(solution)/shard_map/ppermute | solution.py:662
  102.7 11.1 %collective-permute-start.12 = (bf16[16,48,384]{2,1,0:T(8,128)(2,1)S(1)}, bf16[16,48,384]{2,1,0:T(8,128)(2,1)S(1)}, u32[]{:S(2)}, u32[]{:S(2)}) collective-permute-start(bf16[16,48,384]{2,1,0:T(8,128)(2,1)S(1)} %all-to-all-done.3.own_ref), channel_id=1, source_target_pairs={{0,2},{2,0},{1,3},{3,1},{4,6},{6,4},{5,7},{7,5},{8,10},{10,8},{9,1... | collective-permute-start | bytes 1769480 | tf_op jit(solution)/shard_map/ppermute | solution.py:662
  104.4 9.4 %all-to-all-start.4 = ((bf16[8,16,384]{2,1,0:T(8,128)(2,1)}), bf16[8,16,384]{2,1,0:T(8,128)(2,1)S(1)}, u32[]{:S(2)}, u32[]{:S(2)}) async-start(bf16[8,16,384]{2,1,0:T(8,128)(2,1)} %get-tuple-element.78), calls=%async_computation.4 | async-start | bytes 196608 | tf_op jit(solution)/shard_map/all_to_all | solution.py:666
  108.0 18.5 %collective-permute-start.11 = (bf16[64,384]{1,0:T(8,128)(2,1)S(1)}, bf16[64,384]{1,0:T(8,128)(2,1)S(1)}, u32[]{:S(2)}, u32[]{:S(2)}) collective-permute-start(bf16[64,384]{1,0:T(8,128)(2,1)S(1)} %get-tuple-element.79.small_own_ref), channel_id=1, source_target_pairs={{64,0},{65,1},{66,2},{67,3},{68,4},{69,5},{70,6},{71,7},{72,8},{73... | collective-permute-start | bytes 147464 | tf_op jit(solution)/shard_map/ppermute | solution.py:764
  113.8 18.2 %copy-start = (f32[50,384]{1,0:T(8,128)S(1)}, f32[50,384]{1,0:T(8,128)}, u32[]{:S(2)}) copy-start(f32[50,384]{1,0:T(8,128)} %table_ref.3) | copy-start | bytes 230404
  113.8 18.2 %copy-start.2 = (f32[384,9]{0,1:T(8,128)S(1)}, f32[384,9]{0,1:T(8,128)}, u32[]{:S(2)}) copy-start(f32[384,9]{0,1:T(8,128)} %param.22) | copy-start | bytes 41476
  113.8 18.2 %copy-start.3 = (f32[384,12]{0,1:T(8,128)S(1)}, f32[384,12]{0,1:T(8,128)}, u32[]{:S(2)}) copy-start(f32[384,12]{0,1:T(8,128)} %param.24) | copy-start | bytes 55300
  113.8 18.2 %copy-start.4 = (f32[12,384]{1,0:T(8,128)S(1)}, f32[12,384]{1,0:T(8,128)}, u32[]{:S(2)}) copy-start(f32[12,384]{1,0:T(8,128)} %down_ref.3) | copy-start | bytes 55300
  113.8 18.2 %copy-start.5 = (f32[384,9]{0,1:T(8,128)S(1)}, f32[384,9]{0,1:T(8,128)}, u32[]{:S(2)}) copy-start(f32[384,9]{0,1:T(8,128)} %param.26) | copy-start | bytes 41476
  113.8 18.2 %copy-start.6 = (f32[384,12]{0,1:T(8,128)S(1)}, f32[384,12]{0,1:T(8,128)}, u32[]{:S(2)}) copy-start(f32[384,12]{0,1:T(8,128)} %param.28) | copy-start | bytes 55300
  113.8 18.2 %copy-start.7 = (f32[12,384]{1,0:T(8,128)S(1)}, f32[12,384]{1,0:T(8,128)}, u32[]{:S(2)}) copy-start(f32[12,384]{1,0:T(8,128)} %down_m_ref.3) | copy-start | bytes 55300
  113.9 18.2 %copy-start.8 = (f32[50,384]{1,0:T(8,128)S(1)}, f32[50,384]{1,0:T(8,128)}, u32[]{:S(2)}) copy-start(f32[50,384]{1,0:T(8,128)} %pos_m_ref.1) | copy-start | bytes 230404
  113.9 18.2 %copy-start.9 = (f32[4,384]{1,0:T(4,128)S(1)}, f32[4,384]{1,0:T(4,128)}, u32[]{:S(2)}) copy-start(f32[4,384]{1,0:T(4,128)} %norms_ref.3) | copy-start | bytes 18436
  113.9 18.2 %copy-start.10 = (f32[3,384]{1,0:T(4,128)S(1)}, f32[3,384]{1,0:T(4,128)}, u32[]{:S(2)}) copy-start(f32[3,384]{1,0:T(4,128)} %out_ref.3) | copy-start | bytes 13828
  113.9 18.2 %copy-start.11 = (f32[3,384]{1,0:T(4,128)S(1)}, f32[3,384]{1,0:T(4,128)}, u32[]{:S(2)}) copy-start(f32[3,384]{1,0:T(4,128)} %out_m_ref.3) | copy-start | bytes 13828
  123.2 8.8 %all-to-all-start.5 = ((bf16[4,16,384]{2,1,0:T(8,128)(2,1)}), bf16[4,16,384]{2,1,0:T(8,128)(2,1)S(1)}, u32[]{:S(2)}, u32[]{:S(2)}) async-start(bf16[4,16,384]{2,1,0:T(8,128)(2,1)} %orth.1), calls=%async_computation.5 | async-start | bytes 98304 | tf_op jit(solution)/shard_map/all_to_all | solution.py:666
  (10 other events, 84.3 us)

commit v4 on v3

--- a/solution.py
+++ b/solution.py
@@ -209,31 +209,30 @@
     ]
     loads.append(pltpu.make_async_copy(stream_hbm, stream_ref, in_sems.at[8]))
     loads.append(pltpu.make_async_copy(cot_hbm, cot_ref, in_sems.at[9]))
-    for load in loads:
+    for load in loads[8:] + loads[:8]:
         load.start()
 
-    for s in range(2):
+    def grouped(s, xy, first):
+        ahead = xy // 4 + 2 * (xy % 4) - colour + 4
+        return jnp.concatenate(
+            [
+                weights_ref[4 * s + ((ahead - z) & 3), xy].astype(F32)[first : first + BLOCK]
+                for z in range(4)
+            ],
+            axis=0,
+        )
+
+    for load in loads[8:]:
+        load.wait()
+    stream_in = stream_ref[...]
+    g1, s1, g2, s2 = (norms_ref[k : k + 1, :] for k in range(4))
+    n1, r1 = norm_parts(stream_in)
+    y1 = (n1 * g1 + s1).astype(BF)
+    for s, at_core in ((0, core), (1, 1 - core)):
         for load in loads[4 * s : 4 * s + 4]:
             load.wait()
-        for here in range(4):
-
-            @pl.when(colour == here)
-            def _(s=s, here=here):
-                for xy in range(16):
-                    ahead = xy // 4 + 2 * (xy % 4) - here
-                    blocks = [weights_ref[4 * s + (ahead - z) % 4, xy].astype(F32) for z in range(4)]
-                    at = s * 768 + xy * GROUP
-                    groups = [
-                        jnp.concatenate([block[k : k + BLOCK] for block in blocks], axis=0)
-                        for k in (0, 12, 24)
-                    ]
-                    wup[at : at + GROUP] = groups[0].astype(BF)
-                    wdn[at : at + GROUP] = groups[1].astype(BF)
-                    mixed[core if s == 0 else 1 - core, xy * GROUP : (xy + 1) * GROUP] = groups[2]
-
-    for load in loads[8:]:
-        load.wait()
-
+        for xy in range(16):
+            mixed[at_core, xy * GROUP : (xy + 1) * GROUP] = grouped(s, xy, 24)
     for at_core, at, block in blocks_of_rows():
         for first, length, to in qkv_pieces(block):
             sorted_qkv[to : to + length] = mixed[at_core, at + first : at + first + length]
@@ -242,10 +241,6 @@
     wout[...] = sorted_out[...].astype(BF)
 
 
-    stream_in = stream_ref[...]
-    g1, s1, g2, s2 = (norms_ref[k : k + 1, :] for k in range(4))
-    n1, r1 = norm_parts(stream_in)
-    y1 = (n1 * g1 + s1).astype(BF)
     qkv_ref[...] = dot_nt(y1, wqkv[...]).astype(BF)
 
     def segments(shape, dim):
@@ -285,6 +280,10 @@
     out = stream_mid
     d_y2 = 0.0
     for k in range(4):
+        for xy in range(8):
+            at = k * 384 + xy * GROUP
+            wup[at : at + GROUP] = grouped(k // 2, (k % 2) * 8 + xy, 0).astype(BF)
+            wdn[at : at + GROUP] = grouped(k // 2, (k % 2) * 8 + xy, 12).astype(BF)
         wu = wup[k * 384 : (k + 1) * 384, :]
         wd = wdn[k * 384 : (k + 1) * 384, :]
         pre = dot_nt(y2, wu)
@@ -461,29 +460,21 @@
     )(*args)
 
 
-def prepare_kernel(
-    where_ref,
-    qkv_ref,
-    out_ref,
-    up_ref,
-    down_ref,
-    qkv_m_ref,
-    out_m_ref,
-    up_m_ref,
-    down_m_ref,
-    rows_ref,
-    *old_refs,
-):
-    zeros = jnp.zeros((16, D), F32)
+def weights_kernel(qkv_ref, out_ref, up_ref, down_ref, rows_ref):
     rows = jnp.concatenate(
-        [up_ref[...], down_ref[...], qkv_ref[...], out_ref[...], zeros[: SENT - 36]], axis=0
+        [up_ref[...], down_ref[...], qkv_ref[...], out_ref[...], jnp.zeros((SENT - 36, D), F32)],
+        axis=0,
     ).astype(BF)
     rows_ref[...] = jnp.broadcast_to(rows[None], rows_ref.shape)
+
+
+def moments_kernel(where_ref, qkv_ref, out_ref, up_ref, down_ref, *old_refs):
+    zeros = jnp.zeros((9, D), F32)
     old = (
-        up_m_ref[...],
-        jnp.concatenate([zeros[:9], out_m_ref[...]], axis=0),
-        down_m_ref[...],
-        jnp.concatenate([qkv_m_ref[...], zeros[:3]], axis=0),
+        up_ref[...],
+        jnp.concatenate([zeros, out_ref[...]], axis=0),
+        down_ref[...],
+        jnp.concatenate([qkv_ref[...], zeros[:3]], axis=0),
     )
     for z in range(4):
 
@@ -506,6 +497,10 @@
             sent_ref[...] = jnp.broadcast_to(joined[None], sent_ref.shape)
 
 
+def hold_kernel(keep_ref, held_ref):
+    held_ref[...] = keep_ref[...]
+
+
 def sum_kernel(parts_ref, piece_ref, sent_ref):
     total = parts_ref[0].astype(F32)
     for k in range(1, parts_ref.shape[0]):
@@ -519,18 +514,15 @@
     return jnp.where(z == 1, (row >= 9).astype(F32), jnp.where(z == 3, (row < 9).astype(F32), 1.0))
 
 
-def tell_kernel(where_ref, own_ref, piece_ref, places_ref, told_ref, small_ref):
+def tell_kernel(where_ref, own_ref, piece_ref, told_ref):
     z = where_ref[3]
-    valid = valid_rows(z)
+    counts_all = (z == 1) & (where_ref[0] == 0)
+    valid = jnp.where(counts_all, 1.0, valid_rows(z))
     total = jnp.zeros((GROUP, D), F32)
     for xy in range(16):
-        g = own_ref[xy].astype(F32) * valid
+        g = own_ref[xy].astype(F32)
         total = total + g * g
-    small = dot(places_ref[where_ref[1]], own_ref[...].reshape(768, D))
-    small_ref[...] = small.astype(BF)
-    counted = jnp.where((z == 1) & (where_ref[0] == 0), 1.0, 0.0)
-    squares = jnp.sum(total) + counted * jnp.sum(small * small)
-    squares = jnp.full((1, D), squares, F32)
+    squares = jnp.full((1, D), jnp.sum(total * valid), F32)
     high = squares.astype(BF).astype(F32)
     mid = (squares - high).astype(BF).astype(F32)
     low = squares - high - mid
@@ -541,6 +533,10 @@
         ).astype(BF)
         told_ref[2 * to] = rows
         told_ref[2 * to + 1] = rows
+
+
+def small_kernel(where_ref, own_ref, places_ref, small_ref):
+    small_ref[...] = dot(places_ref[where_ref[1]], own_ref[...].reshape(768, D)).astype(BF)
 
 
 def clip(told_ref):
@@ -581,19 +577,19 @@
     inv = 1.0 / (jnp.sqrt(jnp.sum(gram * eye)) + 1e-07)
     gram = gram * (inv * inv)
     mine = (MOMENTUM * old_ref[...].astype(F32) + scaled * piece_ref[...]) * inv
-    for step in range(NS_STEPS):
+    for step in range(NS_STEPS - 2):
         parts = halves(gram)
-        if step in (0, 1, NS_STEPS - 1):
-            square = dot(parts[0], parts[0])
-        else:
-            square = product(parts, parts)
-        poly = COEF_A * eye + COEF_B * gram + COEF_C * square
-        if step == NS_STEPS - 1:
-            mine = dot(mine.astype(BF), poly.astype(BF))
-        else:
-            poly = halves(poly)
-            gram = product(halves(product(poly, parts)), poly)
-            mine = product(halves(mine), poly)
+        poly = halves(COEF_A * eye + COEF_B * gram + COEF_C * dot(parts[0], parts[0]))
+        gram = product(halves(product(poly, parts)), poly)
+        mine = product(halves(mine), poly)
+    parts = halves(gram)
+    poly = (COEF_A * eye + COEF_B * gram + COEF_C * product(parts, parts)).astype(BF)
+    turned = dot(poly, parts[0]).astype(BF)
+    both = dot(jnp.concatenate([turned, mine.astype(BF)], axis=0), poly)
+    gram, mine = both[:D], both[D:]
+    low = gram.astype(BF)
+    poly = COEF_A * eye + COEF_B * gram + COEF_C * dot(low, low)
+    mine = dot(mine.astype(BF), poly.astype(BF))
     for z in range(4):
         out_ref[z] = jnp.concatenate(
             [mine[z * BLOCK : (z + 1) * BLOCK], jnp.zeros((4, D), F32)], axis=0
@@ -604,16 +600,11 @@
     return math.sqrt(max(rows_count, cols_count) / rows_count)
 
 
-def update_kernel(
+def moment_kernel(
     where_ref,
     told_ref,
     small_own_ref,
     small_near_ref,
-    back_ref,
-    qkv_ref,
-    out_ref,
-    up_ref,
-    down_ref,
     qkv_m_ref,
     out_m_ref,
     up_m_ref,
@@ -624,13 +615,9 @@
     pos_m_ref,
     grad_norm_ref,
     qkv_m_next,
-    qkv_next,
     out_m_next,
-    out_next,
     up_m_next,
-    up_next,
     down_m_next,
-    down_next,
     norm_m_next,
     norms_next,
     pos_m_next,
@@ -638,16 +625,14 @@
 ):
     grad_norm, factor = clip(told_ref)
     grad_norm_ref[...] = grad_norm
-    for z, first, last, rate, w_ref, m_ref, w_next, m_next in (
-        (3, 0, 9, step_rate(D, 3 * D), qkv_ref, qkv_m_ref, qkv_next, qkv_m_next),
-        (1, 9, 12, step_rate(D, D), out_ref, out_m_ref, out_next, out_m_next),
-        (0, 0, 12, step_rate(D, FF), up_ref, up_m_ref, up_next, up_m_next),
-        (2, 0, 12, step_rate(FF, D), down_ref, down_m_ref, down_next, down_m_next),
+    for z, first, last, m_ref, m_next in (
+        (3, 0, 9, qkv_m_ref, qkv_m_next),
+        (1, 9, 12, out_m_ref, out_m_next),
+        (0, 0, 12, up_m_ref, up_m_next),
+        (2, 0, 12, down_m_ref, down_m_next),
     ):
         grad = told_ref[2 * z + where_ref[0]].astype(F32)[first:last]
-        orth = back_ref[z].astype(F32)[first:last]
         m_next[...] = MOMENTUM * m_ref[...] + factor * grad
-        w_next[...] = w_ref[...] - rate * orth
     near = (where_ref[3] % 2 == 0).astype(F32)
     small = near * small_near_ref[...].astype(F32) + (1.0 - near) * small_own_ref[...].astype(F32)
     norm_fresh = MOMENTUM * norm_m_ref[...] + factor * small[50:54]
@@ -656,6 +641,18 @@
     pos_fresh = MOMENTUM * pos_m_ref[...] + factor * small[:50]
     pos_m_next[...] = pos_fresh
     table_next[...] = table_ref[...] - SMALL_RATE * pos_fresh
+
+
+def update_kernel(
+    back_ref, qkv_ref, out_ref, up_ref, down_ref, qkv_next, out_next, up_next, down_next
+):
+    for z, first, last, rate, w_ref, w_next in (
+        (3, 0, 9, step_rate(D, 3 * D), qkv_ref, qkv_next),
+        (1, 9, 12, step_rate(D, D), out_ref, out_next),
+        (0, 0, 12, step_rate(D, FF), up_ref, up_next),
+        (2, 0, 12, step_rate(FF, D), down_ref, down_next),
+    ):
+        w_next[...] = w_ref[...] - rate * back_ref[z].astype(F32)[first:last]
 
 
 def swapped(value):
@@ -698,13 +695,15 @@
     weights = (qkv_weight.T, out_weight, up_weight.T, down_weight)
     moments = (qkv_moment.T, out_moment, up_moment.T, down_moment)
 
-    rows, *old = call(
-        prepare_kernel,
-        "prepare",
-        (((16, SENT, D), BF), *(((BLOCK, D), BF) for _ in range(4))),
-        (where, *weights, *moments),
+    (rows,) = call(
+        weights_kernel, "weights", (((16, SENT, D), BF),), weights, vmem_bytes=ALL_VMEM
+    )
+    old = call(
+        moments_kernel,
+        "moments",
+        (((BLOCK, D), BF),) * 4,
+        (where, *moments),
         scalars=1,
-        moved=4_000_000,
         vmem_bytes=ALL_VMEM,
     )
     old = [old[0]] + [lax.ppermute(old[k], AXES, column_step(k)) for k in (1, 2, 3)]
@@ -731,6 +730,7 @@
     )
     own += [lax.ppermute(own[0], AXES, colour_step(step)) for step in (1, 2, 3)]
     other = [swapped(value) for value in own]
+    old_sent, other[0] = lax.optimization_barrier((old_sent, other[0]))
     old_own = exchanged(old_sent, PLANE)
 
     result, in_grad, keep, send = run_layer(
@@ -745,22 +745,25 @@
     )
     keep, send, old_own = lax.optimization_barrier((keep, send, old_own))
     old_other = swapped(old_own)
+    (keep,) = call(hold_kernel, "hold", ((keep.shape, BF),), (keep,))
     pair = (keep.astype(F32) + swapped(send).astype(F32)).astype(BF)
     piece, sent = call(
         sum_kernel, "sum", (((GROUP, D), F32), ((16, GROUP, D), BF)), (exchanged(pair, HALF),)
     )
     grads = exchanged(sent, PLANE)
-    grads_other = swapped(grads)
-
-    told, small = call(
-        tell_kernel,
-        "tell",
-        (((8, 16, D), BF), ((64, D), BF)),
-        (where, grads, piece, jnp.asarray(small_places(), BF)),
+    (told,) = call(
+        tell_kernel, "tell", (((8, 16, D), BF),), (where, grads, piece), scalars=1
+    )
+    told, grads_sent = lax.optimization_barrier((told, grads))
+    told = exchanged(told, COLUMN_CORES)
+    grads_other = swapped(grads_sent)
+    (small,) = call(
+        small_kernel,
+        "small",
+        (((64, D), BF),),
+        (where, grads_sent, jnp.asarray(small_places(), BF)),
         scalars=1,
-        moved=2_000_000,
-    )
-    told = exchanged(told, COLUMN_CORES)
+    )
     small_near = lax.ppermute(small, "zl", [(1, 0)])
     (orth,) = call(
         orth_kernel,
@@ -774,24 +777,35 @@
     )
     back = exchanged(orth, COLUMN)
     like = lambda a: (a.shape, F32)
-    grad_norm, *news = call(
-        update_kernel,
-        "update",
+    grad_norm, *fresh = call(
+        moment_kernel,
+        "moment",
         (
             ((1, 1), F32),
-            *(like(a) for pair_of in zip(moments, weights) for a in pair_of),
+            *(like(a) for a in moments),
             like(norm_moment),
             like(norm_params),
             like(pos_moment),
             like(pos_table),
         ),
-        (where, told, small, small_near, back, *weights, *moments, norm_params, norm_moment, pos_table, pos_moment),
+        (where, told, small, small_near, *moments, norm_params, norm_moment, pos_table, pos_moment),
         scalars=1,
-        moved=2_000_000,
-    )
-    for k in (0, 1, 4, 5):
-        news[k] = news[k].T
-    return (result, in_grad, grad_norm.reshape(()), *news)
+    )
+    news = call(update_kernel, "update", [like(a) for a in weights], (back, *weights))
+    return (
+        result,
+        in_grad,
+        grad_norm.reshape(()),
+        fresh[0].T,
+        news[0].T,
+        fresh[1],
+        news[1],
+        fresh[2].T,
+        news[2].T,
+        fresh[3],
+        news[3],
+        *fresh[4:],
+    )
 
 
 def solution(mesh):

time: 134 us -> 130 us (0.970)
  waiting for transfers between devices: 37.2 us -> 28.5 us
  local copies, waits for them, and re-layouts: 1.54 us -> 4.14 us
    ppermute x3, waiting for transfers between devices: 4.57 us -> 0.01 us  [shards(): own += [lax.ppermute(own[0], AXES, colour_step(step)) for step in (1, 2, 3)]]
    unnamed x46 -> x48, local copies, waits for them, and re-layouts: 0.94 us -> 3.54 us
    all_to_all x4, waiting for transfers between devices: 21.4 us -> 19.2 us  [exchanged(): return lax.all_to_all(value, axes, 0, 0, tiled=True)]
    all_to_all x1, waiting for transfers between devices: 3.84 us -> 1.75 us  [shards(): lax.all_to_all(rows, AXES, 0, 0, axis_index_groups=colour_groups(), tiled...]
    pallas_call x7 -> x11, Pallas kernels: 18.7 us -> 20.3 us  [call(): pl.pallas_call(kernel, out_shape=tuple((jax.ShapeDtypeStruct(shape, dtype...]
  transfers between devices with their start and end apart: 19 -> 19, of which waited for: 10 -> 9; matrix products, arithmetic and copies ran while one was open for 0% -> 0% of each run, Pallas kernels for 21% -> 23%
where the time goes in v4:
time: 130 us; the launch traced here: 129 us
  starting transfers between devices  34.7 us (27%)
  Pallas kernels  33.3 us (26%)
  waiting for transfers between devices  28.5 us (22%)
  blocking collectives  26.6 us (20%)
  local copies, waits for them, and re-layouts  4.14 us (3%)
    all_to_all x1, blocking collectives, exchanged(): return lax.all_to_all(value, axes, 0, 0, tiled=True)  26.6 us
    pallas_call x11, Pallas kernels, call(): pl.pallas_call(kernel, out_shape=tuple((jax.ShapeDtypeStruct(shape, dtype...  20.3 us
    all_to_all x4, waiting for transfers between devices, exchanged(): return lax.all_to_all(value, axes, 0, 0, tiled=True)  19.2 us
    all_to_all x4, starting transfers between devices, exchanged(): return lax.all_to_all(value, axes, 0, 0, tiled=True)  14 us
    pallas_call x1, Pallas kernels, run_layer(): pl.pallas_call(layer_kernel, out_shape=(jax.ShapeDtypeStruct((count, D),...  13 us
    all_to_all x1, starting transfers between devices, shards(): lax.all_to_all(rows, AXES, 0, 0, axis_index_groups=colour_groups(), tiled...  10.4 us
    ppermute x3, starting transfers between devices, shards(): own += [lax.ppermute(own[0], AXES, colour_step(step)) for step in (1, 2, 3)]  4.54 us
    ppermute x7, waiting for transfers between devices, swapped(): return lax.ppermute(value, 'c', [(0, 1), (1, 0)])  4.02 us
  transfers between devices with their start and end apart: 19, of which 9 were waited for; matrix products, arithmetic and copies ran while one was open for 0% of the time, Pallas kernels for 23%

profile of v4, /device:TPU:0, one launch (start us, length us, event | category | flops | bytes accessed | tf_op | source)
XLA Modules:
  0.0 128.6 jit_solution(194769366781532733)
XLA Ops:
  0.6 1.6 %weights.1 = bf16[16,40,384]{2,1,0:T(8,128)(2,1)} custom-call(f32[9,384]{1,0:T(8,128)} %bitcast.19, f32[3,384]{1,0:T(4,128)} %out_ref.5, f32[12,384]{1,0:T(8,128)} %bitcast.21, f32[12,384]{1,0:T(8,128)} %down_ref.5), custom_call_target="tpu_custom_call" | custom-call | tf_op jit(solution)/shard_map/weights/pallas_call | solution.py:451
  2.3 10.4 %all-to-all-start = ((bf16[16,40,384]{2,1,0:T(8,128)(2,1)}), bf16[16,40,384]{2,1,0:T(8,128)(2,1)S(1)}, u32[]{:S(2)}, u32[]{:S(2)}) async-start(bf16[16,40,384]{2,1,0:T(8,128)(2,1)} %weights.1), calls=%async_computation | async-start | bytes 983040 | tf_op jit(solution)/shard_map/all_to_all | solution.py:720
  13.3 1.4 %moments.1 = (bf16[12,384]{1,0:T(8,128)(2,1)}, bf16[12,384]{1,0:T(8,128)(2,1)}, bf16[12,384]{1,0:T(8,128)(2,1)}, bf16[12,384]{1,0:T(8,128)(2,1)}) custom-call(s32[5]{0:T(128)} %stack.23.where_ref, f32[9,384]{1,0:T(8,128)} %bitcast.15, f32[3,384]{1,0:T(4,128)} %out_m_ref.1, f32[12,384]{1,0:T(8,128)} %bitcast.17, f32[12,384]{1,0:T(8,128)} %down_m_ref.1), custom_call_target="tpu_custom_call" | custom-call | tf_op jit(solution)/shard_map/moments/pallas_call | solution.py:451
  14.8 0.7 collective-permute-start
  15.5 2.4 %collective-permute-start.1 = (bf16[12,384]{1,0:T(8,128)(2,1)}, bf16[12,384]{1,0:T(8,128)(2,1)S(1)}, u32[]{:S(2)}, u32[]{:S(2)}) collective-permute-start(bf16[12,384]{1,0:T(8,128)(2,1)} %get-tuple-element.60), channel_id=1, source_target_pairs={{1,0},{3,2},{65,64},{67,66},{0,1},{2,3},{64,65},{66,67},{5,4},{7,6... | collective-permute-start | bytes 27656 | tf_op jit(solution)/shard_map/ppermute | solution.py:709
  17.9 2.2 %embed.1 = (f32[256,384]{1,0:T(8,128)}, bf16[256,384]{1,0:T(8,128)(2,1)}) custom-call(bf16[256,384]{1,0:T(8,128)(2,1)} %tok_ref.1, bf16[256,384]{1,0:T(8,128)(2,1)} %cot_ref.1, f32[50,384]{1,0:T(8,128)} %table_ref.3, s32[1,256]{1,0:T(1,128)} %bitcast.23), custom_call_target="tpu_custom_call" | custom-call | tf_op jit(solution)/shard_map/embed/pallas_call | solution.py:451
  20.1 1.4 %collective-permute-done.1.refs_2_ = bf16[12,384]{1,0:T(8,128)(2,1)S(1)} collective-permute-done((bf16[12,384]{1,0:T(8,128)(2,1)}, bf16[12,384]{1,0:T(8,128)(2,1)S(1)}, u32[]{:S(2)}, u32[]{:S(2)}) %collective-permute-start.1) | collective-permute-done | bytes 9248 | tf_op jit(solution)/shard_map/ppermute | solution.py:709
  21.5 2.0 %collective-permute-done.2.refs_3_ = bf16[12,384]{1,0:T(8,128)(2,1)S(1)} collective-permute-done((bf16[12,384]{1,0:T(8,128)(2,1)}, bf16[12,384]{1,0:T(8,128)(2,1)S(1)}, u32[]{:S(2)}, u32[]{:S(2)}) %collective-permute-start.2) | collective-permute-done | bytes 9248 | tf_op jit(solution)/shard_map/ppermute | solution.py:709
  23.5 1.8 %all-to-all-done.own0 = bf16[16,40,384]{2,1,0:T(8,128)(2,1)S(1)} async-done(((bf16[16,40,384]{2,1,0:T(8,128)(2,1)}), bf16[16,40,384]{2,1,0:T(8,128)(2,1)S(1)}, u32[]{:S(2)}, u32[]{:S(2)}) %all-to-all-start) | async-done | bytes 491552 | tf_op jit(solution)/shard_map/all_to_all | solution.py:720
  25.4 2.2 %collective-permute-start.4 = (bf16[16,40,384]{2,1,0:T(8,128)(2,1)S(1)}, bf16[16,40,384]{2,1,0:T(8,128)(2,1)S(1)}, u32[]{:S(2)}, u32[]{:S(2)}) collective-permute-start(bf16[16,40,384]{2,1,0:T(8,128)(2,1)S(1)} %all-to-all-done.own0), channel_id=1, source_target_pairs={{4,0},{14,2},{68,64},{78,66},{5,1},{15,3},{69,65},{79,67},{8,4},{2... | collective-permute-start | bytes 1474568 | tf_op jit(solution)/shard_map/ppermute | solution.py:731
  27.6 2.2 %collective-permute-start.3 = (bf16[16,40,384]{2,1,0:T(8,128)(2,1)S(1)}, bf16[16,40,384]{2,1,0:T(8,128)(2,1)S(1)}, u32[]{:S(2)}, u32[]{:S(2)}) collective-permute-start(bf16[16,40,384]{2,1,0:T(8,128)(2,1)S(1)} %all-to-all-done.own0), channel_id=1, source_target_pairs={{16,0},{67,2},{80,64},{2,66},{17,1},{66,3},{81,65},{3,67},{20,4},{... | collective-permute-start | bytes 1474568 | tf_op jit(solution)/shard_map/ppermute | solution.py:731
  31.2 1.4 %join.1 = (bf16[48,384]{1,0:T(8,128)(2,1)S(1)}, bf16[16,48,384]{2,1,0:T(8,128)(2,1)}) custom-call(s32[5]{0:T(128)S(1)} %copy-done.10, bf16[12,384]{1,0:T(8,128)(2,1)S(1)} %copy-done.15, bf16[12,384]{1,0:T(8,128)(2,1)S(1)} %collective-permute-done.refs_1_, bf16[12,384]{1,0:T(8,128)(2,1)S(1)} %collective-permute-done.1.refs_2_, ...), custom_call_target="tpu_custom_call" | custom-call | tf_op jit(solution)/shard_map/join/pallas_call | solution.py:451
  32.7 3.6 %all-to-all-start.1 = ((bf16[16,48,384]{2,1,0:T(8,128)(2,1)}), bf16[16,48,384]{2,1,0:T(8,128)(2,1)S(1)}, u32[]{:S(2)}, u32[]{:S(2)}) async-start(bf16[16,48,384]{2,1,0:T(8,128)(2,1)} %get-tuple-element.75), calls=%async_computation.1 | async-start | bytes 1179648 | tf_op jit(solution)/shard_map/all_to_all | solution.py:663
  37.1 1.1 collective-permute-done.9.oth3
  38.2 1.4 %collective-permute-done.8.oth2 = bf16[16,40,384]{2,1,0:T(8,128)(2,1)S(1)} collective-permute-done((bf16[16,40,384]{2,1,0:T(8,128)(2,1)S(1)}, bf16[16,40,384]{2,1,0:T(8,128)(2,1)S(1)}, u32[]{:S(2)}, u32[]{:S(2)}) %collective-permute-start.8) | collective-permute-done | bytes 491552 | tf_op jit(solution)/shard_map/ppermute | solution.py:659
  39.6 0.8 copy-done.23
  40.5 13.0 %layer.1 = (bf16[256,384]{1,0:T(8,128)(2,1)}, f32[256,384]{1,0:T(8,128)}, bf16[32,48,384]{2,1,0:T(8,128)(2,1)}, bf16[32,48,384]{2,1,0:T(8,128)(2,1)}) custom-call(s32[5]{0:T(128)} %stack.23.where_ref, s32[5]{0:T(128)} %res_ref.1, s32[5]{0:T(128)} %off_ref.1, f32[4,384]{1,0:T(4,128)} %norms_ref.3, s32[1,256]{1,0:T(1,128)} %bitcast.24, ...), custom_call_target="tpu_custom_call" | custom-call | tf_op jit(solution)/shard_map/layer/pallas_call | solution.py:398
  53.7 1.3 copy-done
  55.1 1.5 %collective-permute-done.10 = bf16[32,48,384]{2,1,0:T(8,128)(2,1)S(1)} collective-permute-done((bf16[32,48,384]{2,1,0:T(8,128)(2,1)}, bf16[32,48,384]{2,1,0:T(8,128)(2,1)S(1)}, u32[]{:S(2)}, u32[]{:S(2)}) %collective-permute-start.10) | collective-permute-done | bytes 1179680 | tf_op jit(solution)/shard_map/ppermute | solution.py:659
  56.9 26.6 %all_to_all.30.parts_ref = bf16[32,48,384]{2,1,0:T(8,128)(2,1)S(1)} all-to-all(bf16[32,48,384]{2,1,0:T(8,128)(2,1)S(1)} %add_convert_fusion), channel_id=1, replica_groups=mesh['zl'=2,'x'=4,'y'=4,'c'=2,'zh'=2] {'zl','x','y'}, dimensions={0} | all-to-all | bytes 2359296 | tf_op jit(solution)/shard_map/all_to_all | solution.py:663
  83.5 1.0 sum.1
  84.5 3.7 %all-to-all-start.3 = ((bf16[16,48,384]{2,1,0:T(8,128)(2,1)}), bf16[16,48,384]{2,1,0:T(8,128)(2,1)S(1)}, u32[]{:S(2)}, u32[]{:S(2)}) async-start(bf16[16,48,384]{2,1,0:T(8,128)(2,1)} %get-tuple-element.78), calls=%async_computation.3 | async-start | bytes 1179648 | tf_op jit(solution)/shard_map/all_to_all | solution.py:663
  88.4 11.6 %all-to-all-done.3.own_ref = bf16[16,48,384]{2,1,0:T(8,128)(2,1)S(1)} async-done(((bf16[16,48,384]{2,1,0:T(8,128)(2,1)}), bf16[16,48,384]{2,1,0:T(8,128)(2,1)S(1)}, u32[]{:S(2)}, u32[]{:S(2)}) %all-to-all-start.3) | async-done | bytes 589856 | tf_op jit(solution)/shard_map/all_to_all | solution.py:663
  100.0 1.4 %tell.1 = bf16[8,16,384]{2,1,0:T(8,128)(2,1)} custom-call(s32[5]{0:T(128)S(1)} %copy-done.11, bf16[16,48,384]{2,1,0:T(8,128)(2,1)S(1)} %all-to-all-done.3.own_ref, f32[48,384]{1,0:T(8,128)S(1)} %get-tuple-element.79.piece_ref), custom_call_target="tpu_custom_call" | custom-call | tf_op jit(solution)/shard_map/tell/pallas_call | solution.py:451
  101.4 3.4 %all-to-all-start.4 = ((bf16[8,16,384]{2,1,0:T(8,128)(2,1)}), bf16[8,16,384]{2,1,0:T(8,128)(2,1)S(1)}, u32[]{:S(2)}, u32[]{:S(2)}) async-start(bf16[8,16,384]{2,1,0:T(8,128)(2,1)} %tell.1), calls=%async_computation.4 | async-start | bytes 196608 | tf_op jit(solution)/shard_map/all_to_all | solution.py:663
  104.8 0.8 small.1.small_own_ref
  105.6 1.5 %collective-permute-start.11 = (bf16[64,384]{1,0:T(8,128)(2,1)S(1)}, bf16[64,384]{1,0:T(8,128)(2,1)S(1)}, u32[]{:S(2)}, u32[]{:S(2)}) collective-permute-start(bf16[64,384]{1,0:T(8,128)(2,1)S(1)} %small.1.small_own_ref), channel_id=1, source_target_pairs={{64,0},{65,1},{66,2},{67,3},{68,4},{69,5},{70,6},{71,7},{72,8},{73... | collective-permute-start | bytes 147464 | tf_op jit(solution)/shard_map/ppermute | solution.py:767
  107.1 3.5 %all-to-all-done.4.told_ref = bf16[8,16,384]{2,1,0:T(8,128)(2,1)S(1)} async-done(((bf16[8,16,384]{2,1,0:T(8,128)(2,1)}), bf16[8,16,384]{2,1,0:T(8,128)(2,1)S(1)}, u32[]{:S(2)}, u32[]{:S(2)}) %all-to-all-start.4) | async-done | bytes 98336 | tf_op jit(solution)/shard_map/all_to_all | solution.py:663
  110.7 8.4 %orth.1 = bf16[4,16,384]{2,1,0:T(8,128)(2,1)} custom-call(s32[5]{0:T(128)S(1)} %copy-done.11, bf16[8,16,384]{2,1,0:T(8,128)(2,1)S(1)} %all-to-all-done.4.told_ref, bf16[16,48,384]{2,1,0:T(8,128)(2,1)S(1)} %all-to-all-done.3.own_ref, bf16[16,48,384]{2,1,0:T(8,128)(2,1)S(1)} %collective-permute-done.12.oth_ref, ...), custom_call_target="tpu_custom_call" | custom-call | flops 8000000000 | bytes 4000000 | tf_op jit(solution)/shard_map/orth/pallas_call | solution.py:451
  119.1 3.3 %all-to-all-start.5 = ((bf16[4,16,384]{2,1,0:T(8,128)(2,1)}), bf16[4,16,384]{2,1,0:T(8,128)(2,1)S(1)}, u32[]{:S(2)}, u32[]{:S(2)}) async-start(bf16[4,16,384]{2,1,0:T(8,128)(2,1)} %orth.1), calls=%async_computation.5 | async-start | bytes 98304 | tf_op jit(solution)/shard_map/all_to_all | solution.py:663
  122.5 1.3 %moment.1 = (f32[1,1]{1,0:T(1,128)}, f32[9,384]{1,0:T(8,128)}, f32[3,384]{1,0:T(4,128)}, f32[12,384]{1,0:T(8,128)}, f32[12,384]{1,0:T(8,128)}, /*index=5*/f32[4,...) custom-call(s32[5]{0:T(128)S(1)} %copy-done.11, bf16[8,16,384]{2,1,0:T(8,128)(2,1)S(1)} %all-to-all-done.4.told_ref, ...), custom_call_target="tpu_custom_call" | custom-call | tf_op jit(solution)/shard_map/moment/pallas_call | solution.py:451
  123.8 4.1 %all-to-all-done.5.back_ref = bf16[4,16,384]{2,1,0:T(8,128)(2,1)S(1)} async-done(((bf16[4,16,384]{2,1,0:T(8,128)(2,1)}), bf16[4,16,384]{2,1,0:T(8,128)(2,1)S(1)}, u32[]{:S(2)}, u32[]{:S(2)}) %all-to-all-start.5) | async-done | bytes 49184 | tf_op jit(solution)/shard_map/all_to_all | solution.py:663
  (69 shorter events, 4.4 us)
Async XLA Ops:
  2.3 23.0 %all-to-all-start = ((bf16[16,40,384]{2,1,0:T(8,128)(2,1)}), bf16[16,40,384]{2,1,0:T(8,128)(2,1)S(1)}, u32[]{:S(2)}, u32[]{:S(2)}) async-start(bf16[16,40,384]{2,1,0:T(8,128)(2,1)} %weights.1), calls=%async_computation | async-start | bytes 983040 | tf_op jit(solution)/shard_map/all_to_all | solution.py:720
  14.8 5.3 %collective-permute-start = (bf16[12,384]{1,0:T(8,128)(2,1)}, bf16[12,384]{1,0:T(8,128)(2,1)S(1)}, u32[]{:S(2)}, u32[]{:S(2)}) collective-permute-start(bf16[12,384]{1,0:T(8,128)(2,1)} %get-tuple-element.59), channel_id=1, source_target_pairs={{64,0},{66,2},{1,64},{3,66},{65,1},{67,3},{0,65},{2,67},{68,4},{70... | collective-permute-start | bytes 27656 | tf_op jit(solution)/shard_map/ppermute | solution.py:709
  15.5 6.0 %collective-permute-start.1 = (bf16[12,384]{1,0:T(8,128)(2,1)}, bf16[12,384]{1,0:T(8,128)(2,1)S(1)}, u32[]{:S(2)}, u32[]{:S(2)}) collective-permute-start(bf16[12,384]{1,0:T(8,128)(2,1)} %get-tuple-element.60), channel_id=1, source_target_pairs={{1,0},{3,2},{65,64},{67,66},{0,1},{2,3},{64,65},{66,67},{5,4},{7,6... | collective-permute-start | bytes 27656 | tf_op jit(solution)/shard_map/ppermute | solution.py:709
  17.9 5.7 %collective-permute-start.2 = (bf16[12,384]{1,0:T(8,128)(2,1)}, bf16[12,384]{1,0:T(8,128)(2,1)S(1)}, u32[]{:S(2)}, u32[]{:S(2)}) collective-permute-start(bf16[12,384]{1,0:T(8,128)(2,1)} %get-tuple-element.61), channel_id=1, source_target_pairs={{65,0},{67,2},{0,64},{2,66},{64,1},{66,3},{1,65},{3,67},{69,4},{71... | collective-permute-start | bytes 27656 | tf_op jit(solution)/shard_map/ppermute | solution.py:709
  25.3 15.1 %copy-start.17 = (bf16[16,40,384]{2,1,0:T(8,128)(2,1)}, bf16[16,40,384]{2,1,0:T(8,128)(2,1)S(1)}, u32[]{:S(2)}) copy-start(bf16[16,40,384]{2,1,0:T(8,128)(2,1)S(1)} %all-to-all-done.own0) | copy-start | bytes 1474564
  25.3 7.4 %collective-permute-start.6 = (bf16[16,40,384]{2,1,0:T(8,128)(2,1)S(1)}, bf16[16,40,384]{2,1,0:T(8,128)(2,1)S(1)}, u32[]{:S(2)}, u32[]{:S(2)}) collective-permute-start(bf16[16,40,384]{2,1,0:T(8,128)(2,1)S(1)} %all-to-all-done.own0), channel_id=1, source_target_pairs={{0,2},{2,0},{1,3},{3,1},{4,6},{6,4},{5,7},{7,5},{8,10},{10,8},{9,1... | collective-permute-start | bytes 1474568 | tf_op jit(solution)/shard_map/ppermute | solution.py:659
  25.3 11.0 %collective-permute-start.5 = (bf16[16,40,384]{2,1,0:T(8,128)(2,1)S(1)}, bf16[16,40,384]{2,1,0:T(8,128)(2,1)S(1)}, u32[]{:S(2)}, u32[]{:S(2)}) collective-permute-start(bf16[16,40,384]{2,1,0:T(8,128)(2,1)S(1)} %all-to-all-done.own0), channel_id=1, source_target_pairs={{48,0},{66,2},{112,64},{3,66},{49,1},{67,3},{113,65},{2,67},{52,4}... | collective-permute-start | bytes 1474568 | tf_op jit(solution)/shard_map/ppermute | solution.py:731
  25.4 11.0 %collective-permute-start.4 = (bf16[16,40,384]{2,1,0:T(8,128)(2,1)S(1)}, bf16[16,40,384]{2,1,0:T(8,128)(2,1)S(1)}, u32[]{:S(2)}, u32[]{:S(2)}) collective-permute-start(bf16[16,40,384]{2,1,0:T(8,128)(2,1)S(1)} %all-to-all-done.own0), channel_id=1, source_target_pairs={{4,0},{14,2},{68,64},{78,66},{5,1},{15,3},{69,65},{79,67},{8,4},{2... | collective-permute-start | bytes 1474568 | tf_op jit(solution)/shard_map/ppermute | solution.py:731
  27.6 9.2 %collective-permute-start.3 = (bf16[16,40,384]{2,1,0:T(8,128)(2,1)S(1)}, bf16[16,40,384]{2,1,0:T(8,128)(2,1)S(1)}, u32[]{:S(2)}, u32[]{:S(2)}) collective-permute-start(bf16[16,40,384]{2,1,0:T(8,128)(2,1)S(1)} %all-to-all-done.own0), channel_id=1, source_target_pairs={{16,0},{67,2},{80,64},{2,66},{17,1},{66,3},{81,65},{3,67},{20,4},{... | collective-permute-start | bytes 1474568 | tf_op jit(solution)/shard_map/ppermute | solution.py:731
  32.7 20.8 %all-to-all-start.1 = ((bf16[16,48,384]{2,1,0:T(8,128)(2,1)}), bf16[16,48,384]{2,1,0:T(8,128)(2,1)S(1)}, u32[]{:S(2)}, u32[]{:S(2)}) async-start(bf16[16,48,384]{2,1,0:T(8,128)(2,1)} %get-tuple-element.75), calls=%async_computation.1 | async-start | bytes 1179648 | tf_op jit(solution)/shard_map/all_to_all | solution.py:663
  36.3 1.9 %collective-permute-start.9 = (bf16[16,40,384]{2,1,0:T(8,128)(2,1)S(1)}, bf16[16,40,384]{2,1,0:T(8,128)(2,1)S(1)}, u32[]{:S(2)}, u32[]{:S(2)}) collective-permute-start(bf16[16,40,384]{2,1,0:T(8,128)(2,1)S(1)} %collective-permute-done.5.own3), channel_id=1, source_target_pairs={{0,2},{2,0},{1,3},{3,1},{4,6},{6,4},{5,7},{7,5},{8,10},{10,8},{9,1... | collective-permute-start | bytes 1474568 | tf_op jit(solution)/shard_map/ppermute | solution.py:659
  36.4 3.2 %collective-permute-start.8 = (bf16[16,40,384]{2,1,0:T(8,128)(2,1)S(1)}, bf16[16,40,384]{2,1,0:T(8,128)(2,1)S(1)}, u32[]{:S(2)}, u32[]{:S(2)}) collective-permute-start(bf16[16,40,384]{2,1,0:T(8,128)(2,1)S(1)} %collective-permute-done.4.own2), channel_id=1, source_target_pairs={{0,2},{2,0},{1,3},{3,1},{4,6},{6,4},{5,7},{7,5},{8,10},{10,8},{9,1... | collective-permute-start | bytes 1474568 | tf_op jit(solution)/shard_map/ppermute | solution.py:659
  36.9 3.6 %collective-permute-start.7 = (bf16[16,40,384]{2,1,0:T(8,128)(2,1)S(1)}, bf16[16,40,384]{2,1,0:T(8,128)(2,1)}, u32[]{:S(2)}, u32[]{:S(2)}) collective-permute-start(bf16[16,40,384]{2,1,0:T(8,128)(2,1)S(1)} %collective-permute-done.3.own1), channel_id=1, source_target_pairs={{0,2},{2,0},{1,3},{3,1},{4,6},{6,4},{5,7},{7,5},{8,10},{10,8},{9,1... | collective-permute-start | bytes 1474568 | tf_op jit(solution)/shard_map/ppermute | solution.py:659
  53.5 3.1 %collective-permute-start.10 = (bf16[32,48,384]{2,1,0:T(8,128)(2,1)}, bf16[32,48,384]{2,1,0:T(8,128)(2,1)S(1)}, u32[]{:S(2)}, u32[]{:S(2)}) collective-permute-start(bf16[32,48,384]{2,1,0:T(8,128)(2,1)} %get-tuple-element.77), channel_id=1, source_target_pairs={{0,2},{2,0},{1,3},{3,1},{4,6},{6,4},{5,7},{7,5},{8,10},{10,8},{9,1... | collective-permute-start | bytes 3538952 | tf_op jit(solution)/shard_map/ppermute | solution.py:659
  83.5 16.4 %copy-start.11 = (s32[5]{0:T(128)S(1)}, s32[5]{0:T(128)}, u32[]{:S(2)}) copy-start(s32[5]{0:T(128)} %stack.23.where_ref) | copy-start | bytes 64
  84.5 20.3 %copy-start.2 = (bf16[2,64,768]{2,1,0:T(8,128)(2,1)S(1)}, bf16[2,64,768]{2,1,0:T(8,128)(2,1)}, u32[]{:S(2)}) copy-start(bf16[2,64,768]{2,1,0:T(8,128)(2,1)} %constant.36.clone.places_ref) | copy-start | bytes 589828
  84.5 15.4 %all-to-all-start.3 = ((bf16[16,48,384]{2,1,0:T(8,128)(2,1)}), bf16[16,48,384]{2,1,0:T(8,128)(2,1)S(1)}, u32[]{:S(2)}, u32[]{:S(2)}) async-start(bf16[16,48,384]{2,1,0:T(8,128)(2,1)} %get-tuple-element.78), calls=%async_computation.3 | async-start | bytes 1179648 | tf_op jit(solution)/shard_map/all_to_all | solution.py:663
  88.3 18.8 %collective-permute-start.13 = (bf16[16,48,384]{2,1,0:T(8,128)(2,1)S(1)}, bf16[16,48,384]{2,1,0:T(8,128)(2,1)S(1)}, u32[]{:S(2)}, u32[]{:S(2)}) collective-permute-start(bf16[16,48,384]{2,1,0:T(8,128)(2,1)S(1)} %all-to-all-done.1.old_own_ref), channel_id=1, source_target_pairs={{0,2},{2,0},{1,3},{3,1},{4,6},{6,4},{5,7},{7,5},{8,10},{10,8},{9,1... | collective-permute-start | bytes 1769480 | tf_op jit(solution)/shard_map/ppermute | solution.py:659
  101.4 9.2 %collective-permute-start.12 = (bf16[16,48,384]{2,1,0:T(8,128)(2,1)S(1)}, bf16[16,48,384]{2,1,0:T(8,128)(2,1)S(1)}, u32[]{:S(2)}, u32[]{:S(2)}) collective-permute-start(bf16[16,48,384]{2,1,0:T(8,128)(2,1)S(1)} %all-to-all-done.3.own_ref), channel_id=1, source_target_pairs={{0,2},{2,0},{1,3},{3,1},{4,6},{6,4},{5,7},{7,5},{8,10},{10,8},{9,1... | collective-permute-start | bytes 1769480 | tf_op jit(solution)/shard_map/ppermute | solution.py:659
  101.4 9.2 %all-to-all-start.4 = ((bf16[8,16,384]{2,1,0:T(8,128)(2,1)}), bf16[8,16,384]{2,1,0:T(8,128)(2,1)S(1)}, u32[]{:S(2)}, u32[]{:S(2)}) async-start(bf16[8,16,384]{2,1,0:T(8,128)(2,1)} %tell.1), calls=%async_computation.4 | async-start | bytes 196608 | tf_op jit(solution)/shard_map/all_to_all | solution.py:663
  105.6 16.8 %collective-permute-start.11 = (bf16[64,384]{1,0:T(8,128)(2,1)S(1)}, bf16[64,384]{1,0:T(8,128)(2,1)S(1)}, u32[]{:S(2)}, u32[]{:S(2)}) collective-permute-start(bf16[64,384]{1,0:T(8,128)(2,1)S(1)} %small.1.small_own_ref), channel_id=1, source_target_pairs={{64,0},{65,1},{66,2},{67,3},{68,4},{69,5},{70,6},{71,7},{72,8},{73... | collective-permute-start | bytes 147464 | tf_op jit(solution)/shard_map/ppermute | solution.py:767
  110.6 11.8 %copy-start.4 = (f32[384,12]{0,1:T(8,128)S(1)}, f32[384,12]{0,1:T(8,128)}, u32[]{:S(2)}) copy-start(f32[384,12]{0,1:T(8,128)} %param.28) | copy-start | bytes 55300
  110.6 11.8 %copy-start.5 = (f32[12,384]{1,0:T(8,128)S(1)}, f32[12,384]{1,0:T(8,128)}, u32[]{:S(2)}) copy-start(f32[12,384]{1,0:T(8,128)} %down_m_ref.1) | copy-start | bytes 55300
  110.6 11.8 %copy-start.9 = (f32[50,384]{1,0:T(8,128)S(1)}, f32[50,384]{1,0:T(8,128)}, u32[]{:S(2)}) copy-start(f32[50,384]{1,0:T(8,128)} %pos_m_ref.1) | copy-start | bytes 230404
  110.6 11.8 %copy-start.12 = (f32[4,384]{1,0:T(4,128)S(1)}, f32[4,384]{1,0:T(4,128)}, u32[]{:S(2)}) copy-start(f32[4,384]{1,0:T(4,128)} %norms_ref.3) | copy-start | bytes 18436
  110.7 11.8 %copy-start.14 = (f32[3,384]{1,0:T(4,128)S(1)}, f32[3,384]{1,0:T(4,128)}, u32[]{:S(2)}) copy-start(f32[3,384]{1,0:T(4,128)} %out_m_ref.1) | copy-start | bytes 13828
  110.7 11.8 %copy-start.16 = (f32[4,384]{1,0:T(4,128)S(1)}, f32[4,384]{1,0:T(4,128)}, u32[]{:S(2)}) copy-start(f32[4,384]{1,0:T(4,128)} %norm_m_ref.1) | copy-start | bytes 18436
  110.7 17.2 %copy-start.6 = (f32[384,9]{0,1:T(8,128)S(1)}, f32[384,9]{0,1:T(8,128)}, u32[]{:S(2)}) copy-start(f32[384,9]{0,1:T(8,128)} %param.22) | copy-start | bytes 41476
  110.7 17.2 %copy-start.7 = (f32[384,12]{0,1:T(8,128)S(1)}, f32[384,12]{0,1:T(8,128)}, u32[]{:S(2)}) copy-start(f32[384,12]{0,1:T(8,128)} %param.24) | copy-start | bytes 55300
  110.7 17.2 %copy-start.8 = (f32[12,384]{1,0:T(8,128)S(1)}, f32[12,384]{1,0:T(8,128)}, u32[]{:S(2)}) copy-start(f32[12,384]{1,0:T(8,128)} %down_ref.5) | copy-start | bytes 55300
  110.7 17.2 %copy-start.13 = (f32[3,384]{1,0:T(4,128)S(1)}, f32[3,384]{1,0:T(4,128)}, u32[]{:S(2)}) copy-start(f32[3,384]{1,0:T(4,128)} %out_ref.5) | copy-start | bytes 13828
  119.1 8.8 %all-to-all-start.5 = ((bf16[4,16,384]{2,1,0:T(8,128)(2,1)}), bf16[4,16,384]{2,1,0:T(8,128)(2,1)S(1)}, u32[]{:S(2)}, u32[]{:S(2)}) async-start(bf16[4,16,384]{2,1,0:T(8,128)(2,1)} %orth.1), calls=%async_computation.5 | async-start | bytes 98304 | tf_op jit(solution)/shard_map/all_to_all | solution.py:663
  (11 other events, 48.9 us)

commit v5 on v4

--- a/solution.py
+++ b/solution.py
@@ -109,6 +109,10 @@
     return ((((z % 2) * 4 + x) * 4 + y) * 2 + core) * 2 + z // 2
 
 
+def chip_z():
+    return 2 * lax.axis_index("zh") + lax.axis_index("zl")
+
+
 def devices():
     return [(x, y, z, c) for x in range(4) for y in range(4) for z in range(4) for c in range(2)]
 
@@ -119,7 +123,7 @@
 
 def colour_groups():
     return [
-        [device(x, y, x + 2 * y - colour, core) for x in range(4) for y in range(4)]
+        [device(x, y, x + 2 * y + colour, core) for x in range(4) for y in range(4)]
         for colour in range(4)
         for core in range(2)
     ]
@@ -127,9 +131,9 @@
 
 def colour_step(step):
     sources = {
-        1: ((1, 0, 0), (0, 0, -1)),
+        1: ((-1, 0, 0), (0, 0, 1)),
         2: ((0, 1, 0), (0, -1, 0)),
-        3: ((-1, 0, 0), (0, 0, 1)),
+        3: ((1, 0, 0), (0, 0, -1)),
     }[step]
     return [
         (device(x + sources[c][0], y + sources[c][1], z + sources[c][2], c), device(x, y, z, c))
@@ -201,7 +205,7 @@
 ):
     core = where_ref[0]
     half = where_ref[1]
-    colour = where_ref[4]
+    colour = where_ref[2]
     count = cot_ref.shape[0]
     loads = [
         pltpu.make_async_copy(source, weights_ref.at[k], in_sems.at[k])
@@ -213,10 +217,10 @@
         load.start()
 
     def grouped(s, xy, first):
-        ahead = xy // 4 + 2 * (xy % 4) - colour + 4
+        behind = xy // 4 + 2 * (xy % 4) + colour
         return jnp.concatenate(
             [
-                weights_ref[4 * s + ((ahead - z) & 3), xy].astype(F32)[first : first + BLOCK]
+                weights_ref[4 * s + ((z + 12 - behind) & 3), xy].astype(F32)[first : first + BLOCK]
                 for z in range(4)
             ],
             axis=0,
@@ -445,13 +449,12 @@
     return dot(first, jnp.concatenate([bh, bh], axis=0)) + dot(ah, bl)
 
 
-def call(kernel, name, outs, args, scalars=0, scratch=(), flops=0, moved=0, vmem_bytes=VMEM):
-    smem = pl.BlockSpec(memory_space=pltpu.SMEM)
+def call(kernel, name, outs, args, scratch=(), flops=0, moved=0, vmem_bytes=VMEM):
     vmem = pl.BlockSpec(memory_space=pltpu.VMEM)
     return pl.pallas_call(
         kernel,
         out_shape=tuple(jax.ShapeDtypeStruct(shape, dtype) for shape, dtype in outs),
-        in_specs=[smem] * scalars + [vmem] * (len(args) - scalars),
+        in_specs=[vmem] * len(args),
         out_specs=(vmem,) * len(outs),
         scratch_shapes=scratch,
         compiler_params=pltpu.CompilerParams(vmem_limit_bytes=vmem_bytes),
@@ -468,7 +471,7 @@
     rows_ref[...] = jnp.broadcast_to(rows[None], rows_ref.shape)
 
 
-def moments_kernel(where_ref, qkv_ref, out_ref, up_ref, down_ref, *old_refs):
+def moments_kernel(qkv_ref, out_ref, up_ref, down_ref, *old_refs):
     zeros = jnp.zeros((9, D), F32)
     old = (
         up_ref[...],
@@ -478,17 +481,17 @@
     )
     for z in range(4):
 
-        @pl.when(where_ref[3] == z)
+        @pl.when(chip_z() == z)
         def _(z=z):
             for step, ref in enumerate(old_refs):
                 ref[...] = old[(z - step) % 4].astype(BF)
 
 
-def join_kernel(where_ref, *refs):
+def join_kernel(*refs):
     *sources, joined_ref, sent_ref = refs
     for z in range(4):
 
-        @pl.when(where_ref[3] == z)
+        @pl.when(chip_z() == z)
         def _(z=z):
             joined = jnp.concatenate(
                 [sources[(at - z) % 4][...].astype(F32) for at in range(4)], axis=0
@@ -514,9 +517,9 @@
     return jnp.where(z == 1, (row >= 9).astype(F32), jnp.where(z == 3, (row < 9).astype(F32), 1.0))
 
 
-def tell_kernel(where_ref, own_ref, piece_ref, told_ref):
-    z = where_ref[3]
-    counts_all = (z == 1) & (where_ref[0] == 0)
+def tell_kernel(own_ref, piece_ref, told_ref):
+    z = chip_z()
+    counts_all = (z == 1) & (lax.axis_index("c") == 0)
     valid = jnp.where(counts_all, 1.0, valid_rows(z))
     total = jnp.zeros((GROUP, D), F32)
     for xy in range(16):
@@ -535,8 +538,8 @@
         told_ref[2 * to + 1] = rows
 
 
-def small_kernel(where_ref, own_ref, places_ref, small_ref):
-    small_ref[...] = dot(places_ref[where_ref[1]], own_ref[...].reshape(768, D)).astype(BF)
+def small_kernel(own_ref, places_ref, small_ref):
+    small_ref[...] = dot(places_ref[lax.axis_index("zh")], own_ref[...].reshape(768, D)).astype(BF)
 
 
 def clip(told_ref):
@@ -549,7 +552,6 @@
 
 
 def orth_kernel(
-    where_ref,
     told_ref,
     own_ref,
     oth_ref,
@@ -557,10 +559,10 @@
     old_oth_ref,
     old_ref,
     piece_ref,
-    out_ref,
-    whole_ref,
+    *refs,
 ):
-    valid = valid_rows(where_ref[3])
+    *out_refs, whole_ref = refs
+    valid = valid_rows(chip_z())
     factor = clip(told_ref)[1]
     scaled = factor * valid
     for s, (grad_ref, before_ref) in enumerate(((own_ref, old_own_ref), (oth_ref, old_oth_ref))):
@@ -591,9 +593,12 @@
     poly = COEF_A * eye + COEF_B * gram + COEF_C * dot(low, low)
     mine = dot(mine.astype(BF), poly.astype(BF))
     for z in range(4):
-        out_ref[z] = jnp.concatenate(
-            [mine[z * BLOCK : (z + 1) * BLOCK], jnp.zeros((4, D), F32)], axis=0
-        ).astype(BF)
+
+        @pl.when(chip_z() == z)
+        def _(z=z):
+            for step, ref in enumerate(out_refs):
+                to = (z - step) % 4
+                ref[...] = mine[to * BLOCK : (to + 1) * BLOCK].astype(BF)
 
 
 def step_rate(rows_count, cols_count):
@@ -601,7 +606,6 @@
 
 
 def moment_kernel(
-    where_ref,
     told_ref,
     small_own_ref,
     small_near_ref,
@@ -631,9 +635,9 @@
         (0, 0, 12, up_m_ref, up_m_next),
         (2, 0, 12, down_m_ref, down_m_next),
     ):
-        grad = told_ref[2 * z + where_ref[0]].astype(F32)[first:last]
+        grad = told_ref[2 * z + lax.axis_index("c")].astype(F32)[first:last]
         m_next[...] = MOMENTUM * m_ref[...] + factor * grad
-    near = (where_ref[3] % 2 == 0).astype(F32)
+    near = (lax.axis_index("zl") == 0).astype(F32)
     small = near * small_near_ref[...].astype(F32) + (1.0 - near) * small_own_ref[...].astype(F32)
     norm_fresh = MOMENTUM * norm_m_ref[...] + factor * small[50:54]
     norm_m_next[...] = norm_fresh
@@ -644,15 +648,31 @@
 
 
 def update_kernel(
-    back_ref, qkv_ref, out_ref, up_ref, down_ref, qkv_next, out_next, up_next, down_next
+    orth0,
+    orth1,
+    orth2,
+    orth3,
+    qkv_ref,
+    out_ref,
+    up_ref,
+    down_ref,
+    qkv_next,
+    out_next,
+    up_next,
+    down_next,
 ):
+    here = chip_z()
+    sources = [ref[...].astype(F32) for ref in (orth0, orth1, orth2, orth3)]
     for z, first, last, rate, w_ref, w_next in (
         (3, 0, 9, step_rate(D, 3 * D), qkv_ref, qkv_next),
         (1, 9, 12, step_rate(D, D), out_ref, out_next),
         (0, 0, 12, step_rate(D, FF), up_ref, up_next),
         (2, 0, 12, step_rate(FF, D), down_ref, down_next),
     ):
-        w_next[...] = w_ref[...] - rate * back_ref[z].astype(F32)[first:last]
+        orth = sources[z]
+        for step in range(1, 4):
+            orth = jnp.where(here == step, sources[(z - step) % 4], orth)
+        w_next[...] = w_ref[...] - rate * orth[first:last]
 
 
 def swapped(value):
@@ -687,11 +707,6 @@
     offsets,
     pos_index,
 ):
-    z = lax.axis_index(COLUMN)
-    colour = (lax.axis_index("x") + 2 * lax.axis_index("y") - z) % 4
-    where = jnp.stack(
-        [lax.axis_index("c"), lax.axis_index("zh"), lax.axis_index(PLANE), z, colour]
-    ).astype(jnp.int32)
     weights = (qkv_weight.T, out_weight, up_weight.T, down_weight)
     moments = (qkv_moment.T, out_moment, up_moment.T, down_moment)
 
@@ -702,9 +717,7 @@
         moments_kernel,
         "moments",
         (((BLOCK, D), BF),) * 4,
-        (where, *moments),
-        scalars=1,
-        vmem_bytes=ALL_VMEM,
+        moments,
     )
     old = [old[0]] + [lax.ppermute(old[k], AXES, column_step(k)) for k in (1, 2, 3)]
     pos = pos_index.reshape(1, -1)
@@ -725,14 +738,15 @@
         join_kernel,
         "join",
         (((GROUP, D), BF), ((16, GROUP, D), BF)),
-        (where, *old),
-        scalars=1,
+        old,
     )
     own += [lax.ppermute(own[0], AXES, colour_step(step)) for step in (1, 2, 3)]
     other = [swapped(value) for value in own]
     old_sent, other[0] = lax.optimization_barrier((old_sent, other[0]))
     old_own = exchanged(old_sent, PLANE)
 
+    colour = (chip_z() + 12 - lax.axis_index("x") - 2 * lax.axis_index("y")) & 3
+    where = jnp.stack([lax.axis_index("c"), lax.axis_index("zh"), colour]).astype(jnp.int32)
     result, in_grad, keep, send = run_layer(
         where,
         res_ids,
@@ -752,7 +766,7 @@
     )
     grads = exchanged(sent, PLANE)
     (told,) = call(
-        tell_kernel, "tell", (((8, 16, D), BF),), (where, grads, piece), scalars=1
+        tell_kernel, "tell", (((8, 16, D), BF),), (grads, piece)
     )
     told, grads_sent = lax.optimization_barrier((told, grads))
     told = exchanged(told, COLUMN_CORES)
@@ -761,21 +775,19 @@
         small_kernel,
         "small",
         (((64, D), BF),),
-        (where, grads_sent, jnp.asarray(small_places(), BF)),
-        scalars=1,
+        (grads_sent, jnp.asarray(small_places(), BF)),
     )
     small_near = lax.ppermute(small, "zl", [(1, 0)])
-    (orth,) = call(
+    orth = call(
         orth_kernel,
         "orth",
-        (((4, 16, D), BF),),
-        (where, told, grads, grads_other, old_own, old_other, old, piece),
-        scalars=1,
+        (((BLOCK, D), BF),) * 4,
+        (told, grads, grads_other, old_own, old_other, old, piece),
         scratch=[pltpu.VMEM((1536, D), BF)],
         flops=8_000_000_000,
         moved=4_000_000,
     )
-    back = exchanged(orth, COLUMN)
+    back = [orth[0]] + [lax.ppermute(orth[k], AXES, column_step(k)) for k in (1, 2, 3)]
     like = lambda a: (a.shape, F32)
     grad_norm, *fresh = call(
         moment_kernel,
@@ -788,10 +800,11 @@
             like(pos_moment),
             like(pos_table),
         ),
-        (where, told, small, small_near, *moments, norm_params, norm_moment, pos_table, pos_moment),
-        scalars=1,
-    )
-    news = call(update_kernel, "update", [like(a) for a in weights], (back, *weights))
+        (told, small, small_near, *moments, norm_params, norm_moment, pos_table, pos_moment),
+    )
+    news = call(
+        update_kernel, "update", [like(a) for a in weights], (*back, *weights)
+    )
     return (
         result,
         in_grad,

time: 130 us -> 124 us (0.954)
  Pallas kernels: 33.3 us -> 28.6 us
  waiting for transfers between devices: 28.5 us -> 32 us
  local copies, waits for them, and re-layouts: 4.14 us -> 1.35 us
  blocking collectives: 26.6 us -> 25.3 us
    pallas_call x11, Pallas kernels: 20.3 us -> 15.6 us  [call(): pl.pallas_call(kernel, out_shape=tuple((jax.ShapeDtypeStruct(shape, dtype...]
    ppermute x0 -> x3, waiting for transfers between devices: none -> 4.08 us  [shards(): lax.ppermute(orth[k], AXES, column_step(k))]
    all_to_all x4 -> x3, waiting for transfers between devices: 19.2 us -> 15.6 us  [exchanged(): return lax.all_to_all(value, axes, 0, 0, tiled=True)]
    ppermute x0 -> x3, starting transfers between devices: none -> 2.73 us  [shards(): lax.ppermute(orth[k], AXES, column_step(k))]
    ppermute x3, starting transfers between devices: 4.54 us -> 2.04 us  [shards(): own += [lax.ppermute(own[0], AXES, colour_step(step)) for step in (1, 2, 3)]]
    ppermute x3, waiting for transfers between devices: 0.01 us -> 2.31 us  [shards(): own += [lax.ppermute(own[0], AXES, colour_step(step)) for step in (1, 2, 3)]]
    unnamed x48 -> x38, local copies, waits for them, and re-layouts: 3.54 us -> 1.35 us
    all_to_all x1, waiting for transfers between devices: 1.75 us -> 3.84 us  [shards(): lax.all_to_all(rows, AXES, 0, 0, axis_index_groups=colour_groups(), tiled...]
  transfers between devices with their start and end apart: 19 -> 21, of which waited for: 9 -> 13; matrix products, arithmetic and copies ran while one was open for 0% -> 1% of each run, Pallas kernels for 23% -> 21%
where the time goes in v5:
time: 124 us; the launch traced here: 123 us
  starting transfers between devices  34 us (27%)
  waiting for transfers between devices  32 us (26%)
  Pallas kernels  28.6 us (23%)
  blocking collectives  25.3 us (20%)
  local copies, waits for them, and re-layouts  1.35 us (1%)
    all_to_all x1, blocking collectives, exchanged(): return lax.all_to_all(value, axes, 0, 0, tiled=True)  25.3 us
    pallas_call x11, Pallas kernels, call(): pl.pallas_call(kernel, out_shape=tuple((jax.ShapeDtypeStruct(shape, dtype...  15.6 us
    all_to_all x3, waiting for transfers between devices, exchanged(): return lax.all_to_all(value, axes, 0, 0, tiled=True)  15.6 us
    all_to_all x3, starting transfers between devices, exchanged(): return lax.all_to_all(value, axes, 0, 0, tiled=True)  13.1 us
    pallas_call x1, Pallas kernels, run_layer(): pl.pallas_call(layer_kernel, out_shape=(jax.ShapeDtypeStruct((count, D),...  13 us
    all_to_all x1, starting transfers between devices, shards(): lax.all_to_all(rows, AXES, 0, 0, axis_index_groups=colour_groups(), tiled...  10.4 us
    ppermute x3, waiting for transfers between devices, shards(): lax.ppermute(orth[k], AXES, column_step(k))  4.08 us
    all_to_all x1, waiting for transfers between devices, shards(): lax.all_to_all(rows, AXES, 0, 0, axis_index_groups=colour_groups(), tiled...  3.84 us
  transfers between devices with their start and end apart: 21, of which 13 were waited for; matrix products, arithmetic and copies ran while one was open for 1% of the time, Pallas kernels for 21%

profile of v5, /device:TPU:0, one launch (start us, length us, event | category | flops | bytes accessed | tf_op | source)
XLA Modules:
  0.0 123.2 jit_solution(14117697385646855818)
XLA Ops:
  0.7 1.7 %weights.1 = bf16[16,40,384]{2,1,0:T(8,128)(2,1)} custom-call(f32[9,384]{1,0:T(8,128)} %bitcast.17, f32[3,384]{1,0:T(4,128)} %out_ref.5, f32[12,384]{1,0:T(8,128)} %bitcast.19, f32[12,384]{1,0:T(8,128)} %down_ref.5), custom_call_target="tpu_custom_call" | custom-call | tf_op jit(solution)/shard_map/weights/pallas_call | solution.py:454
  2.3 10.4 %all-to-all-start = ((bf16[16,40,384]{2,1,0:T(8,128)(2,1)}), bf16[16,40,384]{2,1,0:T(8,128)(2,1)S(1)}, u32[]{:S(2)}, u32[]{:S(2)}) async-start(bf16[16,40,384]{2,1,0:T(8,128)(2,1)} %weights.1), calls=%async_computation | async-start | bytes 983040 | tf_op jit(solution)/shard_map/all_to_all | solution.py:733
  12.9 0.8 collective-permute-start
  13.6 2.4 %collective-permute-start.1 = (bf16[12,384]{1,0:T(8,128)(2,1)S(1)}, bf16[12,384]{1,0:T(8,128)(2,1)S(1)}, u32[]{:S(2)}, u32[]{:S(2)}) collective-permute-start(bf16[12,384]{1,0:T(8,128)(2,1)S(1)} %get-tuple-element.64), channel_id=1, source_target_pairs={{1,0},{3,2},{65,64},{67,66},{0,1},{2,3},{64,65},{66,67},{5,4},{7,6... | collective-permute-start | bytes 27656 | tf_op jit(solution)/shard_map/ppermute | solution.py:722
  16.0 2.2 %embed.1 = (f32[256,384]{1,0:T(8,128)}, bf16[256,384]{1,0:T(8,128)(2,1)}) custom-call(bf16[256,384]{1,0:T(8,128)(2,1)} %tok_ref.1, bf16[256,384]{1,0:T(8,128)(2,1)} %cot_ref.1, f32[50,384]{1,0:T(8,128)} %table_ref.3, s32[1,256]{1,0:T(1,128)} %bitcast.21), custom_call_target="tpu_custom_call" | custom-call | tf_op jit(solution)/shard_map/embed/pallas_call | solution.py:454
  18.2 3.1 %collective-permute-done.1.refs_2_ = bf16[12,384]{1,0:T(8,128)(2,1)S(1)} collective-permute-done((bf16[12,384]{1,0:T(8,128)(2,1)S(1)}, bf16[12,384]{1,0:T(8,128)(2,1)S(1)}, u32[]{:S(2)}, u32[]{:S(2)}) %collective-permute-start.1) | collective-permute-done | bytes 9248 | tf_op jit(solution)/shard_map/ppermute | solution.py:722
  21.5 3.8 %all-to-all-done.own0 = bf16[16,40,384]{2,1,0:T(8,128)(2,1)S(1)} async-done(((bf16[16,40,384]{2,1,0:T(8,128)(2,1)}), bf16[16,40,384]{2,1,0:T(8,128)(2,1)S(1)}, u32[]{:S(2)}, u32[]{:S(2)}) %all-to-all-start) | async-done | bytes 491552 | tf_op jit(solution)/shard_map/all_to_all | solution.py:733
  25.4 2.0 %collective-permute-start.5 = (bf16[16,40,384]{2,1,0:T(8,128)(2,1)S(1)}, bf16[16,40,384]{2,1,0:T(8,128)(2,1)S(1)}, u32[]{:S(2)}, u32[]{:S(2)}) collective-permute-start(bf16[16,40,384]{2,1,0:T(8,128)(2,1)S(1)} %all-to-all-done.own0), channel_id=1, source_target_pairs={{16,0},{67,2},{80,64},{2,66},{17,1},{66,3},{81,65},{3,67},{20,4},{... | collective-permute-start | bytes 1474568 | tf_op jit(solution)/shard_map/ppermute | solution.py:743
  27.4 0.9 join.1
  28.3 6.0 %all-to-all-start.1 = ((bf16[16,48,384]{2,1,0:T(8,128)(2,1)}), bf16[16,48,384]{2,1,0:T(8,128)(2,1)S(1)}, u32[]{:S(2)}, u32[]{:S(2)}) async-start(bf16[16,48,384]{2,1,0:T(8,128)(2,1)} %get-tuple-element.79), calls=%async_computation.1 | async-start | bytes 1179648 | tf_op jit(solution)/shard_map/all_to_all | solution.py:683
  34.3 0.7 collective-permute-start.9
  35.1 1.1 collective-permute-done.4.own2
  36.2 1.2 collective-permute-done.3.own1
  37.4 0.7 pad_add_fusion.where_ref
  38.2 1.2 collective-permute-done.7.oth1
  39.4 13.0 %layer.1 = (bf16[256,384]{1,0:T(8,128)(2,1)}, f32[256,384]{1,0:T(8,128)}, bf16[32,48,384]{2,1,0:T(8,128)(2,1)}, bf16[32,48,384]{2,1,0:T(8,128)(2,1)}) custom-call(s32[3]{0:T(128)} %pad_add_fusion.where_ref, s32[5]{0:T(128)} %res_ref.1, s32[5]{0:T(128)} %off_ref.1, f32[4,384]{1,0:T(4,128)} %norms_ref.3, s32[1,256]{1,0:T(1,128)} %bitcast.22, ...), custom_call_target="tpu_custom_call" | custom-call | tf_op jit(solution)/shard_map/layer/pallas_call | solution.py:402
  52.7 1.3 %copy-done = bf16[32,48,384]{2,1,0:T(8,128)(2,1)S(1)} copy-done((bf16[32,48,384]{2,1,0:T(8,128)(2,1)S(1)}, bf16[32,48,384]{2,1,0:T(8,128)(2,1)}, u32[]{:S(2)}) %copy-start) | copy-done | bytes 1179672
  54.0 1.5 %collective-permute-done.10 = bf16[32,48,384]{2,1,0:T(8,128)(2,1)S(1)} collective-permute-done((bf16[32,48,384]{2,1,0:T(8,128)(2,1)}, bf16[32,48,384]{2,1,0:T(8,128)(2,1)S(1)}, u32[]{:S(2)}, u32[]{:S(2)}) %collective-permute-start.10) | collective-permute-done | bytes 1179680 | tf_op jit(solution)/shard_map/ppermute | solution.py:679
  55.9 25.3 %all_to_all.25.parts_ref = bf16[32,48,384]{2,1,0:T(8,128)(2,1)S(1)} all-to-all(bf16[32,48,384]{2,1,0:T(8,128)(2,1)S(1)} %add_convert_fusion), channel_id=1, replica_groups=mesh['zl'=2,'x'=4,'y'=4,'c'=2,'zh'=2] {'zl','x','y'}, dimensions={0} | all-to-all | bytes 2359296 | tf_op jit(solution)/shard_map/all_to_all | solution.py:683
  81.2 1.0 sum.1
  82.2 3.7 %all-to-all-start.3 = ((bf16[16,48,384]{2,1,0:T(8,128)(2,1)}), bf16[16,48,384]{2,1,0:T(8,128)(2,1)S(1)}, u32[]{:S(2)}, u32[]{:S(2)}) async-start(bf16[16,48,384]{2,1,0:T(8,128)(2,1)} %get-tuple-element.82), calls=%async_computation.3 | async-start | bytes 1179648 | tf_op jit(solution)/shard_map/all_to_all | solution.py:683
  86.0 11.6 %all-to-all-done.3.own_ref = bf16[16,48,384]{2,1,0:T(8,128)(2,1)S(1)} async-done(((bf16[16,48,384]{2,1,0:T(8,128)(2,1)}), bf16[16,48,384]{2,1,0:T(8,128)(2,1)S(1)}, u32[]{:S(2)}, u32[]{:S(2)}) %all-to-all-start.3) | async-done | bytes 589856 | tf_op jit(solution)/shard_map/all_to_all | solution.py:683
  97.6 0.9 tell.1
  98.5 3.4 %all-to-all-start.4 = ((bf16[8,16,384]{2,1,0:T(8,128)(2,1)}), bf16[8,16,384]{2,1,0:T(8,128)(2,1)S(1)}, u32[]{:S(2)}, u32[]{:S(2)}) async-start(bf16[8,16,384]{2,1,0:T(8,128)(2,1)} %tell.1), calls=%async_computation.4 | async-start | bytes 196608 | tf_op jit(solution)/shard_map/all_to_all | solution.py:683
  102.1 1.5 %collective-permute-start.11 = (bf16[64,384]{1,0:T(8,128)(2,1)S(1)}, bf16[64,384]{1,0:T(8,128)(2,1)S(1)}, u32[]{:S(2)}, u32[]{:S(2)}) collective-permute-start(bf16[64,384]{1,0:T(8,128)(2,1)S(1)} %small.1.small_own_ref), channel_id=1, source_target_pairs={{64,0},{65,1},{66,2},{67,3},{68,4},{69,5},{70,6},{71,7},{72,8},{73... | collective-permute-start | bytes 147464 | tf_op jit(solution)/shard_map/ppermute | solution.py:780
  103.6 3.9 %all-to-all-done.4.told_ref = bf16[8,16,384]{2,1,0:T(8,128)(2,1)S(1)} async-done(((bf16[8,16,384]{2,1,0:T(8,128)(2,1)}), bf16[8,16,384]{2,1,0:T(8,128)(2,1)S(1)}, u32[]{:S(2)}, u32[]{:S(2)}) %all-to-all-start.4) | async-done | bytes 98336 | tf_op jit(solution)/shard_map/all_to_all | solution.py:683
  107.7 7.3 %orth.1 = (bf16[12,384]{1,0:T(8,128)(2,1)S(1)}, bf16[12,384]{1,0:T(8,128)(2,1)S(1)}, bf16[12,384]{1,0:T(8,128)(2,1)S(1)}, bf16[12,384]{1,0:T(8,128)(2,1)S(1)}) custom-call(bf16[8,16,384]{2,1,0:T(8,128)(2,1)S(1)} %all-to-all-done.4.told_ref, bf16[16,48,384]{2,1,0:T(8,128)(2,1)S(1)} %all-to-all-done.3.own_ref, ...), custom_call_target="tpu_custom_call" | custom-call | flops 8000000000 | bytes 4000000 | tf_op jit(solution)/shard_map/orth/pallas_call | solution.py:454
  114.9 1.2 collective-permute-start.14
  116.1 1.5 %collective-permute-start.15 = (bf16[12,384]{1,0:T(8,128)(2,1)S(1)}, bf16[12,384]{1,0:T(8,128)(2,1)S(1)}, u32[]{:S(2)}, u32[]{:S(2)}) collective-permute-start(bf16[12,384]{1,0:T(8,128)(2,1)S(1)} %get-tuple-element.92), channel_id=1, source_target_pairs={{1,0},{3,2},{65,64},{67,66},{0,1},{2,3},{64,65},{66,67},{5,4},{7,6... | collective-permute-start | bytes 27656 | tf_op jit(solution)/shard_map/ppermute | solution.py:790
  117.7 0.8 moment.1
  118.7 2.7 %collective-permute-done.15.orth2 = bf16[12,384]{1,0:T(8,128)(2,1)S(1)} collective-permute-done((bf16[12,384]{1,0:T(8,128)(2,1)S(1)}, bf16[12,384]{1,0:T(8,128)(2,1)S(1)}, u32[]{:S(2)}, u32[]{:S(2)}) %collective-permute-start.15) | collective-permute-done | bytes 9248 | tf_op jit(solution)/shard_map/ppermute | solution.py:790
  121.3 1.2 collective-permute-done.16.orth3
  (63 shorter events, 2.3 us)
Async XLA Ops:
  0.6 12.1 %copy-start.5 = (f32[12,384]{1,0:T(8,128)S(1)}, f32[12,384]{1,0:T(8,128)}, u32[]{:S(2)}) copy-start(f32[12,384]{1,0:T(8,128)} %down_m_ref.1) | copy-start | bytes 55300
  0.7 12.1 %copy-start.12 = (f32[3,384]{1,0:T(4,128)S(1)}, f32[3,384]{1,0:T(4,128)}, u32[]{:S(2)}) copy-start(f32[3,384]{1,0:T(4,128)} %out_m_ref.1) | copy-start | bytes 13828
  0.7 12.1 %copy-start.4 = (f32[384,12]{0,1:T(8,128)S(1)}, f32[384,12]{0,1:T(8,128)}, u32[]{:S(2)}) copy-start(f32[384,12]{0,1:T(8,128)} %param.28) | copy-start | bytes 55300
  0.7 12.1 %copy-start.3 = (f32[384,9]{0,1:T(8,128)S(1)}, f32[384,9]{0,1:T(8,128)}, u32[]{:S(2)}) copy-start(f32[384,9]{0,1:T(8,128)} %param.26) | copy-start | bytes 41476
  2.3 23.0 %all-to-all-start = ((bf16[16,40,384]{2,1,0:T(8,128)(2,1)}), bf16[16,40,384]{2,1,0:T(8,128)(2,1)S(1)}, u32[]{:S(2)}, u32[]{:S(2)}) async-start(bf16[16,40,384]{2,1,0:T(8,128)(2,1)} %weights.1), calls=%async_computation | async-start | bytes 983040 | tf_op jit(solution)/shard_map/all_to_all | solution.py:733
  12.9 5.4 %collective-permute-start = (bf16[12,384]{1,0:T(8,128)(2,1)S(1)}, bf16[12,384]{1,0:T(8,128)(2,1)S(1)}, u32[]{:S(2)}, u32[]{:S(2)}) collective-permute-start(bf16[12,384]{1,0:T(8,128)(2,1)S(1)} %get-tuple-element.63), channel_id=1, source_target_pairs={{64,0},{66,2},{1,64},{3,66},{65,1},{67,3},{0,65},{2,67},{68,4},{70... | collective-permute-start | bytes 27656 | tf_op jit(solution)/shard_map/ppermute | solution.py:722
  13.6 7.7 %collective-permute-start.1 = (bf16[12,384]{1,0:T(8,128)(2,1)S(1)}, bf16[12,384]{1,0:T(8,128)(2,1)S(1)}, u32[]{:S(2)}, u32[]{:S(2)}) collective-permute-start(bf16[12,384]{1,0:T(8,128)(2,1)S(1)} %get-tuple-element.64), channel_id=1, source_target_pairs={{1,0},{3,2},{65,64},{67,66},{0,1},{2,3},{64,65},{66,67},{5,4},{7,6... | collective-permute-start | bytes 27656 | tf_op jit(solution)/shard_map/ppermute | solution.py:722
  16.0 5.5 %collective-permute-start.2 = (bf16[12,384]{1,0:T(8,128)(2,1)S(1)}, bf16[12,384]{1,0:T(8,128)(2,1)S(1)}, u32[]{:S(2)}, u32[]{:S(2)}) collective-permute-start(bf16[12,384]{1,0:T(8,128)(2,1)S(1)} %get-tuple-element.65), channel_id=1, source_target_pairs={{65,0},{67,2},{0,64},{2,66},{64,1},{66,3},{1,65},{3,67},{69,4},{71... | collective-permute-start | bytes 27656 | tf_op jit(solution)/shard_map/ppermute | solution.py:722
  25.4 14.0 %copy-start.14 = (bf16[16,40,384]{2,1,0:T(8,128)(2,1)}, bf16[16,40,384]{2,1,0:T(8,128)(2,1)S(1)}, u32[]{:S(2)}) copy-start(bf16[16,40,384]{2,1,0:T(8,128)(2,1)S(1)} %all-to-all-done.own0) | copy-start | bytes 1474564
  25.4 2.9 %collective-permute-start.6 = (bf16[16,40,384]{2,1,0:T(8,128)(2,1)S(1)}, bf16[16,40,384]{2,1,0:T(8,128)(2,1)S(1)}, u32[]{:S(2)}, u32[]{:S(2)}) collective-permute-start(bf16[16,40,384]{2,1,0:T(8,128)(2,1)S(1)} %all-to-all-done.own0), channel_id=1, source_target_pairs={{0,2},{2,0},{1,3},{3,1},{4,6},{6,4},{5,7},{7,5},{8,10},{10,8},{9,1... | collective-permute-start | bytes 1474568 | tf_op jit(solution)/shard_map/ppermute | solution.py:679
  25.4 8.9 %collective-permute-start.5 = (bf16[16,40,384]{2,1,0:T(8,128)(2,1)S(1)}, bf16[16,40,384]{2,1,0:T(8,128)(2,1)S(1)}, u32[]{:S(2)}, u32[]{:S(2)}) collective-permute-start(bf16[16,40,384]{2,1,0:T(8,128)(2,1)S(1)} %all-to-all-done.own0), channel_id=1, source_target_pairs={{16,0},{67,2},{80,64},{2,66},{17,1},{66,3},{81,65},{3,67},{20,4},{... | collective-permute-start | bytes 1474568 | tf_op jit(solution)/shard_map/ppermute | solution.py:743
  27.3 8.8 %collective-permute-start.4 = (bf16[16,40,384]{2,1,0:T(8,128)(2,1)S(1)}, bf16[16,40,384]{2,1,0:T(8,128)(2,1)S(1)}, u32[]{:S(2)}, u32[]{:S(2)}) collective-permute-start(bf16[16,40,384]{2,1,0:T(8,128)(2,1)S(1)} %all-to-all-done.own0), channel_id=1, source_target_pairs={{4,0},{14,2},{68,64},{78,66},{5,1},{15,3},{69,65},{79,67},{8,4},{2... | collective-permute-start | bytes 1474568 | tf_op jit(solution)/shard_map/ppermute | solution.py:743
  27.3 10.0 %collective-permute-start.3 = (bf16[16,40,384]{2,1,0:T(8,128)(2,1)S(1)}, bf16[16,40,384]{2,1,0:T(8,128)(2,1)S(1)}, u32[]{:S(2)}, u32[]{:S(2)}) collective-permute-start(bf16[16,40,384]{2,1,0:T(8,128)(2,1)S(1)} %all-to-all-done.own0), channel_id=1, source_target_pairs={{48,0},{66,2},{112,64},{3,66},{49,1},{67,3},{113,65},{2,67},{52,4}... | collective-permute-start | bytes 1474568 | tf_op jit(solution)/shard_map/ppermute | solution.py:743
  28.3 11.1 %copy-start.15 = (bf16[16,40,384]{2,1,0:T(8,128)(2,1)}, bf16[16,40,384]{2,1,0:T(8,128)(2,1)S(1)}, u32[]{:S(2)}) copy-start(bf16[16,40,384]{2,1,0:T(8,128)(2,1)S(1)} %collective-permute-done.6.oth0) | copy-start | bytes 1474564
  28.3 24.1 %all-to-all-start.1 = ((bf16[16,48,384]{2,1,0:T(8,128)(2,1)}), bf16[16,48,384]{2,1,0:T(8,128)(2,1)S(1)}, u32[]{:S(2)}, u32[]{:S(2)}) async-start(bf16[16,48,384]{2,1,0:T(8,128)(2,1)} %get-tuple-element.79), calls=%async_computation.1 | async-start | bytes 1179648 | tf_op jit(solution)/shard_map/all_to_all | solution.py:683
  34.3 3.7 %collective-permute-start.9 = (bf16[16,40,384]{2,1,0:T(8,128)(2,1)S(1)}, bf16[16,40,384]{2,1,0:T(8,128)(2,1)}, u32[]{:S(2)}, u32[]{:S(2)}) collective-permute-start(bf16[16,40,384]{2,1,0:T(8,128)(2,1)S(1)} %collective-permute-done.5.own3), channel_id=1, source_target_pairs={{0,2},{2,0},{1,3},{3,1},{4,6},{6,4},{5,7},{7,5},{8,10},{10,8},{9,1... | collective-permute-start | bytes 1474568 | tf_op jit(solution)/shard_map/ppermute | solution.py:679
  36.2 2.0 %collective-permute-start.8 = (bf16[16,40,384]{2,1,0:T(8,128)(2,1)S(1)}, bf16[16,40,384]{2,1,0:T(8,128)(2,1)}, u32[]{:S(2)}, u32[]{:S(2)}) collective-permute-start(bf16[16,40,384]{2,1,0:T(8,128)(2,1)S(1)} %collective-permute-done.4.own2), channel_id=1, source_target_pairs={{0,2},{2,0},{1,3},{3,1},{4,6},{6,4},{5,7},{7,5},{8,10},{10,8},{9,1... | collective-permute-start | bytes 1474568 | tf_op jit(solution)/shard_map/ppermute | solution.py:679
  37.4 2.0 %collective-permute-start.7 = (bf16[16,40,384]{2,1,0:T(8,128)(2,1)S(1)}, bf16[16,40,384]{2,1,0:T(8,128)(2,1)}, u32[]{:S(2)}, u32[]{:S(2)}) collective-permute-start(bf16[16,40,384]{2,1,0:T(8,128)(2,1)S(1)} %collective-permute-done.3.own1), channel_id=1, source_target_pairs={{0,2},{2,0},{1,3},{3,1},{4,6},{6,4},{5,7},{7,5},{8,10},{10,8},{9,1... | collective-permute-start | bytes 1474568 | tf_op jit(solution)/shard_map/ppermute | solution.py:679
  52.4 3.1 %collective-permute-start.10 = (bf16[32,48,384]{2,1,0:T(8,128)(2,1)}, bf16[32,48,384]{2,1,0:T(8,128)(2,1)S(1)}, u32[]{:S(2)}, u32[]{:S(2)}) collective-permute-start(bf16[32,48,384]{2,1,0:T(8,128)(2,1)} %get-tuple-element.81), channel_id=1, source_target_pairs={{0,2},{2,0},{1,3},{3,1},{4,6},{6,4},{5,7},{7,5},{8,10},{10,8},{9,1... | collective-permute-start | bytes 3538952 | tf_op jit(solution)/shard_map/ppermute | solution.py:679
  82.2 19.7 %copy-start.2 = (bf16[2,64,768]{2,1,0:T(8,128)(2,1)S(1)}, bf16[2,64,768]{2,1,0:T(8,128)(2,1)}, u32[]{:S(2)}) copy-start(bf16[2,64,768]{2,1,0:T(8,128)(2,1)} %constant.27.clone.places_ref) | copy-start | bytes 589828
  82.2 15.4 %all-to-all-start.3 = ((bf16[16,48,384]{2,1,0:T(8,128)(2,1)}), bf16[16,48,384]{2,1,0:T(8,128)(2,1)S(1)}, u32[]{:S(2)}, u32[]{:S(2)}) async-start(bf16[16,48,384]{2,1,0:T(8,128)(2,1)} %get-tuple-element.82), calls=%async_computation.3 | async-start | bytes 1179648 | tf_op jit(solution)/shard_map/all_to_all | solution.py:683
  85.9 17.7 %collective-permute-start.13 = (bf16[16,48,384]{2,1,0:T(8,128)(2,1)S(1)}, bf16[16,48,384]{2,1,0:T(8,128)(2,1)S(1)}, u32[]{:S(2)}, u32[]{:S(2)}) collective-permute-start(bf16[16,48,384]{2,1,0:T(8,128)(2,1)S(1)} %all-to-all-done.1.old_own_ref), channel_id=1, source_target_pairs={{0,2},{2,0},{1,3},{3,1},{4,6},{6,4},{5,7},{7,5},{8,10},{10,8},{9,1... | collective-permute-start | bytes 1769480 | tf_op jit(solution)/shard_map/ppermute | solution.py:679
  98.5 9.1 %collective-permute-start.12 = (bf16[16,48,384]{2,1,0:T(8,128)(2,1)S(1)}, bf16[16,48,384]{2,1,0:T(8,128)(2,1)S(1)}, u32[]{:S(2)}, u32[]{:S(2)}) collective-permute-start(bf16[16,48,384]{2,1,0:T(8,128)(2,1)S(1)} %all-to-all-done.3.own_ref), channel_id=1, source_target_pairs={{0,2},{2,0},{1,3},{3,1},{4,6},{6,4},{5,7},{7,5},{8,10},{10,8},{9,1... | collective-permute-start | bytes 1769480 | tf_op jit(solution)/shard_map/ppermute | solution.py:679
  98.5 9.1 %all-to-all-start.4 = ((bf16[8,16,384]{2,1,0:T(8,128)(2,1)}), bf16[8,16,384]{2,1,0:T(8,128)(2,1)S(1)}, u32[]{:S(2)}, u32[]{:S(2)}) async-start(bf16[8,16,384]{2,1,0:T(8,128)(2,1)} %tell.1), calls=%async_computation.4 | async-start | bytes 196608 | tf_op jit(solution)/shard_map/all_to_all | solution.py:683
  102.1 15.6 %collective-permute-start.11 = (bf16[64,384]{1,0:T(8,128)(2,1)S(1)}, bf16[64,384]{1,0:T(8,128)(2,1)S(1)}, u32[]{:S(2)}, u32[]{:S(2)}) collective-permute-start(bf16[64,384]{1,0:T(8,128)(2,1)S(1)} %small.1.small_own_ref), channel_id=1, source_target_pairs={{64,0},{65,1},{66,2},{67,3},{68,4},{69,5},{70,6},{71,7},{72,8},{73... | collective-permute-start | bytes 147464 | tf_op jit(solution)/shard_map/ppermute | solution.py:780
  107.6 15.0 %copy-start.6 = (f32[384,9]{0,1:T(8,128)S(1)}, f32[384,9]{0,1:T(8,128)}, u32[]{:S(2)}) copy-start(f32[384,9]{0,1:T(8,128)} %param.22) | copy-start | bytes 41476
  107.6 14.9 %copy-start.7 = (f32[384,12]{0,1:T(8,128)S(1)}, f32[384,12]{0,1:T(8,128)}, u32[]{:S(2)}) copy-start(f32[384,12]{0,1:T(8,128)} %param.24) | copy-start | bytes 55300
  107.6 14.9 %copy-start.8 = (f32[12,384]{1,0:T(8,128)S(1)}, f32[12,384]{1,0:T(8,128)}, u32[]{:S(2)}) copy-start(f32[12,384]{1,0:T(8,128)} %down_ref.5) | copy-start | bytes 55300
  107.6 14.9 %copy-start.11 = (f32[3,384]{1,0:T(4,128)S(1)}, f32[3,384]{1,0:T(4,128)}, u32[]{:S(2)}) copy-start(f32[3,384]{1,0:T(4,128)} %out_ref.5) | copy-start | bytes 13828
  114.9 3.8 %collective-permute-start.14 = (bf16[12,384]{1,0:T(8,128)(2,1)S(1)}, bf16[12,384]{1,0:T(8,128)(2,1)S(1)}, u32[]{:S(2)}, u32[]{:S(2)}) collective-permute-start(bf16[12,384]{1,0:T(8,128)(2,1)S(1)} %get-tuple-element.91), channel_id=1, source_target_pairs={{64,0},{66,2},{1,64},{3,66},{65,1},{67,3},{0,65},{2,67},{68,4},{70... | collective-permute-start | bytes 27656 | tf_op jit(solution)/shard_map/ppermute | solution.py:790
  116.1 5.2 %collective-permute-start.15 = (bf16[12,384]{1,0:T(8,128)(2,1)S(1)}, bf16[12,384]{1,0:T(8,128)(2,1)S(1)}, u32[]{:S(2)}, u32[]{:S(2)}) collective-permute-start(bf16[12,384]{1,0:T(8,128)(2,1)S(1)} %get-tuple-element.92), channel_id=1, source_target_pairs={{1,0},{3,2},{65,64},{67,66},{0,1},{2,3},{64,65},{66,67},{5,4},{7,6... | collective-permute-start | bytes 27656 | tf_op jit(solution)/shard_map/ppermute | solution.py:790
  117.7 4.9 %collective-permute-start.16 = (bf16[12,384]{1,0:T(8,128)(2,1)S(1)}, bf16[12,384]{1,0:T(8,128)(2,1)S(1)}, u32[]{:S(2)}, u32[]{:S(2)}) collective-permute-start(bf16[12,384]{1,0:T(8,128)(2,1)S(1)} %get-tuple-element.93), channel_id=1, source_target_pairs={{65,0},{67,2},{0,64},{2,66},{64,1},{66,3},{1,65},{3,67},{69,4},{71... | collective-permute-start | bytes 27656 | tf_op jit(solution)/shard_map/ppermute | solution.py:790
  (8 other events, 51.9 us)

commit v6 on v5

--- a/solution.py
+++ b/solution.py
@@ -40,7 +40,7 @@
 SENT = 40
 VMEM = 24 << 20
 ALL_VMEM = 60 << 20
-LAYER_VMEM = 60 << 20
+LAYER_VMEM = 57 << 20
 
 
 def qkv_pieces(block):
@@ -193,7 +193,6 @@
     ctx_ref,
     dqkv_ref,
     small_ref,
-    weights_ref,
     stream_ref,
     cot_ref,
     result_ref,
@@ -207,36 +206,37 @@
     half = where_ref[1]
     colour = where_ref[2]
     count = cot_ref.shape[0]
+    parts = ((own0, own1, own2, own3), (oth0, oth1, oth2, oth3))
     loads = [
-        pltpu.make_async_copy(source, weights_ref.at[k], in_sems.at[k])
-        for k, source in enumerate((own0, own1, own2, own3, oth0, oth1, oth2, oth3))
+        pltpu.make_async_copy(stream_hbm, stream_ref, in_sems.at[0]),
+        pltpu.make_async_copy(cot_hbm, cot_ref, in_sems.at[1]),
     ]
-    loads.append(pltpu.make_async_copy(stream_hbm, stream_ref, in_sems.at[8]))
-    loads.append(pltpu.make_async_copy(cot_hbm, cot_ref, in_sems.at[9]))
-    for load in loads[8:] + loads[:8]:
+    for load in loads:
         load.start()
 
-    def grouped(s, xy, first):
-        behind = xy // 4 + 2 * (xy % 4) + colour
-        return jnp.concatenate(
-            [
-                weights_ref[4 * s + ((z + 12 - behind) & 3), xy].astype(F32)[first : first + BLOCK]
-                for z in range(4)
-            ],
-            axis=0,
-        )
-
-    for load in loads[8:]:
+    for here in range(4):
+
+        @pl.when(colour == here)
+        def _(here=here):
+            for s in range(2):
+                for xy in range(16):
+                    behind = xy // 4 + 2 * (xy % 4) + here
+                    blocks = [parts[s][(z - behind) % 4][xy].astype(F32) for z in range(4)]
+                    groups = [
+                        jnp.concatenate([block[k : k + BLOCK] for block in blocks], axis=0)
+                        for k in (0, 12, 24)
+                    ]
+                    at = s * 768 + xy * GROUP
+                    wup[at : at + GROUP] = groups[0].astype(BF)
+                    wdn[at : at + GROUP] = groups[1].astype(BF)
+                    mixed[core if s == 0 else 1 - core, xy * GROUP : (xy + 1) * GROUP] = groups[2]
+
+    for load in loads:
         load.wait()
     stream_in = stream_ref[...]
     g1, s1, g2, s2 = (norms_ref[k : k + 1, :] for k in range(4))
     n1, r1 = norm_parts(stream_in)
     y1 = (n1 * g1 + s1).astype(BF)
-    for s, at_core in ((0, core), (1, 1 - core)):
-        for load in loads[4 * s : 4 * s + 4]:
-            load.wait()
-        for xy in range(16):
-            mixed[at_core, xy * GROUP : (xy + 1) * GROUP] = grouped(s, xy, 24)
     for at_core, at, block in blocks_of_rows():
         for first, length, to in qkv_pieces(block):
             sorted_qkv[to : to + length] = mixed[at_core, at + first : at + first + length]
@@ -283,13 +283,9 @@
     right = jnp.where(half == 0, y2, cot)
     out = stream_mid
     d_y2 = 0.0
-    for k in range(4):
-        for xy in range(8):
-            at = k * 384 + xy * GROUP
-            wup[at : at + GROUP] = grouped(k // 2, (k % 2) * 8 + xy, 0).astype(BF)
-            wdn[at : at + GROUP] = grouped(k // 2, (k % 2) * 8 + xy, 12).astype(BF)
-        wu = wup[k * 384 : (k + 1) * 384, :]
-        wd = wdn[k * 384 : (k + 1) * 384, :]
+    for k, target in enumerate((kept, sent)):
+        wu = wup[k * 768 : (k + 1) * 768, :]
+        wd = wdn[k * 768 : (k + 1) * 768, :]
         pre = dot_nt(y2, wu)
         cdf = 0.5 * (1.0 + lax.erf(pre * (2.0**-0.5)))
         hidden = (pre * cdf).astype(BF)
@@ -297,19 +293,19 @@
         d_pre = (slope * dot_nt(cot, wd)).astype(BF)
         out = out + dot(hidden, wd)
         d_y2 = d_y2 + dot(d_pre, wu)
-        grad = dot_tn(jnp.where(half == 0, d_pre, hidden), right).reshape(8, GROUP, 384)
-        at = (k % 2) * 8
-        if k < 2:
-            kept[at : at + 8] = grad.astype(BF)
-        else:
-            sent[at : at + 8] = grad.astype(BF)
+        grad = dot_tn(jnp.where(half == 0, d_pre, hidden), right)
+        target[...] = grad.astype(BF).reshape(16, GROUP, D)
     result_ref[...] = out.astype(BF)
     stores = [
-        pltpu.make_async_copy(
-            source.at[pl.ds(16 * k, 16)], target.at[pl.ds(16 * k, 16)], out_sems.at[2 * k + j]
+        pltpu.make_async_copy(source, target.at[pl.ds(first, 16)], out_sems.at[k])
+        for k, (source, target, first) in enumerate(
+            (
+                (sent, send_hbm, 0),
+                (kept, keep_hbm, 0),
+                (message.at[1 - core], send_hbm, 16),
+                (message.at[core], keep_hbm, 16),
+            )
         )
-        for k in range(2)
-        for j, (source, target) in enumerate(((sent, send_hbm), (kept, keep_hbm)))
     ]
     stores.append(pltpu.make_async_copy(result_ref, result_hbm, out_sems.at[4]))
     stores.append(pltpu.make_async_copy(in_grad_ref, in_grad_hbm, out_sems.at[5]))
@@ -386,9 +382,7 @@
                     rows += [small_ref[xy * 4 + z : xy * 4 + z + 1], zeros]
                 message[at_core, xy] = jnp.concatenate(rows, axis=0).astype(BF)
 
-    sent[16:] = message[1 - core]
     stores[2].start()
-    kept[16:] = message[core]
     stores[3].start()
     for store in stores:
         store.wait()
@@ -407,7 +401,7 @@
             jax.ShapeDtypeStruct((32, GROUP, D), BF),
             jax.ShapeDtypeStruct((32, GROUP, D), BF),
         ),
-        in_specs=[smem] * 3 + [vmem] * 2 + [hbm] * 10,
+        in_specs=[smem] * 3 + [vmem] * 2 + [hbm] * 2 + [vmem] * 8,
         out_specs=(hbm,) * 4,
         scratch_shapes=[
             pltpu.VMEM((1536, D), BF),
@@ -423,14 +417,13 @@
             pltpu.VMEM((count, D), BF),
             pltpu.VMEM((count, 1152), BF),
             pltpu.VMEM((64, D), F32),
-            pltpu.VMEM((8, 16, SENT, D), BF),
             pltpu.VMEM((count, D), F32),
             pltpu.VMEM((count, D), BF),
             pltpu.VMEM((count, D), BF),
             pltpu.VMEM((count, D), F32),
-            pltpu.VMEM((32, GROUP, D), BF),
-            pltpu.VMEM((32, GROUP, D), BF),
-            pltpu.SemaphoreType.DMA((10,)),
+            pltpu.VMEM((16, GROUP, D), BF),
+            pltpu.VMEM((16, GROUP, D), BF),
+            pltpu.SemaphoreType.DMA((2,)),
             pltpu.SemaphoreType.DMA((6,)),
         ],
         compiler_params=pltpu.CompilerParams(vmem_limit_bytes=LAYER_VMEM),
@@ -579,19 +572,24 @@
     inv = 1.0 / (jnp.sqrt(jnp.sum(gram * eye)) + 1e-07)
     gram = gram * (inv * inv)
     mine = (MOMENTUM * old_ref[...].astype(F32) + scaled * piece_ref[...]) * inv
+    turned = mine.T
     for step in range(NS_STEPS - 2):
         parts = halves(gram)
         poly = halves(COEF_A * eye + COEF_B * gram + COEF_C * dot(parts[0], parts[0]))
-        gram = product(halves(product(poly, parts)), poly)
-        mine = product(halves(mine), poly)
+        inner = halves(product(poly, parts))
+        more = halves(turned)
+        both = product(
+            poly, [jnp.concatenate([inner[k], more[k]], axis=1) for k in range(2)]
+        )
+        gram, turned = both[:, :D], both[:, D:]
     parts = halves(gram)
     poly = (COEF_A * eye + COEF_B * gram + COEF_C * product(parts, parts)).astype(BF)
-    turned = dot(poly, parts[0]).astype(BF)
-    both = dot(jnp.concatenate([turned, mine.astype(BF)], axis=0), poly)
-    gram, mine = both[:D], both[D:]
+    inner = dot(poly, parts[0]).astype(BF)
+    both = dot(poly, jnp.concatenate([inner, turned.astype(BF)], axis=1))
+    gram, turned = both[:, :D], both[:, D:]
     low = gram.astype(BF)
     poly = COEF_A * eye + COEF_B * gram + COEF_C * dot(low, low)
-    mine = dot(mine.astype(BF), poly.astype(BF))
+    mine = dot(poly.astype(BF), turned.astype(BF)).T
     for z in range(4):
 
         @pl.when(chip_z() == z)

time: 124 us -> 124 us (level)
  transfers between devices with their start and end apart: 21 -> 21, of which waited for: 13 -> 13; matrix products, arithmetic and copies ran while one was open for 1% -> 1% of each run, Pallas kernels for 21% -> 20%
where the time goes in v6:
time: 124 us; the launch traced here: 123 us
  starting transfers between devices  34 us (27%)
  waiting for transfers between devices  32 us (26%)
  Pallas kernels  28.3 us (23%)
  blocking collectives  25.3 us (20%)
  local copies, waits for them, and re-layouts  1.35 us (1%)
    all_to_all x1, blocking collectives, exchanged(): return lax.all_to_all(value, axes, 0, 0, tiled=True)  25.3 us
    pallas_call x11, Pallas kernels, call(): pl.pallas_call(kernel, out_shape=tuple((jax.ShapeDtypeStruct(shape, dtype...  15.6 us
    all_to_all x3, waiting for transfers between devices, exchanged(): return lax.all_to_all(value, axes, 0, 0, tiled=True)  15.6 us
    all_to_all x3, starting transfers between devices, exchanged(): return lax.all_to_all(value, axes, 0, 0, tiled=True)  13.1 us
    pallas_call x1, Pallas kernels, run_layer(): pl.pallas_call(layer_kernel, out_shape=(jax.ShapeDtypeStruct((count, D),...  12.7 us
    all_to_all x1, starting transfers between devices, shards(): lax.all_to_all(rows, AXES, 0, 0, axis_index_groups=colour_groups(), tiled...  10.4 us
    ppermute x3, waiting for transfers between devices, shards(): lax.ppermute(orth[k], AXES, column_step(k))  4.08 us
    all_to_all x1, waiting for transfers between devices, shards(): lax.all_to_all(rows, AXES, 0, 0, axis_index_groups=colour_groups(), tiled...  3.84 us
  transfers between devices with their start and end apart: 21, of which 13 were waited for; matrix products, arithmetic and copies ran while one was open for 1% of the time, Pallas kernels for 20%

profile of v6, /device:TPU:0, one launch (start us, length us, event | category | flops | bytes accessed | tf_op | source)
XLA Modules:
  0.0 122.9 jit_solution(6153265422456608240)
XLA Ops:
  0.7 1.7 %weights.1 = bf16[16,40,384]{2,1,0:T(8,128)(2,1)} custom-call(f32[9,384]{1,0:T(8,128)} %bitcast.17, f32[3,384]{1,0:T(4,128)} %out_ref.5, f32[12,384]{1,0:T(8,128)} %bitcast.19, f32[12,384]{1,0:T(8,128)} %down_ref.5), custom_call_target="tpu_custom_call" | custom-call | tf_op jit(solution)/shard_map/weights/pallas_call | solution.py:447
  2.3 10.4 %all-to-all-start = ((bf16[16,40,384]{2,1,0:T(8,128)(2,1)}), bf16[16,40,384]{2,1,0:T(8,128)(2,1)S(1)}, u32[]{:S(2)}, u32[]{:S(2)}) async-start(bf16[16,40,384]{2,1,0:T(8,128)(2,1)} %weights.1), calls=%async_computation | async-start | bytes 983040 | tf_op jit(solution)/shard_map/all_to_all | solution.py:731
  12.9 0.8 collective-permute-start
  13.6 2.4 %collective-permute-start.1 = (bf16[12,384]{1,0:T(8,128)(2,1)S(1)}, bf16[12,384]{1,0:T(8,128)(2,1)S(1)}, u32[]{:S(2)}, u32[]{:S(2)}) collective-permute-start(bf16[12,384]{1,0:T(8,128)(2,1)S(1)} %get-tuple-element.64), channel_id=1, source_target_pairs={{1,0},{3,2},{65,64},{67,66},{0,1},{2,3},{64,65},{66,67},{5,4},{7,6... | collective-permute-start | bytes 27656 | tf_op jit(solution)/shard_map/ppermute | solution.py:720
  16.0 2.2 %embed.1 = (f32[256,384]{1,0:T(8,128)}, bf16[256,384]{1,0:T(8,128)(2,1)}) custom-call(bf16[256,384]{1,0:T(8,128)(2,1)} %tok_ref.1, bf16[256,384]{1,0:T(8,128)(2,1)} %cot_ref.1, f32[50,384]{1,0:T(8,128)} %table_ref.3, s32[1,256]{1,0:T(1,128)} %bitcast.21), custom_call_target="tpu_custom_call" | custom-call | tf_op jit(solution)/shard_map/embed/pallas_call | solution.py:447
  18.2 3.1 %collective-permute-done.1.refs_2_ = bf16[12,384]{1,0:T(8,128)(2,1)S(1)} collective-permute-done((bf16[12,384]{1,0:T(8,128)(2,1)S(1)}, bf16[12,384]{1,0:T(8,128)(2,1)S(1)}, u32[]{:S(2)}, u32[]{:S(2)}) %collective-permute-start.1) | collective-permute-done | bytes 9248 | tf_op jit(solution)/shard_map/ppermute | solution.py:720
  21.5 3.8 %all-to-all-done.own0 = bf16[16,40,384]{2,1,0:T(8,128)(2,1)S(1)} async-done(((bf16[16,40,384]{2,1,0:T(8,128)(2,1)}), bf16[16,40,384]{2,1,0:T(8,128)(2,1)S(1)}, u32[]{:S(2)}, u32[]{:S(2)}) %all-to-all-start) | async-done | bytes 491552 | tf_op jit(solution)/shard_map/all_to_all | solution.py:731
  25.4 2.0 %collective-permute-start.5 = (bf16[16,40,384]{2,1,0:T(8,128)(2,1)S(1)}, bf16[16,40,384]{2,1,0:T(8,128)(2,1)S(1)}, u32[]{:S(2)}, u32[]{:S(2)}) collective-permute-start(bf16[16,40,384]{2,1,0:T(8,128)(2,1)S(1)} %all-to-all-done.own0), channel_id=1, source_target_pairs={{16,0},{67,2},{80,64},{2,66},{17,1},{66,3},{81,65},{3,67},{20,4},{... | collective-permute-start | bytes 1474568 | tf_op jit(solution)/shard_map/ppermute | solution.py:741
  27.4 0.9 join.1
  28.3 6.0 %all-to-all-start.1 = ((bf16[16,48,384]{2,1,0:T(8,128)(2,1)}), bf16[16,48,384]{2,1,0:T(8,128)(2,1)S(1)}, u32[]{:S(2)}, u32[]{:S(2)}) async-start(bf16[16,48,384]{2,1,0:T(8,128)(2,1)} %get-tuple-element.79), calls=%async_computation.1 | async-start | bytes 1179648 | tf_op jit(solution)/shard_map/all_to_all | solution.py:681
  34.3 0.7 collective-permute-start.9
  35.1 1.1 collective-permute-done.4.own2
  36.2 1.2 collective-permute-done.3.own1
  37.4 0.7 pad_add_fusion.where_ref
  38.2 1.2 collective-permute-done.7.oth1
  39.4 12.7 %layer.1 = (bf16[256,384]{1,0:T(8,128)(2,1)}, f32[256,384]{1,0:T(8,128)}, bf16[32,48,384]{2,1,0:T(8,128)(2,1)}, bf16[32,48,384]{2,1,0:T(8,128)(2,1)}) custom-call(s32[3]{0:T(128)} %pad_add_fusion.where_ref, s32[5]{0:T(128)} %res_ref.1, s32[5]{0:T(128)} %off_ref.1, f32[4,384]{1,0:T(4,128)} %norms_ref.3, s32[1,256]{1,0:T(1,128)} %bitcast.22, ...), custom_call_target="tpu_custom_call" | custom-call | tf_op jit(solution)/shard_map/layer/pallas_call | solution.py:396
  52.3 1.3 %copy-done = bf16[32,48,384]{2,1,0:T(8,128)(2,1)S(1)} copy-done((bf16[32,48,384]{2,1,0:T(8,128)(2,1)S(1)}, bf16[32,48,384]{2,1,0:T(8,128)(2,1)}, u32[]{:S(2)}) %copy-start) | copy-done | bytes 1179672
  53.7 1.6 %collective-permute-done.10 = bf16[32,48,384]{2,1,0:T(8,128)(2,1)S(1)} collective-permute-done((bf16[32,48,384]{2,1,0:T(8,128)(2,1)}, bf16[32,48,384]{2,1,0:T(8,128)(2,1)S(1)}, u32[]{:S(2)}, u32[]{:S(2)}) %collective-permute-start.10) | collective-permute-done | bytes 1179680 | tf_op jit(solution)/shard_map/ppermute | solution.py:677
  55.6 25.3 %all_to_all.25.parts_ref = bf16[32,48,384]{2,1,0:T(8,128)(2,1)S(1)} all-to-all(bf16[32,48,384]{2,1,0:T(8,128)(2,1)S(1)} %add_convert_fusion), channel_id=1, replica_groups=mesh['zl'=2,'x'=4,'y'=4,'c'=2,'zh'=2] {'zl','x','y'}, dimensions={0} | all-to-all | bytes 2359296 | tf_op jit(solution)/shard_map/all_to_all | solution.py:681
  80.9 1.0 sum.1
  81.9 3.7 %all-to-all-start.3 = ((bf16[16,48,384]{2,1,0:T(8,128)(2,1)}), bf16[16,48,384]{2,1,0:T(8,128)(2,1)S(1)}, u32[]{:S(2)}, u32[]{:S(2)}) async-start(bf16[16,48,384]{2,1,0:T(8,128)(2,1)} %get-tuple-element.82), calls=%async_computation.3 | async-start | bytes 1179648 | tf_op jit(solution)/shard_map/all_to_all | solution.py:681
  85.7 11.6 %all-to-all-done.3.own_ref = bf16[16,48,384]{2,1,0:T(8,128)(2,1)S(1)} async-done(((bf16[16,48,384]{2,1,0:T(8,128)(2,1)}), bf16[16,48,384]{2,1,0:T(8,128)(2,1)S(1)}, u32[]{:S(2)}, u32[]{:S(2)}) %all-to-all-start.3) | async-done | bytes 589856 | tf_op jit(solution)/shard_map/all_to_all | solution.py:681
  97.3 0.9 tell.1
  98.2 3.4 %all-to-all-start.4 = ((bf16[8,16,384]{2,1,0:T(8,128)(2,1)}), bf16[8,16,384]{2,1,0:T(8,128)(2,1)S(1)}, u32[]{:S(2)}, u32[]{:S(2)}) async-start(bf16[8,16,384]{2,1,0:T(8,128)(2,1)} %tell.1), calls=%async_computation.4 | async-start | bytes 196608 | tf_op jit(solution)/shard_map/all_to_all | solution.py:681
  101.8 1.5 %collective-permute-start.11 = (bf16[64,384]{1,0:T(8,128)(2,1)S(1)}, bf16[64,384]{1,0:T(8,128)(2,1)S(1)}, u32[]{:S(2)}, u32[]{:S(2)}) collective-permute-start(bf16[64,384]{1,0:T(8,128)(2,1)S(1)} %small.1.small_own_ref), channel_id=1, source_target_pairs={{64,0},{65,1},{66,2},{67,3},{68,4},{69,5},{70,6},{71,7},{72,8},{73... | collective-permute-start | bytes 147464 | tf_op jit(solution)/shard_map/ppermute | solution.py:778
  103.3 3.9 %all-to-all-done.4.told_ref = bf16[8,16,384]{2,1,0:T(8,128)(2,1)S(1)} async-done(((bf16[8,16,384]{2,1,0:T(8,128)(2,1)}), bf16[8,16,384]{2,1,0:T(8,128)(2,1)S(1)}, u32[]{:S(2)}, u32[]{:S(2)}) %all-to-all-start.4) | async-done | bytes 98336 | tf_op jit(solution)/shard_map/all_to_all | solution.py:681
  107.3 7.3 %orth.1 = (bf16[12,384]{1,0:T(8,128)(2,1)S(1)}, bf16[12,384]{1,0:T(8,128)(2,1)S(1)}, bf16[12,384]{1,0:T(8,128)(2,1)S(1)}, bf16[12,384]{1,0:T(8,128)(2,1)S(1)}) custom-call(bf16[8,16,384]{2,1,0:T(8,128)(2,1)S(1)} %all-to-all-done.4.told_ref, bf16[16,48,384]{2,1,0:T(8,128)(2,1)S(1)} %all-to-all-done.3.own_ref, ...), custom_call_target="tpu_custom_call" | custom-call | flops 8000000000 | bytes 4000000 | tf_op jit(solution)/shard_map/orth/pallas_call | solution.py:447
  114.6 1.2 collective-permute-start.14
  115.8 1.5 %collective-permute-start.15 = (bf16[12,384]{1,0:T(8,128)(2,1)S(1)}, bf16[12,384]{1,0:T(8,128)(2,1)S(1)}, u32[]{:S(2)}, u32[]{:S(2)}) collective-permute-start(bf16[12,384]{1,0:T(8,128)(2,1)S(1)} %get-tuple-element.92), channel_id=1, source_target_pairs={{1,0},{3,2},{65,64},{67,66},{0,1},{2,3},{64,65},{66,67},{5,4},{7,6... | collective-permute-start | bytes 27656 | tf_op jit(solution)/shard_map/ppermute | solution.py:788
  117.3 0.8 moment.1
  118.4 2.6 %collective-permute-done.15.orth2 = bf16[12,384]{1,0:T(8,128)(2,1)S(1)} collective-permute-done((bf16[12,384]{1,0:T(8,128)(2,1)S(1)}, bf16[12,384]{1,0:T(8,128)(2,1)S(1)}, u32[]{:S(2)}, u32[]{:S(2)}) %collective-permute-start.15) | collective-permute-done | bytes 9248 | tf_op jit(solution)/shard_map/ppermute | solution.py:788
  121.0 1.2 collective-permute-done.16.orth3
  (63 shorter events, 2.3 us)
Async XLA Ops:
  0.6 12.1 %copy-start.5 = (f32[12,384]{1,0:T(8,128)S(1)}, f32[12,384]{1,0:T(8,128)}, u32[]{:S(2)}) copy-start(f32[12,384]{1,0:T(8,128)} %down_m_ref.1) | copy-start | bytes 55300
  0.7 12.1 %copy-start.12 = (f32[3,384]{1,0:T(4,128)S(1)}, f32[3,384]{1,0:T(4,128)}, u32[]{:S(2)}) copy-start(f32[3,384]{1,0:T(4,128)} %out_m_ref.1) | copy-start | bytes 13828
  0.7 12.1 %copy-start.4 = (f32[384,12]{0,1:T(8,128)S(1)}, f32[384,12]{0,1:T(8,128)}, u32[]{:S(2)}) copy-start(f32[384,12]{0,1:T(8,128)} %param.28) | copy-start | bytes 55300
  0.7 12.1 %copy-start.3 = (f32[384,9]{0,1:T(8,128)S(1)}, f32[384,9]{0,1:T(8,128)}, u32[]{:S(2)}) copy-start(f32[384,9]{0,1:T(8,128)} %param.26) | copy-start | bytes 41476
  2.3 23.0 %all-to-all-start = ((bf16[16,40,384]{2,1,0:T(8,128)(2,1)}), bf16[16,40,384]{2,1,0:T(8,128)(2,1)S(1)}, u32[]{:S(2)}, u32[]{:S(2)}) async-start(bf16[16,40,384]{2,1,0:T(8,128)(2,1)} %weights.1), calls=%async_computation | async-start | bytes 983040 | tf_op jit(solution)/shard_map/all_to_all | solution.py:731
  12.9 5.4 %collective-permute-start = (bf16[12,384]{1,0:T(8,128)(2,1)S(1)}, bf16[12,384]{1,0:T(8,128)(2,1)S(1)}, u32[]{:S(2)}, u32[]{:S(2)}) collective-permute-start(bf16[12,384]{1,0:T(8,128)(2,1)S(1)} %get-tuple-element.63), channel_id=1, source_target_pairs={{64,0},{66,2},{1,64},{3,66},{65,1},{67,3},{0,65},{2,67},{68,4},{70... | collective-permute-start | bytes 27656 | tf_op jit(solution)/shard_map/ppermute | solution.py:720
  13.6 7.7 %collective-permute-start.1 = (bf16[12,384]{1,0:T(8,128)(2,1)S(1)}, bf16[12,384]{1,0:T(8,128)(2,1)S(1)}, u32[]{:S(2)}, u32[]{:S(2)}) collective-permute-start(bf16[12,384]{1,0:T(8,128)(2,1)S(1)} %get-tuple-element.64), channel_id=1, source_target_pairs={{1,0},{3,2},{65,64},{67,66},{0,1},{2,3},{64,65},{66,67},{5,4},{7,6... | collective-permute-start | bytes 27656 | tf_op jit(solution)/shard_map/ppermute | solution.py:720
  16.0 5.5 %collective-permute-start.2 = (bf16[12,384]{1,0:T(8,128)(2,1)S(1)}, bf16[12,384]{1,0:T(8,128)(2,1)S(1)}, u32[]{:S(2)}, u32[]{:S(2)}) collective-permute-start(bf16[12,384]{1,0:T(8,128)(2,1)S(1)} %get-tuple-element.65), channel_id=1, source_target_pairs={{65,0},{67,2},{0,64},{2,66},{64,1},{66,3},{1,65},{3,67},{69,4},{71... | collective-permute-start | bytes 27656 | tf_op jit(solution)/shard_map/ppermute | solution.py:720
  25.4 14.0 %copy-start.14 = (bf16[16,40,384]{2,1,0:T(8,128)(2,1)}, bf16[16,40,384]{2,1,0:T(8,128)(2,1)S(1)}, u32[]{:S(2)}) copy-start(bf16[16,40,384]{2,1,0:T(8,128)(2,1)S(1)} %all-to-all-done.own0) | copy-start | bytes 1474564
  25.4 2.9 %collective-permute-start.6 = (bf16[16,40,384]{2,1,0:T(8,128)(2,1)S(1)}, bf16[16,40,384]{2,1,0:T(8,128)(2,1)S(1)}, u32[]{:S(2)}, u32[]{:S(2)}) collective-permute-start(bf16[16,40,384]{2,1,0:T(8,128)(2,1)S(1)} %all-to-all-done.own0), channel_id=1, source_target_pairs={{0,2},{2,0},{1,3},{3,1},{4,6},{6,4},{5,7},{7,5},{8,10},{10,8},{9,1... | collective-permute-start | bytes 1474568 | tf_op jit(solution)/shard_map/ppermute | solution.py:677
  25.4 8.9 %collective-permute-start.5 = (bf16[16,40,384]{2,1,0:T(8,128)(2,1)S(1)}, bf16[16,40,384]{2,1,0:T(8,128)(2,1)S(1)}, u32[]{:S(2)}, u32[]{:S(2)}) collective-permute-start(bf16[16,40,384]{2,1,0:T(8,128)(2,1)S(1)} %all-to-all-done.own0), channel_id=1, source_target_pairs={{16,0},{67,2},{80,64},{2,66},{17,1},{66,3},{81,65},{3,67},{20,4},{... | collective-permute-start | bytes 1474568 | tf_op jit(solution)/shard_map/ppermute | solution.py:741
  27.3 8.8 %collective-permute-start.4 = (bf16[16,40,384]{2,1,0:T(8,128)(2,1)S(1)}, bf16[16,40,384]{2,1,0:T(8,128)(2,1)S(1)}, u32[]{:S(2)}, u32[]{:S(2)}) collective-permute-start(bf16[16,40,384]{2,1,0:T(8,128)(2,1)S(1)} %all-to-all-done.own0), channel_id=1, source_target_pairs={{4,0},{14,2},{68,64},{78,66},{5,1},{15,3},{69,65},{79,67},{8,4},{2... | collective-permute-start | bytes 1474568 | tf_op jit(solution)/shard_map/ppermute | solution.py:741
  27.3 10.0 %collective-permute-start.3 = (bf16[16,40,384]{2,1,0:T(8,128)(2,1)S(1)}, bf16[16,40,384]{2,1,0:T(8,128)(2,1)S(1)}, u32[]{:S(2)}, u32[]{:S(2)}) collective-permute-start(bf16[16,40,384]{2,1,0:T(8,128)(2,1)S(1)} %all-to-all-done.own0), channel_id=1, source_target_pairs={{48,0},{66,2},{112,64},{3,66},{49,1},{67,3},{113,65},{2,67},{52,4}... | collective-permute-start | bytes 1474568 | tf_op jit(solution)/shard_map/ppermute | solution.py:741
  28.3 11.1 %copy-start.15 = (bf16[16,40,384]{2,1,0:T(8,128)(2,1)}, bf16[16,40,384]{2,1,0:T(8,128)(2,1)S(1)}, u32[]{:S(2)}) copy-start(bf16[16,40,384]{2,1,0:T(8,128)(2,1)S(1)} %collective-permute-done.6.oth0) | copy-start | bytes 1474564
  28.3 23.8 %all-to-all-start.1 = ((bf16[16,48,384]{2,1,0:T(8,128)(2,1)}), bf16[16,48,384]{2,1,0:T(8,128)(2,1)S(1)}, u32[]{:S(2)}, u32[]{:S(2)}) async-start(bf16[16,48,384]{2,1,0:T(8,128)(2,1)} %get-tuple-element.79), calls=%async_computation.1 | async-start | bytes 1179648 | tf_op jit(solution)/shard_map/all_to_all | solution.py:681
  34.3 3.7 %collective-permute-start.9 = (bf16[16,40,384]{2,1,0:T(8,128)(2,1)S(1)}, bf16[16,40,384]{2,1,0:T(8,128)(2,1)}, u32[]{:S(2)}, u32[]{:S(2)}) collective-permute-start(bf16[16,40,384]{2,1,0:T(8,128)(2,1)S(1)} %collective-permute-done.5.own3), channel_id=1, source_target_pairs={{0,2},{2,0},{1,3},{3,1},{4,6},{6,4},{5,7},{7,5},{8,10},{10,8},{9,1... | collective-permute-start | bytes 1474568 | tf_op jit(solution)/shard_map/ppermute | solution.py:677
  36.2 2.0 %collective-permute-start.8 = (bf16[16,40,384]{2,1,0:T(8,128)(2,1)S(1)}, bf16[16,40,384]{2,1,0:T(8,128)(2,1)}, u32[]{:S(2)}, u32[]{:S(2)}) collective-permute-start(bf16[16,40,384]{2,1,0:T(8,128)(2,1)S(1)} %collective-permute-done.4.own2), channel_id=1, source_target_pairs={{0,2},{2,0},{1,3},{3,1},{4,6},{6,4},{5,7},{7,5},{8,10},{10,8},{9,1... | collective-permute-start | bytes 1474568 | tf_op jit(solution)/shard_map/ppermute | solution.py:677
  37.4 2.0 %collective-permute-start.7 = (bf16[16,40,384]{2,1,0:T(8,128)(2,1)S(1)}, bf16[16,40,384]{2,1,0:T(8,128)(2,1)}, u32[]{:S(2)}, u32[]{:S(2)}) collective-permute-start(bf16[16,40,384]{2,1,0:T(8,128)(2,1)S(1)} %collective-permute-done.3.own1), channel_id=1, source_target_pairs={{0,2},{2,0},{1,3},{3,1},{4,6},{6,4},{5,7},{7,5},{8,10},{10,8},{9,1... | collective-permute-start | bytes 1474568 | tf_op jit(solution)/shard_map/ppermute | solution.py:677
  52.1 3.1 %collective-permute-start.10 = (bf16[32,48,384]{2,1,0:T(8,128)(2,1)}, bf16[32,48,384]{2,1,0:T(8,128)(2,1)S(1)}, u32[]{:S(2)}, u32[]{:S(2)}) collective-permute-start(bf16[32,48,384]{2,1,0:T(8,128)(2,1)} %get-tuple-element.81), channel_id=1, source_target_pairs={{0,2},{2,0},{1,3},{3,1},{4,6},{6,4},{5,7},{7,5},{8,10},{10,8},{9,1... | collective-permute-start | bytes 3538952 | tf_op jit(solution)/shard_map/ppermute | solution.py:677
  81.9 19.7 %copy-start.2 = (bf16[2,64,768]{2,1,0:T(8,128)(2,1)S(1)}, bf16[2,64,768]{2,1,0:T(8,128)(2,1)}, u32[]{:S(2)}) copy-start(bf16[2,64,768]{2,1,0:T(8,128)(2,1)} %constant.27.clone.places_ref) | copy-start | bytes 589828
  81.9 15.4 %all-to-all-start.3 = ((bf16[16,48,384]{2,1,0:T(8,128)(2,1)}), bf16[16,48,384]{2,1,0:T(8,128)(2,1)S(1)}, u32[]{:S(2)}, u32[]{:S(2)}) async-start(bf16[16,48,384]{2,1,0:T(8,128)(2,1)} %get-tuple-element.82), calls=%async_computation.3 | async-start | bytes 1179648 | tf_op jit(solution)/shard_map/all_to_all | solution.py:681
  85.6 17.7 %collective-permute-start.13 = (bf16[16,48,384]{2,1,0:T(8,128)(2,1)S(1)}, bf16[16,48,384]{2,1,0:T(8,128)(2,1)S(1)}, u32[]{:S(2)}, u32[]{:S(2)}) collective-permute-start(bf16[16,48,384]{2,1,0:T(8,128)(2,1)S(1)} %all-to-all-done.1.old_own_ref), channel_id=1, source_target_pairs={{0,2},{2,0},{1,3},{3,1},{4,6},{6,4},{5,7},{7,5},{8,10},{10,8},{9,1... | collective-permute-start | bytes 1769480 | tf_op jit(solution)/shard_map/ppermute | solution.py:677
  98.2 9.1 %collective-permute-start.12 = (bf16[16,48,384]{2,1,0:T(8,128)(2,1)S(1)}, bf16[16,48,384]{2,1,0:T(8,128)(2,1)S(1)}, u32[]{:S(2)}, u32[]{:S(2)}) collective-permute-start(bf16[16,48,384]{2,1,0:T(8,128)(2,1)S(1)} %all-to-all-done.3.own_ref), channel_id=1, source_target_pairs={{0,2},{2,0},{1,3},{3,1},{4,6},{6,4},{5,7},{7,5},{8,10},{10,8},{9,1... | collective-permute-start | bytes 1769480 | tf_op jit(solution)/shard_map/ppermute | solution.py:677
  98.2 9.1 %all-to-all-start.4 = ((bf16[8,16,384]{2,1,0:T(8,128)(2,1)}), bf16[8,16,384]{2,1,0:T(8,128)(2,1)S(1)}, u32[]{:S(2)}, u32[]{:S(2)}) async-start(bf16[8,16,384]{2,1,0:T(8,128)(2,1)} %tell.1), calls=%async_computation.4 | async-start | bytes 196608 | tf_op jit(solution)/shard_map/all_to_all | solution.py:681
  101.8 15.5 %collective-permute-start.11 = (bf16[64,384]{1,0:T(8,128)(2,1)S(1)}, bf16[64,384]{1,0:T(8,128)(2,1)S(1)}, u32[]{:S(2)}, u32[]{:S(2)}) collective-permute-start(bf16[64,384]{1,0:T(8,128)(2,1)S(1)} %small.1.small_own_ref), channel_id=1, source_target_pairs={{64,0},{65,1},{66,2},{67,3},{68,4},{69,5},{70,6},{71,7},{72,8},{73... | collective-permute-start | bytes 147464 | tf_op jit(solution)/shard_map/ppermute | solution.py:778
  107.3 14.9 %copy-start.6 = (f32[384,9]{0,1:T(8,128)S(1)}, f32[384,9]{0,1:T(8,128)}, u32[]{:S(2)}) copy-start(f32[384,9]{0,1:T(8,128)} %param.22) | copy-start | bytes 41476
  107.3 14.9 %copy-start.7 = (f32[384,12]{0,1:T(8,128)S(1)}, f32[384,12]{0,1:T(8,128)}, u32[]{:S(2)}) copy-start(f32[384,12]{0,1:T(8,128)} %param.24) | copy-start | bytes 55300
  107.3 14.9 %copy-start.8 = (f32[12,384]{1,0:T(8,128)S(1)}, f32[12,384]{1,0:T(8,128)}, u32[]{:S(2)}) copy-start(f32[12,384]{1,0:T(8,128)} %down_ref.5) | copy-start | bytes 55300
  107.3 14.9 %copy-start.11 = (f32[3,384]{1,0:T(4,128)S(1)}, f32[3,384]{1,0:T(4,128)}, u32[]{:S(2)}) copy-start(f32[3,384]{1,0:T(4,128)} %out_ref.5) | copy-start | bytes 13828
  114.6 3.8 %collective-permute-start.14 = (bf16[12,384]{1,0:T(8,128)(2,1)S(1)}, bf16[12,384]{1,0:T(8,128)(2,1)S(1)}, u32[]{:S(2)}, u32[]{:S(2)}) collective-permute-start(bf16[12,384]{1,0:T(8,128)(2,1)S(1)} %get-tuple-element.91), channel_id=1, source_target_pairs={{64,0},{66,2},{1,64},{3,66},{65,1},{67,3},{0,65},{2,67},{68,4},{70... | collective-permute-start | bytes 27656 | tf_op jit(solution)/shard_map/ppermute | solution.py:788
  115.8 5.2 %collective-permute-start.15 = (bf16[12,384]{1,0:T(8,128)(2,1)S(1)}, bf16[12,384]{1,0:T(8,128)(2,1)S(1)}, u32[]{:S(2)}, u32[]{:S(2)}) collective-permute-start(bf16[12,384]{1,0:T(8,128)(2,1)S(1)} %get-tuple-element.92), channel_id=1, source_target_pairs={{1,0},{3,2},{65,64},{67,66},{0,1},{2,3},{64,65},{66,67},{5,4},{7,6... | collective-permute-start | bytes 27656 | tf_op jit(solution)/shard_map/ppermute | solution.py:788
  117.3 4.9 %collective-permute-start.16 = (bf16[12,384]{1,0:T(8,128)(2,1)S(1)}, bf16[12,384]{1,0:T(8,128)(2,1)S(1)}, u32[]{:S(2)}, u32[]{:S(2)}) collective-permute-start(bf16[12,384]{1,0:T(8,128)(2,1)S(1)} %get-tuple-element.93), channel_id=1, source_target_pairs={{65,0},{67,2},{0,64},{2,66},{64,1},{66,3},{1,65},{3,67},{69,4},{71... | collective-permute-start | bytes 27656 | tf_op jit(solution)/shard_map/ppermute | solution.py:788
  (8 other events, 51.8 us)

commit v7 on v6

--- a/solution.py
+++ b/solution.py
@@ -261,6 +261,7 @@
     lane = lax.broadcasted_iota(jnp.int32, (1, 128), 1)
     masks = ((lane < HD).astype(F32).astype(BF), (lane >= HD).astype(F32).astype(BF))
     scale = HD**-0.5
+    scaled_masks = [mask * scale for mask in masks]
     for p in range(HEADS // 2):
         lo = p * 128
         q = qkv_ref[:, lo : lo + 128]
@@ -268,10 +269,10 @@
         v = qkv_ref[:, 768 + lo : 896 + lo]
         ctx = 0.0
         for hh in range(2):
-            scores = dot_nt(q * masks[hh], k) * scale
+            scores = dot_nt(q * scaled_masks[hh], k)
             scores = jnp.where(allowed, scores, -1e30)
             expo = jnp.exp(scores - jnp.max(scores, axis=-1, keepdims=True))
-            probs = expo / jnp.sum(expo, axis=-1, keepdims=True)
+            probs = expo * (1.0 / jnp.sum(expo, axis=-1, keepdims=True))
             probs_ref[2 * p + hh] = probs
             ctx = ctx + dot(probs.astype(BF), v * masks[hh])
         ctx_ref[:, lo : lo + 128] = ctx.astype(BF)
@@ -554,18 +555,20 @@
     piece_ref,
     *refs,
 ):
-    *out_refs, whole_ref = refs
+    out_refs = refs
     valid = valid_rows(chip_z())
     factor = clip(told_ref)[1]
     scaled = factor * valid
-    for s, (grad_ref, before_ref) in enumerate(((own_ref, old_own_ref), (oth_ref, old_oth_ref))):
-        for xy in range(16):
-            at = s * 768 + xy * GROUP
-            whole_ref[at : at + GROUP] = (
-                MOMENTUM * before_ref[xy].astype(F32) + scaled * grad_ref[xy].astype(F32)
-            ).astype(BF)
-    whole = whole_ref[...]
-    gram = dot_tn(whole, whole)
+    gram = 0.0
+    for grad_ref, before_ref in ((own_ref, old_own_ref), (oth_ref, old_oth_ref)):
+        rows = jnp.concatenate(
+            [
+                (MOMENTUM * before_ref[xy].astype(F32) + scaled * grad_ref[xy].astype(F32)).astype(BF)
+                for xy in range(16)
+            ],
+            axis=0,
+        )
+        gram = gram + dot_tn(rows, rows)
     eye = (
         lax.broadcasted_iota(jnp.int32, (D, D), 0) == lax.broadcasted_iota(jnp.int32, (D, D), 1)
     ).astype(F32)
@@ -781,7 +784,6 @@
         "orth",
         (((BLOCK, D), BF),) * 4,
         (told, grads, grads_other, old_own, old_other, old, piece),
-        scratch=[pltpu.VMEM((1536, D), BF)],
         flops=8_000_000_000,
         moved=4_000_000,
     )

time: 124 us -> 124 us (level)
  no operation moved by 1% of the time
where the time goes in v7:
time: 124 us; the launch traced here: 123 us
  starting transfers between devices  34 us (27%)
  waiting for transfers between devices  32 us (26%)
  Pallas kernels  28.3 us (23%)
  blocking collectives  25.3 us (20%)
  local copies, waits for them, and re-layouts  1.35 us (1%)
    all_to_all x1, blocking collectives, exchanged(): return lax.all_to_all(value, axes, 0, 0, tiled=True)  25.3 us
    pallas_call x11, Pallas kernels, call(): pl.pallas_call(kernel, out_shape=tuple((jax.ShapeDtypeStruct(shape, dtype...  15.6 us
    all_to_all x3, waiting for transfers between devices, exchanged(): return lax.all_to_all(value, axes, 0, 0, tiled=True)  15.6 us
    all_to_all x3, starting transfers between devices, exchanged(): return lax.all_to_all(value, axes, 0, 0, tiled=True)  13.1 us
    pallas_call x1, Pallas kernels, run_layer(): pl.pallas_call(layer_kernel, out_shape=(jax.ShapeDtypeStruct((count, D),...  12.7 us
    all_to_all x1, starting transfers between devices, shards(): lax.all_to_all(rows, AXES, 0, 0, axis_index_groups=colour_groups(), tiled...  10.4 us
    ppermute x3, waiting for transfers between devices, shards(): lax.ppermute(orth[k], AXES, column_step(k))  4.08 us
    all_to_all x1, waiting for transfers between devices, shards(): lax.all_to_all(rows, AXES, 0, 0, axis_index_groups=colour_groups(), tiled...  3.84 us
  transfers between devices with their start and end apart: 21, of which 13 were waited for; matrix products, arithmetic and copies ran while one was open for 1% of the time, Pallas kernels for 20%

profile of v7, /device:TPU:0, one launch (start us, length us, event | category | flops | bytes accessed | tf_op | source)
XLA Modules:
  0.0 122.8 jit_solution(8970975230099347842)
XLA Ops:
  0.7 1.7 %weights.1 = bf16[16,40,384]{2,1,0:T(8,128)(2,1)} custom-call(f32[9,384]{1,0:T(8,128)} %bitcast.17, f32[3,384]{1,0:T(4,128)} %out_ref.5, f32[12,384]{1,0:T(8,128)} %bitcast.19, f32[12,384]{1,0:T(8,128)} %down_ref.5), custom_call_target="tpu_custom_call" | custom-call | tf_op jit(solution)/shard_map/weights/pallas_call | solution.py:448
  2.3 10.4 %all-to-all-start = ((bf16[16,40,384]{2,1,0:T(8,128)(2,1)}), bf16[16,40,384]{2,1,0:T(8,128)(2,1)S(1)}, u32[]{:S(2)}, u32[]{:S(2)}) async-start(bf16[16,40,384]{2,1,0:T(8,128)(2,1)} %weights.1), calls=%async_computation | async-start | bytes 983040 | tf_op jit(solution)/shard_map/all_to_all | solution.py:734
  12.9 0.8 collective-permute-start
  13.6 2.4 %collective-permute-start.1 = (bf16[12,384]{1,0:T(8,128)(2,1)S(1)}, bf16[12,384]{1,0:T(8,128)(2,1)S(1)}, u32[]{:S(2)}, u32[]{:S(2)}) collective-permute-start(bf16[12,384]{1,0:T(8,128)(2,1)S(1)} %get-tuple-element.64), channel_id=1, source_target_pairs={{1,0},{3,2},{65,64},{67,66},{0,1},{2,3},{64,65},{66,67},{5,4},{7,6... | collective-permute-start | bytes 27656 | tf_op jit(solution)/shard_map/ppermute | solution.py:723
  16.0 2.2 %embed.1 = (f32[256,384]{1,0:T(8,128)}, bf16[256,384]{1,0:T(8,128)(2,1)}) custom-call(bf16[256,384]{1,0:T(8,128)(2,1)} %tok_ref.1, bf16[256,384]{1,0:T(8,128)(2,1)} %cot_ref.1, f32[50,384]{1,0:T(8,128)} %table_ref.3, s32[1,256]{1,0:T(1,128)} %bitcast.21), custom_call_target="tpu_custom_call" | custom-call | tf_op jit(solution)/shard_map/embed/pallas_call | solution.py:448
  18.2 3.1 %collective-permute-done.1.refs_2_ = bf16[12,384]{1,0:T(8,128)(2,1)S(1)} collective-permute-done((bf16[12,384]{1,0:T(8,128)(2,1)S(1)}, bf16[12,384]{1,0:T(8,128)(2,1)S(1)}, u32[]{:S(2)}, u32[]{:S(2)}) %collective-permute-start.1) | collective-permute-done | bytes 9248 | tf_op jit(solution)/shard_map/ppermute | solution.py:723
  21.5 3.8 %all-to-all-done.own0 = bf16[16,40,384]{2,1,0:T(8,128)(2,1)S(1)} async-done(((bf16[16,40,384]{2,1,0:T(8,128)(2,1)}), bf16[16,40,384]{2,1,0:T(8,128)(2,1)S(1)}, u32[]{:S(2)}, u32[]{:S(2)}) %all-to-all-start) | async-done | bytes 491552 | tf_op jit(solution)/shard_map/all_to_all | solution.py:734
  25.4 2.0 %collective-permute-start.5 = (bf16[16,40,384]{2,1,0:T(8,128)(2,1)S(1)}, bf16[16,40,384]{2,1,0:T(8,128)(2,1)S(1)}, u32[]{:S(2)}, u32[]{:S(2)}) collective-permute-start(bf16[16,40,384]{2,1,0:T(8,128)(2,1)S(1)} %all-to-all-done.own0), channel_id=1, source_target_pairs={{16,0},{67,2},{80,64},{2,66},{17,1},{66,3},{81,65},{3,67},{20,4},{... | collective-permute-start | bytes 1474568 | tf_op jit(solution)/shard_map/ppermute | solution.py:744
  27.4 0.9 join.1
  28.3 6.0 %all-to-all-start.1 = ((bf16[16,48,384]{2,1,0:T(8,128)(2,1)}), bf16[16,48,384]{2,1,0:T(8,128)(2,1)S(1)}, u32[]{:S(2)}, u32[]{:S(2)}) async-start(bf16[16,48,384]{2,1,0:T(8,128)(2,1)} %get-tuple-element.79), calls=%async_computation.1 | async-start | bytes 1179648 | tf_op jit(solution)/shard_map/all_to_all | solution.py:684
  34.3 0.7 collective-permute-start.9
  35.1 1.1 collective-permute-done.4.own2
  36.2 1.2 collective-permute-done.3.own1
  37.4 0.7 pad_add_fusion.where_ref
  38.2 1.2 collective-permute-done.7.oth1
  39.4 12.7 %layer.1 = (bf16[256,384]{1,0:T(8,128)(2,1)}, f32[256,384]{1,0:T(8,128)}, bf16[32,48,384]{2,1,0:T(8,128)(2,1)}, bf16[32,48,384]{2,1,0:T(8,128)(2,1)}) custom-call(s32[3]{0:T(128)} %pad_add_fusion.where_ref, s32[5]{0:T(128)} %res_ref.1, s32[5]{0:T(128)} %off_ref.1, f32[4,384]{1,0:T(4,128)} %norms_ref.3, s32[1,256]{1,0:T(1,128)} %bitcast.22, ...), custom_call_target="tpu_custom_call" | custom-call | tf_op jit(solution)/shard_map/layer/pallas_call | solution.py:397
  52.3 1.3 %copy-done = bf16[32,48,384]{2,1,0:T(8,128)(2,1)S(1)} copy-done((bf16[32,48,384]{2,1,0:T(8,128)(2,1)S(1)}, bf16[32,48,384]{2,1,0:T(8,128)(2,1)}, u32[]{:S(2)}) %copy-start) | copy-done | bytes 1179672
  53.7 1.6 %collective-permute-done.10 = bf16[32,48,384]{2,1,0:T(8,128)(2,1)S(1)} collective-permute-done((bf16[32,48,384]{2,1,0:T(8,128)(2,1)}, bf16[32,48,384]{2,1,0:T(8,128)(2,1)S(1)}, u32[]{:S(2)}, u32[]{:S(2)}) %collective-permute-start.10) | collective-permute-done | bytes 1179680 | tf_op jit(solution)/shard_map/ppermute | solution.py:680
  55.6 25.3 %all_to_all.25.parts_ref = bf16[32,48,384]{2,1,0:T(8,128)(2,1)S(1)} all-to-all(bf16[32,48,384]{2,1,0:T(8,128)(2,1)S(1)} %add_convert_fusion), channel_id=1, replica_groups=mesh['zl'=2,'x'=4,'y'=4,'c'=2,'zh'=2] {'zl','x','y'}, dimensions={0} | all-to-all | bytes 2359296 | tf_op jit(solution)/shard_map/all_to_all | solution.py:684
  80.9 1.0 sum.1
  81.9 3.7 %all-to-all-start.3 = ((bf16[16,48,384]{2,1,0:T(8,128)(2,1)}), bf16[16,48,384]{2,1,0:T(8,128)(2,1)S(1)}, u32[]{:S(2)}, u32[]{:S(2)}) async-start(bf16[16,48,384]{2,1,0:T(8,128)(2,1)} %get-tuple-element.82), calls=%async_computation.3 | async-start | bytes 1179648 | tf_op jit(solution)/shard_map/all_to_all | solution.py:684
  85.7 11.6 %all-to-all-done.3.own_ref = bf16[16,48,384]{2,1,0:T(8,128)(2,1)S(1)} async-done(((bf16[16,48,384]{2,1,0:T(8,128)(2,1)}), bf16[16,48,384]{2,1,0:T(8,128)(2,1)S(1)}, u32[]{:S(2)}, u32[]{:S(2)}) %all-to-all-start.3) | async-done | bytes 589856 | tf_op jit(solution)/shard_map/all_to_all | solution.py:684
  97.3 0.9 tell.1
  98.2 3.4 %all-to-all-start.4 = ((bf16[8,16,384]{2,1,0:T(8,128)(2,1)}), bf16[8,16,384]{2,1,0:T(8,128)(2,1)S(1)}, u32[]{:S(2)}, u32[]{:S(2)}) async-start(bf16[8,16,384]{2,1,0:T(8,128)(2,1)} %tell.1), calls=%async_computation.4 | async-start | bytes 196608 | tf_op jit(solution)/shard_map/all_to_all | solution.py:684
  101.8 1.5 %collective-permute-start.11 = (bf16[64,384]{1,0:T(8,128)(2,1)S(1)}, bf16[64,384]{1,0:T(8,128)(2,1)S(1)}, u32[]{:S(2)}, u32[]{:S(2)}) collective-permute-start(bf16[64,384]{1,0:T(8,128)(2,1)S(1)} %small.1.small_own_ref), channel_id=1, source_target_pairs={{64,0},{65,1},{66,2},{67,3},{68,4},{69,5},{70,6},{71,7},{72,8},{73... | collective-permute-start | bytes 147464 | tf_op jit(solution)/shard_map/ppermute | solution.py:781
  103.3 3.9 %all-to-all-done.4.told_ref = bf16[8,16,384]{2,1,0:T(8,128)(2,1)S(1)} async-done(((bf16[8,16,384]{2,1,0:T(8,128)(2,1)}), bf16[8,16,384]{2,1,0:T(8,128)(2,1)S(1)}, u32[]{:S(2)}, u32[]{:S(2)}) %all-to-all-start.4) | async-done | bytes 98336 | tf_op jit(solution)/shard_map/all_to_all | solution.py:684
  107.3 7.2 %orth.1 = (bf16[12,384]{1,0:T(8,128)(2,1)S(1)}, bf16[12,384]{1,0:T(8,128)(2,1)S(1)}, bf16[12,384]{1,0:T(8,128)(2,1)S(1)}, bf16[12,384]{1,0:T(8,128)(2,1)S(1)}) custom-call(bf16[8,16,384]{2,1,0:T(8,128)(2,1)S(1)} %all-to-all-done.4.told_ref, bf16[16,48,384]{2,1,0:T(8,128)(2,1)S(1)} %all-to-all-done.3.own_ref, ...), custom_call_target="tpu_custom_call" | custom-call | flops 8000000000 | bytes 4000000 | tf_op jit(solution)/shard_map/orth/pallas_call | solution.py:448
  114.6 1.2 collective-permute-start.14
  115.8 1.5 %collective-permute-start.15 = (bf16[12,384]{1,0:T(8,128)(2,1)S(1)}, bf16[12,384]{1,0:T(8,128)(2,1)S(1)}, u32[]{:S(2)}, u32[]{:S(2)}) collective-permute-start(bf16[12,384]{1,0:T(8,128)(2,1)S(1)} %get-tuple-element.92), channel_id=1, source_target_pairs={{1,0},{3,2},{65,64},{67,66},{0,1},{2,3},{64,65},{66,67},{5,4},{7,6... | collective-permute-start | bytes 27656 | tf_op jit(solution)/shard_map/ppermute | solution.py:790
  117.3 0.8 moment.1
  118.3 2.6 %collective-permute-done.15.orth2 = bf16[12,384]{1,0:T(8,128)(2,1)S(1)} collective-permute-done((bf16[12,384]{1,0:T(8,128)(2,1)S(1)}, bf16[12,384]{1,0:T(8,128)(2,1)S(1)}, u32[]{:S(2)}, u32[]{:S(2)}) %collective-permute-start.15) | collective-permute-done | bytes 9248 | tf_op jit(solution)/shard_map/ppermute | solution.py:790
  121.0 1.2 collective-permute-done.16.orth3
  (63 shorter events, 2.3 us)
Async XLA Ops:
  0.6 12.1 %copy-start.5 = (f32[12,384]{1,0:T(8,128)S(1)}, f32[12,384]{1,0:T(8,128)}, u32[]{:S(2)}) copy-start(f32[12,384]{1,0:T(8,128)} %down_m_ref.1) | copy-start | bytes 55300
  0.7 12.1 %copy-start.12 = (f32[3,384]{1,0:T(4,128)S(1)}, f32[3,384]{1,0:T(4,128)}, u32[]{:S(2)}) copy-start(f32[3,384]{1,0:T(4,128)} %out_m_ref.1) | copy-start | bytes 13828
  0.7 12.1 %copy-start.4 = (f32[384,12]{0,1:T(8,128)S(1)}, f32[384,12]{0,1:T(8,128)}, u32[]{:S(2)}) copy-start(f32[384,12]{0,1:T(8,128)} %param.28) | copy-start | bytes 55300
  0.7 12.1 %copy-start.3 = (f32[384,9]{0,1:T(8,128)S(1)}, f32[384,9]{0,1:T(8,128)}, u32[]{:S(2)}) copy-start(f32[384,9]{0,1:T(8,128)} %param.26) | copy-start | bytes 41476
  2.3 23.0 %all-to-all-start = ((bf16[16,40,384]{2,1,0:T(8,128)(2,1)}), bf16[16,40,384]{2,1,0:T(8,128)(2,1)S(1)}, u32[]{:S(2)}, u32[]{:S(2)}) async-start(bf16[16,40,384]{2,1,0:T(8,128)(2,1)} %weights.1), calls=%async_computation | async-start | bytes 983040 | tf_op jit(solution)/shard_map/all_to_all | solution.py:734
  12.9 5.4 %collective-permute-start = (bf16[12,384]{1,0:T(8,128)(2,1)S(1)}, bf16[12,384]{1,0:T(8,128)(2,1)S(1)}, u32[]{:S(2)}, u32[]{:S(2)}) collective-permute-start(bf16[12,384]{1,0:T(8,128)(2,1)S(1)} %get-tuple-element.63), channel_id=1, source_target_pairs={{64,0},{66,2},{1,64},{3,66},{65,1},{67,3},{0,65},{2,67},{68,4},{70... | collective-permute-start | bytes 27656 | tf_op jit(solution)/shard_map/ppermute | solution.py:723
  13.6 7.7 %collective-permute-start.1 = (bf16[12,384]{1,0:T(8,128)(2,1)S(1)}, bf16[12,384]{1,0:T(8,128)(2,1)S(1)}, u32[]{:S(2)}, u32[]{:S(2)}) collective-permute-start(bf16[12,384]{1,0:T(8,128)(2,1)S(1)} %get-tuple-element.64), channel_id=1, source_target_pairs={{1,0},{3,2},{65,64},{67,66},{0,1},{2,3},{64,65},{66,67},{5,4},{7,6... | collective-permute-start | bytes 27656 | tf_op jit(solution)/shard_map/ppermute | solution.py:723
  16.0 5.5 %collective-permute-start.2 = (bf16[12,384]{1,0:T(8,128)(2,1)S(1)}, bf16[12,384]{1,0:T(8,128)(2,1)S(1)}, u32[]{:S(2)}, u32[]{:S(2)}) collective-permute-start(bf16[12,384]{1,0:T(8,128)(2,1)S(1)} %get-tuple-element.65), channel_id=1, source_target_pairs={{65,0},{67,2},{0,64},{2,66},{64,1},{66,3},{1,65},{3,67},{69,4},{71... | collective-permute-start | bytes 27656 | tf_op jit(solution)/shard_map/ppermute | solution.py:723
  25.4 14.0 %copy-start.14 = (bf16[16,40,384]{2,1,0:T(8,128)(2,1)}, bf16[16,40,384]{2,1,0:T(8,128)(2,1)S(1)}, u32[]{:S(2)}) copy-start(bf16[16,40,384]{2,1,0:T(8,128)(2,1)S(1)} %all-to-all-done.own0) | copy-start | bytes 1474564
  25.4 2.9 %collective-permute-start.6 = (bf16[16,40,384]{2,1,0:T(8,128)(2,1)S(1)}, bf16[16,40,384]{2,1,0:T(8,128)(2,1)S(1)}, u32[]{:S(2)}, u32[]{:S(2)}) collective-permute-start(bf16[16,40,384]{2,1,0:T(8,128)(2,1)S(1)} %all-to-all-done.own0), channel_id=1, source_target_pairs={{0,2},{2,0},{1,3},{3,1},{4,6},{6,4},{5,7},{7,5},{8,10},{10,8},{9,1... | collective-permute-start | bytes 1474568 | tf_op jit(solution)/shard_map/ppermute | solution.py:680
  25.4 8.9 %collective-permute-start.5 = (bf16[16,40,384]{2,1,0:T(8,128)(2,1)S(1)}, bf16[16,40,384]{2,1,0:T(8,128)(2,1)S(1)}, u32[]{:S(2)}, u32[]{:S(2)}) collective-permute-start(bf16[16,40,384]{2,1,0:T(8,128)(2,1)S(1)} %all-to-all-done.own0), channel_id=1, source_target_pairs={{16,0},{67,2},{80,64},{2,66},{17,1},{66,3},{81,65},{3,67},{20,4},{... | collective-permute-start | bytes 1474568 | tf_op jit(solution)/shard_map/ppermute | solution.py:744
  27.3 8.8 %collective-permute-start.4 = (bf16[16,40,384]{2,1,0:T(8,128)(2,1)S(1)}, bf16[16,40,384]{2,1,0:T(8,128)(2,1)S(1)}, u32[]{:S(2)}, u32[]{:S(2)}) collective-permute-start(bf16[16,40,384]{2,1,0:T(8,128)(2,1)S(1)} %all-to-all-done.own0), channel_id=1, source_target_pairs={{4,0},{14,2},{68,64},{78,66},{5,1},{15,3},{69,65},{79,67},{8,4},{2... | collective-permute-start | bytes 1474568 | tf_op jit(solution)/shard_map/ppermute | solution.py:744
  27.3 10.0 %collective-permute-start.3 = (bf16[16,40,384]{2,1,0:T(8,128)(2,1)S(1)}, bf16[16,40,384]{2,1,0:T(8,128)(2,1)S(1)}, u32[]{:S(2)}, u32[]{:S(2)}) collective-permute-start(bf16[16,40,384]{2,1,0:T(8,128)(2,1)S(1)} %all-to-all-done.own0), channel_id=1, source_target_pairs={{48,0},{66,2},{112,64},{3,66},{49,1},{67,3},{113,65},{2,67},{52,4}... | collective-permute-start | bytes 1474568 | tf_op jit(solution)/shard_map/ppermute | solution.py:744
  28.3 11.1 %copy-start.15 = (bf16[16,40,384]{2,1,0:T(8,128)(2,1)}, bf16[16,40,384]{2,1,0:T(8,128)(2,1)S(1)}, u32[]{:S(2)}) copy-start(bf16[16,40,384]{2,1,0:T(8,128)(2,1)S(1)} %collective-permute-done.6.oth0) | copy-start | bytes 1474564
  28.3 23.8 %all-to-all-start.1 = ((bf16[16,48,384]{2,1,0:T(8,128)(2,1)}), bf16[16,48,384]{2,1,0:T(8,128)(2,1)S(1)}, u32[]{:S(2)}, u32[]{:S(2)}) async-start(bf16[16,48,384]{2,1,0:T(8,128)(2,1)} %get-tuple-element.79), calls=%async_computation.1 | async-start | bytes 1179648 | tf_op jit(solution)/shard_map/all_to_all | solution.py:684
  34.3 3.7 %collective-permute-start.9 = (bf16[16,40,384]{2,1,0:T(8,128)(2,1)S(1)}, bf16[16,40,384]{2,1,0:T(8,128)(2,1)}, u32[]{:S(2)}, u32[]{:S(2)}) collective-permute-start(bf16[16,40,384]{2,1,0:T(8,128)(2,1)S(1)} %collective-permute-done.5.own3), channel_id=1, source_target_pairs={{0,2},{2,0},{1,3},{3,1},{4,6},{6,4},{5,7},{7,5},{8,10},{10,8},{9,1... | collective-permute-start | bytes 1474568 | tf_op jit(solution)/shard_map/ppermute | solution.py:680
  36.2 2.0 %collective-permute-start.8 = (bf16[16,40,384]{2,1,0:T(8,128)(2,1)S(1)}, bf16[16,40,384]{2,1,0:T(8,128)(2,1)}, u32[]{:S(2)}, u32[]{:S(2)}) collective-permute-start(bf16[16,40,384]{2,1,0:T(8,128)(2,1)S(1)} %collective-permute-done.4.own2), channel_id=1, source_target_pairs={{0,2},{2,0},{1,3},{3,1},{4,6},{6,4},{5,7},{7,5},{8,10},{10,8},{9,1... | collective-permute-start | bytes 1474568 | tf_op jit(solution)/shard_map/ppermute | solution.py:680
  37.4 2.0 %collective-permute-start.7 = (bf16[16,40,384]{2,1,0:T(8,128)(2,1)S(1)}, bf16[16,40,384]{2,1,0:T(8,128)(2,1)}, u32[]{:S(2)}, u32[]{:S(2)}) collective-permute-start(bf16[16,40,384]{2,1,0:T(8,128)(2,1)S(1)} %collective-permute-done.3.own1), channel_id=1, source_target_pairs={{0,2},{2,0},{1,3},{3,1},{4,6},{6,4},{5,7},{7,5},{8,10},{10,8},{9,1... | collective-permute-start | bytes 1474568 | tf_op jit(solution)/shard_map/ppermute | solution.py:680
  52.1 3.1 %collective-permute-start.10 = (bf16[32,48,384]{2,1,0:T(8,128)(2,1)}, bf16[32,48,384]{2,1,0:T(8,128)(2,1)S(1)}, u32[]{:S(2)}, u32[]{:S(2)}) collective-permute-start(bf16[32,48,384]{2,1,0:T(8,128)(2,1)} %get-tuple-element.81), channel_id=1, source_target_pairs={{0,2},{2,0},{1,3},{3,1},{4,6},{6,4},{5,7},{7,5},{8,10},{10,8},{9,1... | collective-permute-start | bytes 3538952 | tf_op jit(solution)/shard_map/ppermute | solution.py:680
  81.9 19.7 %copy-start.2 = (bf16[2,64,768]{2,1,0:T(8,128)(2,1)S(1)}, bf16[2,64,768]{2,1,0:T(8,128)(2,1)}, u32[]{:S(2)}) copy-start(bf16[2,64,768]{2,1,0:T(8,128)(2,1)} %constant.27.clone.places_ref) | copy-start | bytes 589828
  81.9 15.4 %all-to-all-start.3 = ((bf16[16,48,384]{2,1,0:T(8,128)(2,1)}), bf16[16,48,384]{2,1,0:T(8,128)(2,1)S(1)}, u32[]{:S(2)}, u32[]{:S(2)}) async-start(bf16[16,48,384]{2,1,0:T(8,128)(2,1)} %get-tuple-element.82), calls=%async_computation.3 | async-start | bytes 1179648 | tf_op jit(solution)/shard_map/all_to_all | solution.py:684
  85.6 17.7 %collective-permute-start.13 = (bf16[16,48,384]{2,1,0:T(8,128)(2,1)S(1)}, bf16[16,48,384]{2,1,0:T(8,128)(2,1)S(1)}, u32[]{:S(2)}, u32[]{:S(2)}) collective-permute-start(bf16[16,48,384]{2,1,0:T(8,128)(2,1)S(1)} %all-to-all-done.1.old_own_ref), channel_id=1, source_target_pairs={{0,2},{2,0},{1,3},{3,1},{4,6},{6,4},{5,7},{7,5},{8,10},{10,8},{9,1... | collective-permute-start | bytes 1769480 | tf_op jit(solution)/shard_map/ppermute | solution.py:680
  98.2 9.1 %collective-permute-start.12 = (bf16[16,48,384]{2,1,0:T(8,128)(2,1)S(1)}, bf16[16,48,384]{2,1,0:T(8,128)(2,1)S(1)}, u32[]{:S(2)}, u32[]{:S(2)}) collective-permute-start(bf16[16,48,384]{2,1,0:T(8,128)(2,1)S(1)} %all-to-all-done.3.own_ref), channel_id=1, source_target_pairs={{0,2},{2,0},{1,3},{3,1},{4,6},{6,4},{5,7},{7,5},{8,10},{10,8},{9,1... | collective-permute-start | bytes 1769480 | tf_op jit(solution)/shard_map/ppermute | solution.py:680
  98.2 9.1 %all-to-all-start.4 = ((bf16[8,16,384]{2,1,0:T(8,128)(2,1)}), bf16[8,16,384]{2,1,0:T(8,128)(2,1)S(1)}, u32[]{:S(2)}, u32[]{:S(2)}) async-start(bf16[8,16,384]{2,1,0:T(8,128)(2,1)} %tell.1), calls=%async_computation.4 | async-start | bytes 196608 | tf_op jit(solution)/shard_map/all_to_all | solution.py:684
  101.8 15.5 %collective-permute-start.11 = (bf16[64,384]{1,0:T(8,128)(2,1)S(1)}, bf16[64,384]{1,0:T(8,128)(2,1)S(1)}, u32[]{:S(2)}, u32[]{:S(2)}) collective-permute-start(bf16[64,384]{1,0:T(8,128)(2,1)S(1)} %small.1.small_own_ref), channel_id=1, source_target_pairs={{64,0},{65,1},{66,2},{67,3},{68,4},{69,5},{70,6},{71,7},{72,8},{73... | collective-permute-start | bytes 147464 | tf_op jit(solution)/shard_map/ppermute | solution.py:781
  107.3 14.9 %copy-start.6 = (f32[384,9]{0,1:T(8,128)S(1)}, f32[384,9]{0,1:T(8,128)}, u32[]{:S(2)}) copy-start(f32[384,9]{0,1:T(8,128)} %param.22) | copy-start | bytes 41476
  107.3 14.9 %copy-start.7 = (f32[384,12]{0,1:T(8,128)S(1)}, f32[384,12]{0,1:T(8,128)}, u32[]{:S(2)}) copy-start(f32[384,12]{0,1:T(8,128)} %param.24) | copy-start | bytes 55300
  107.3 14.9 %copy-start.8 = (f32[12,384]{1,0:T(8,128)S(1)}, f32[12,384]{1,0:T(8,128)}, u32[]{:S(2)}) copy-start(f32[12,384]{1,0:T(8,128)} %down_ref.5) | copy-start | bytes 55300
  107.3 14.9 %copy-start.11 = (f32[3,384]{1,0:T(4,128)S(1)}, f32[3,384]{1,0:T(4,128)}, u32[]{:S(2)}) copy-start(f32[3,384]{1,0:T(4,128)} %out_ref.5) | copy-start | bytes 13828
  114.6 3.8 %collective-permute-start.14 = (bf16[12,384]{1,0:T(8,128)(2,1)S(1)}, bf16[12,384]{1,0:T(8,128)(2,1)S(1)}, u32[]{:S(2)}, u32[]{:S(2)}) collective-permute-start(bf16[12,384]{1,0:T(8,128)(2,1)S(1)} %get-tuple-element.91), channel_id=1, source_target_pairs={{64,0},{66,2},{1,64},{3,66},{65,1},{67,3},{0,65},{2,67},{68,4},{70... | collective-permute-start | bytes 27656 | tf_op jit(solution)/shard_map/ppermute | solution.py:790
  115.8 5.2 %collective-permute-start.15 = (bf16[12,384]{1,0:T(8,128)(2,1)S(1)}, bf16[12,384]{1,0:T(8,128)(2,1)S(1)}, u32[]{:S(2)}, u32[]{:S(2)}) collective-permute-start(bf16[12,384]{1,0:T(8,128)(2,1)S(1)} %get-tuple-element.92), channel_id=1, source_target_pairs={{1,0},{3,2},{65,64},{67,66},{0,1},{2,3},{64,65},{66,67},{5,4},{7,6... | collective-permute-start | bytes 27656 | tf_op jit(solution)/shard_map/ppermute | solution.py:790
  117.3 4.9 %collective-permute-start.16 = (bf16[12,384]{1,0:T(8,128)(2,1)S(1)}, bf16[12,384]{1,0:T(8,128)(2,1)S(1)}, u32[]{:S(2)}, u32[]{:S(2)}) collective-permute-start(bf16[12,384]{1,0:T(8,128)(2,1)S(1)} %get-tuple-element.93), channel_id=1, source_target_pairs={{65,0},{67,2},{0,64},{2,66},{64,1},{66,3},{1,65},{3,67},{69,4},{71... | collective-permute-start | bytes 27656 | tf_op jit(solution)/shard_map/ppermute | solution.py:790
  (8 other events, 51.7 us)
